TPU v7x, 32 devices: a whole 2x2x4 slice. The times are simulated.
32 devices in a mesh: ctx: 4 (over x, core), wshard: 8 (over z, y).
Axes of the slice: x: 2, y: 2, z: 4, core: 2. Of those that a mesh axis runs over, the one named last changes fastest.
Arguments:
- layer_input: float32 [8, 2048, 768], P('wshard', 'ctx'), may hold values from -6 to 6
- segments: int32 [8, 2048], P('wshard'), may hold values from 0 to 2, as said below
- global_blocks: int32 [8, 2], P('wshard'), may hold values from 0 to 31
- random_blocks: int32 [32, 12, 3], replicated, may hold values from 0 to 31
- thresholds: float32 [12], replicated, may hold values from 4 to 40
- w_query: float32 [768, 768], P(None, 'wshard'), may hold values from -0.3125 to 0.3125
- w_key: float32 [768, 768], P(None, 'wshard'), may hold values from -0.3125 to 0.3125
- w_value: float32 [768, 768], P(None, 'wshard'), may hold values from -0.21875 to 0.21875
- w_output: float32 [768, 768], P(None, 'wshard'), may hold values from -0.875 to 0.875
- w_inner: float32 [768, 3072], P(None, 'wshard'), may hold values from -0.21875 to 0.21875
- w_outer: float32 [3072, 768], P(None, 'wshard'), may hold values from -0.15625 to 0.15625
- query_bias: float32 [768], P('wshard'), may hold values from -3 to 3
- value_bias: float32 [768], P('wshard'), may hold values from -3 to 3
- output_bias: float32 [768], P('wshard'), may hold values from -3 to 3
- inner_bias: float32 [3072], P('wshard'), may hold values from -3 to 3
- outer_bias: float32 [768], P('wshard'), may hold values from -3 to 3
- gain_attn: float32 [768], P('wshard'), may hold values from 0.5 to 1.5
- shift_attn: float32 [768], P('wshard'), may hold values from -3 to 3
- gain_mlp: float32 [768], P('wshard'), may hold values from 0.5 to 1.5
- shift_mlp: float32 [768], P('wshard'), may hold values from -3 to 3
- out_grad: float32 [8, 2048, 768], P('wshard', 'ctx'), may hold values from -6 to 6
Outputs:
- layer_output: float32 [8, 2048, 768], P('wshard', 'ctx')
- input_grad: float32 [8, 2048, 768], P('wshard', 'ctx')
- grad_query: float32 [768, 768], P(None, 'wshard')
- grad_key: float32 [768, 768], P(None, 'wshard')
- grad_value: float32 [768, 768], P(None, 'wshard')
- grad_output: float32 [768, 768], P(None, 'wshard')
- grad_inner: float32 [768, 3072], P(None, 'wshard')
- grad_outer: float32 [3072, 768], P(None, 'wshard')
- grad_query_bias: float32 [768], P('wshard')
- grad_value_bias: float32 [768], P('wshard')
- grad_output_bias: float32 [768], P('wshard')
- grad_inner_bias: float32 [3072], P('wshard')
- grad_outer_bias: float32 [768], P('wshard')
- grad_attn_gain: float32 [768], P('wshard')
- grad_attn_shift: float32 [768], P('wshard')
- grad_mlp_gain: float32 [768], P('wshard')
- grad_mlp_shift: float32 [768], P('wshard')
- clipped_query: float32 [768, 768], P(None, 'wshard')
- clipped_key: float32 [768, 768], P(None, 'wshard')
- head_maxima: float32 [12], replicated
Inputs may be any that keep to these rules, and one draw needn't show every extreme that they name: `segments`: each sequence holds three documents, numbered 0, 1, 2 in order: the first ends within the first 512 tokens, the last begins within the last 512 tokens; each has at least one token. `global_blocks`: two entries of a sequence may name the same block. `random_blocks`: shared by all sequences; entries may repeat or name neighbour or global blocks.
All inputs are finite; a program needn't handle non-finite values.
Results may differ from a plain program's by a relative error of at most 0.02.
The roundings to bfloat16 on the way count: a program that leaves them out, or rounds other values in their place, can miss the bound.
Values may be sent and summed in bfloat16 or wider, within the bound.
No kernel may reach another device: no remote copies, remote signals or barrier semaphores. Data moves between devices by JAX's collectives and lax.ppermute only.
A program may use at most 320 MiB of HBM per device.

v0:
```python
import jax
import jax.numpy as jnp
from jax import lax
from jax.sharding import PartitionSpec as P

BLK = 64


EPSILON = 1e-05


def matmul(left, right):
    return jnp.dot(left, right, preferred_element_type=jnp.float32)


def matmul_tn(left, right):
    return lax.dot_general(
        left, right, (((0,), (0,)), ((), ())), preferred_element_type=jnp.float32
    )


def matmul_nt(left, right):
    return lax.dot_general(
        left, right, (((1,), (1,)), ((), ())), preferred_element_type=jnp.float32
    )


def norm_forward(values, gain, shift):
    centre = values - jnp.mean(values, axis=-1, keepdims=True)
    inverse = lax.rsqrt(jnp.mean(centre * centre, axis=-1, keepdims=True) + EPSILON)
    normed = centre * inverse
    return (normed * gain + shift, normed, inverse)


def norm_backward(upstream, normed, inverse, gain):
    scaled = upstream * gain
    mean_one = jnp.mean(scaled, axis=-1, keepdims=True)
    mean_two = jnp.mean(scaled * normed, axis=-1, keepdims=True)
    result = inverse * (scaled - mean_one - normed * mean_two)
    return (result, jnp.sum(upstream * normed, axis=0), jnp.sum(upstream, axis=0))


def block_lists(first, row_blocks, nblocks, global_pos, random_rows, heads):
    blocks = first + jnp.arange(row_blocks, dtype=jnp.int32)
    offsets = jnp.arange(-1, 2, dtype=jnp.int32)
    slide = jnp.clip(blocks[:, None] + offsets[None, :], 0, nblocks - 1)
    slide = jnp.broadcast_to(slide[:, None, :], (row_blocks, heads, 3))
    glob = jnp.broadcast_to(global_pos[None, None, :], (row_blocks, heads, global_pos.shape[0]))
    lists = jnp.concatenate([slide, glob, random_rows], axis=2)
    slots = lists.shape[2]
    equal = lists[..., :, None] == lists[..., None, :]
    earlier = jnp.arange(slots)[:, None] < jnp.arange(slots)[None, :]
    active = jnp.logical_not(jnp.any(equal & earlier[None, None], axis=-2))
    return (blocks, lists, active)


def softmax_rows(scores):
    highest = jnp.max(scores, axis=-1, keepdims=True)
    powers = jnp.exp(scores - highest)
    totals = jnp.sum(powers, axis=-1, keepdims=True)
    return (powers / totals, highest + jnp.log(totals))


def per_device(
    layer_input,
    segments,
    global_blocks,
    random_blocks,
    thresholds,
    w_query,
    w_key,
    w_value,
    w_output,
    w_inner,
    w_outer,
    query_bias,
    value_bias,
    output_bias,
    inner_bias,
    outer_bias,
    gain_attn,
    shift_attn,
    gain_mlp,
    shift_mlp,
    out_grad,
):
    tokens = layer_input[0]
    rows_here, width = tokens.shape
    seg_all = segments[0]
    seq_len = seg_all.shape[0]
    global_pos = global_blocks[0]
    heads = thresholds.shape[0]
    head_dim = width // heads
    nblocks = seq_len // BLK
    row_blocks = rows_here // BLK
    first = lax.axis_index("ctx") * row_blocks
    seg_own = lax.dynamic_slice_in_dim(seg_all, first * BLK, rows_here)
    seg_query = seg_own.reshape(row_blocks, BLK)
    seg_blocks = seg_all.reshape(nblocks, BLK)
    random_own = lax.dynamic_slice_in_dim(random_blocks, first, row_blocks, 0)
    gathered = (
        lax.all_gather(w_query.astype(jnp.bfloat16), "wshard", axis=1, tiled=True),
        lax.all_gather(w_key.astype(jnp.bfloat16), "wshard", axis=1, tiled=True),
        lax.all_gather(w_value.astype(jnp.bfloat16), "wshard", axis=1, tiled=True),
        lax.all_gather(w_output.astype(jnp.bfloat16), "wshard", axis=1, tiled=True),
        lax.all_gather(w_inner.astype(jnp.bfloat16), "wshard", axis=1, tiled=True),
        lax.all_gather(w_outer.astype(jnp.bfloat16), "wshard", axis=1, tiled=True),
        lax.all_gather(query_bias.astype(jnp.bfloat16), "wshard", axis=0, tiled=True),
        lax.all_gather(value_bias.astype(jnp.bfloat16), "wshard", axis=0, tiled=True),
        lax.all_gather(output_bias.astype(jnp.bfloat16), "wshard", axis=0, tiled=True),
        lax.all_gather(inner_bias.astype(jnp.bfloat16), "wshard", axis=0, tiled=True),
        lax.all_gather(outer_bias.astype(jnp.bfloat16), "wshard", axis=0, tiled=True),
        lax.all_gather(gain_attn.astype(jnp.bfloat16), "wshard", axis=0, tiled=True),
        lax.all_gather(shift_attn.astype(jnp.bfloat16), "wshard", axis=0, tiled=True),
        lax.all_gather(gain_mlp.astype(jnp.bfloat16), "wshard", axis=0, tiled=True),
        lax.all_gather(shift_mlp.astype(jnp.bfloat16), "wshard", axis=0, tiled=True),
    )
    full_query, full_key, full_value, full_output, full_inner, full_outer = gathered[:6]
    bias_query = gathered[6].astype(jnp.float32)
    bias_value = gathered[7].astype(jnp.float32)
    bias_output = gathered[8].astype(jnp.float32)
    bias_inner = gathered[9].astype(jnp.float32)
    bias_outer = gathered[10].astype(jnp.float32)
    attn_gain = gathered[11].astype(jnp.float32)
    attn_shift = gathered[12].astype(jnp.float32)
    mlp_gain = gathered[13].astype(jnp.float32)
    mlp_shift = gathered[14].astype(jnp.float32)
    inputs_low = tokens.astype(jnp.bfloat16)
    query = (matmul(inputs_low, full_query) + bias_query).astype(jnp.bfloat16)
    key_local = matmul(inputs_low, full_key).astype(jnp.bfloat16)
    value_local = (matmul(inputs_low, full_value) + bias_value).astype(jnp.bfloat16)
    keys_all, values_all = (
        lax.all_gather(key_local, "ctx", axis=0, tiled=True),
        lax.all_gather(value_local, "ctx", axis=0, tiled=True),
    )
    key_heads = keys_all.reshape(nblocks, BLK, heads, head_dim)
    value_heads = values_all.reshape(nblocks, BLK, heads, head_dim)
    keys_flat = keys_all.reshape(seq_len, heads, head_dim)
    values_flat = values_all.reshape(seq_len, heads, head_dim)
    blocks, lists, active = block_lists(first, row_blocks, nblocks, global_pos, random_own, heads)
    slots = lists.shape[2]
    head_ids = jnp.arange(heads)[None, :, None]
    key_sel = key_heads[lists, :, head_ids].reshape(row_blocks, heads, slots * BLK, head_dim)
    value_sel = value_heads[lists, :, head_ids].reshape(row_blocks, heads, slots * BLK, head_dim)
    seg_sel = seg_blocks[lists].reshape(row_blocks, heads, slots * BLK)
    slot_mask = jnp.repeat(active, BLK, axis=2)
    mask = slot_mask[:, :, None, :] & (seg_query[:, None, :, None] == seg_sel[:, :, None, :])
    query_heads = query.reshape(row_blocks, BLK, heads, head_dim)

    def sparse_scores():
        raw = (
            jnp.einsum("qahd,qhkd->qhak", query_heads, key_sel, preferred_element_type=jnp.float32)
            * 0.125
        )
        return jnp.where(mask, raw, -jnp.inf)

    def global_scores(rows, seg_rows):
        raw = (
            jnp.einsum("ahd,khd->hak", rows, keys_flat, preferred_element_type=jnp.float32) * 0.125
        )
        return jnp.where(seg_rows[None, :, None] == seg_all[None, None, :], raw, -jnp.inf)

    scores = sparse_scores()
    probs, sparse_lse = softmax_rows(scores)
    probs_low = probs.astype(jnp.bfloat16)
    attended = jnp.einsum(
        "qhak,qhkd->qahd", probs_low, value_sel, preferred_element_type=jnp.float32
    )
    is_global = jnp.zeros((row_blocks,), dtype=bool)
    for number in range(global_pos.shape[0]):
        is_global = is_global | (blocks == global_pos[number])
    local_peak = jnp.max(
        jnp.where(is_global[:, None, None, None], -jnp.inf, scores), axis=(0, 2, 3)
    )
    slot_rows = []
    slot_lse = []
    slot_low = []
    slot_place = []
    slot_use = []
    slot_owned = []
    slot_block = []
    for number in range(global_pos.shape[0] - 1, -1, -1):
        offset = global_pos[number] - first
        owned = (offset >= 0) & (offset < row_blocks)
        place = jnp.clip(offset, 0, row_blocks - 1)
        rows = lax.dynamic_index_in_dim(query_heads, place, 0, keepdims=False)
        seg_rows = lax.dynamic_index_in_dim(seg_query, place, 0, keepdims=False)
        gscores = global_scores(rows, seg_rows)
        gprobs, glse = softmax_rows(gscores)
        glow = gprobs.astype(jnp.bfloat16)
        gout = jnp.einsum("hak,khd->ahd", glow, values_flat, preferred_element_type=jnp.float32)
        here = blocks == global_pos[number]
        attended = jnp.where(here[:, None, None, None], gout[None], attended)
        local_peak = jnp.maximum(
            local_peak, jnp.where(owned, jnp.max(gscores, axis=(1, 2)), -jnp.inf)
        )
        distinct = jnp.all(global_pos[:number] != global_pos[number])
        slot_rows.append(rows)
        slot_lse.append(glse)
        slot_low.append(glow)
        slot_place.append(place)
        slot_use.append(owned & distinct)
        slot_owned.append(owned)
        slot_block.append(global_pos[number])
    maxima = lax.pmax(local_peak, ("ctx", "wshard"))
    attn_low = attended.reshape(rows_here, width).astype(jnp.bfloat16)
    mixed = matmul(attn_low, full_output) + bias_output
    hidden, normed_one, inverse_one = norm_forward(tokens + mixed, attn_gain, attn_shift)
    hidden_low = hidden.astype(jnp.bfloat16)
    inner = matmul(hidden_low, full_inner) + bias_inner
    activation_low = jax.nn.gelu(inner, approximate=True).astype(jnp.bfloat16)
    outer = matmul(activation_low, full_outer) + bias_outer
    layer_output, normed_two, inverse_two = norm_forward(hidden + outer, mlp_gain, mlp_shift)
    resid_two, mlp_gain_grad, mlp_shift_grad = norm_backward(
        out_grad[0], normed_two, inverse_two, mlp_gain
    )
    outer_grad = resid_two.astype(jnp.bfloat16)
    outer_weight_grad = matmul_tn(activation_low, outer_grad)
    outer_bias_grad = jnp.sum(outer_grad.astype(jnp.float32), axis=0)
    upstream = matmul_nt(outer_grad, full_outer)
    gelu_pull = jax.vjp(lambda values: jax.nn.gelu(values, approximate=True), inner)[1]
    inner_grad = gelu_pull(upstream)[0].astype(jnp.bfloat16)
    inner_weight_grad = matmul_tn(hidden_low, inner_grad)
    inner_bias_grad = jnp.sum(inner_grad.astype(jnp.float32), axis=0)
    hidden_grad = resid_two + matmul_nt(inner_grad, full_inner)
    resid_one, attn_gain_grad, attn_shift_grad = norm_backward(
        hidden_grad, normed_one, inverse_one, attn_gain
    )
    mixed_grad = resid_one.astype(jnp.bfloat16)
    output_weight_grad = matmul_tn(attn_low, mixed_grad)
    output_bias_grad = jnp.sum(mixed_grad.astype(jnp.float32), axis=0)
    attn_grad = matmul_nt(mixed_grad, full_output).astype(jnp.bfloat16)
    attn_heads = attn_grad.reshape(row_blocks, BLK, heads, head_dim)
    sparse_grad = jnp.where(is_global[:, None, None, None], jnp.zeros_like(attn_heads), attn_heads)
    probs_again = jnp.exp(sparse_scores() - sparse_lse)
    dprobs = jnp.einsum(
        "qahd,qhkd->qhak", sparse_grad, value_sel, preferred_element_type=jnp.float32
    )
    inner_sum = jnp.sum(probs_again * dprobs, axis=-1, keepdims=True)
    dscore_low = (probs_again * (dprobs - inner_sum)).astype(jnp.bfloat16)
    dquery = (
        jnp.einsum("qhak,qhkd->qahd", dscore_low, key_sel, preferred_element_type=jnp.float32)
        * 0.125
    )
    dkey_sel = (
        jnp.einsum("qhak,qahd->qhkd", dscore_low, query_heads, preferred_element_type=jnp.float32)
        * 0.125
    )
    dvalue_sel = jnp.einsum(
        "qhak,qahd->qhkd", probs_low, sparse_grad, preferred_element_type=jnp.float32
    )
    dkey_full = (
        jnp.zeros((nblocks, BLK, heads, head_dim), jnp.float32)
        .at[lists, :, head_ids]
        .add(dkey_sel.reshape(row_blocks, heads, slots, BLK, head_dim))
    )
    dvalue_full = (
        jnp.zeros((nblocks, BLK, heads, head_dim), jnp.float32)
        .at[lists, :, head_ids]
        .add(dvalue_sel.reshape(row_blocks, heads, slots, BLK, head_dim))
    )
    dkey_full = dkey_full.reshape(seq_len, heads, head_dim)
    dvalue_full = dvalue_full.reshape(seq_len, heads, head_dim)
    for number in range(len(slot_rows)):
        rows = slot_rows[number]
        place = slot_place[number]
        picked = lax.dynamic_index_in_dim(attn_heads, place, 0, keepdims=False)
        rows_grad = jnp.where(slot_use[number], picked, jnp.zeros_like(picked))
        seg_rows = lax.dynamic_index_in_dim(seg_query, place, 0, keepdims=False)
        gprobs = jnp.exp(global_scores(rows, seg_rows) - slot_lse[number])
        gdprobs = jnp.einsum(
            "ahd,khd->hak", rows_grad, values_flat, preferred_element_type=jnp.float32
        )
        ginner = jnp.sum(gprobs * gdprobs, axis=-1, keepdims=True)
        gscore_low = (gprobs * (gdprobs - ginner)).astype(jnp.bfloat16)
        row_query_grad = (
            jnp.einsum("hak,khd->ahd", gscore_low, keys_flat, preferred_element_type=jnp.float32)
            * 0.125
        )
        dkey_full = (
            dkey_full
            + jnp.einsum("hak,ahd->khd", gscore_low, rows, preferred_element_type=jnp.float32)
            * 0.125
        )
        dvalue_full = dvalue_full + jnp.einsum(
            "hak,ahd->khd", slot_low[number], rows_grad, preferred_element_type=jnp.float32
        )
        dquery = dquery.at[place].add(row_query_grad)
    dkey_own, dvalue_own = (
        lax.psum_scatter(
            dkey_full.reshape(seq_len, width).astype(jnp.bfloat16),
            "ctx",
            scatter_dimension=0,
            tiled=True,
        ).astype(jnp.float32),
        lax.psum_scatter(
            dvalue_full.reshape(seq_len, width).astype(jnp.bfloat16),
            "ctx",
            scatter_dimension=0,
            tiled=True,
        ).astype(jnp.float32),
    )
    dquery_low = dquery.reshape(rows_here, width).astype(jnp.bfloat16)
    dkey_low = dkey_own.astype(jnp.bfloat16)
    dvalue_low = dvalue_own.astype(jnp.bfloat16)
    query_weight_grad = matmul_tn(inputs_low, dquery_low)
    key_weight_grad = matmul_tn(inputs_low, dkey_low)
    value_weight_grad = matmul_tn(inputs_low, dvalue_low)
    query_bias_grad = jnp.sum(dquery_low.astype(jnp.float32), axis=0)
    value_bias_grad = jnp.sum(dvalue_low.astype(jnp.float32), axis=0)
    input_grad = (
        resid_one
        + matmul_nt(dquery_low, full_query)
        + matmul_nt(dkey_low, full_key)
        + matmul_nt(dvalue_low, full_value)
    )
    shards = (
        lax.psum_scatter(
            query_weight_grad.astype(jnp.bfloat16), "wshard", scatter_dimension=1, tiled=True
        ).astype(jnp.float32),
        lax.psum_scatter(
            key_weight_grad.astype(jnp.bfloat16), "wshard", scatter_dimension=1, tiled=True
        ).astype(jnp.float32),
        lax.psum_scatter(
            value_weight_grad.astype(jnp.bfloat16), "wshard", scatter_dimension=1, tiled=True
        ).astype(jnp.float32),
        lax.psum_scatter(
            output_weight_grad.astype(jnp.bfloat16), "wshard", scatter_dimension=1, tiled=True
        ).astype(jnp.float32),
        lax.psum_scatter(
            inner_weight_grad.astype(jnp.bfloat16), "wshard", scatter_dimension=1, tiled=True
        ).astype(jnp.float32),
        lax.psum_scatter(
            outer_weight_grad.astype(jnp.bfloat16), "wshard", scatter_dimension=1, tiled=True
        ).astype(jnp.float32),
        lax.psum_scatter(
            query_bias_grad.astype(jnp.bfloat16), "wshard", scatter_dimension=0, tiled=True
        ).astype(jnp.float32),
        lax.psum_scatter(
            value_bias_grad.astype(jnp.bfloat16), "wshard", scatter_dimension=0, tiled=True
        ).astype(jnp.float32),
        lax.psum_scatter(
            output_bias_grad.astype(jnp.bfloat16), "wshard", scatter_dimension=0, tiled=True
        ).astype(jnp.float32),
        lax.psum_scatter(
            inner_bias_grad.astype(jnp.bfloat16), "wshard", scatter_dimension=0, tiled=True
        ).astype(jnp.float32),
        lax.psum_scatter(
            outer_bias_grad.astype(jnp.bfloat16), "wshard", scatter_dimension=0, tiled=True
        ).astype(jnp.float32),
        lax.psum_scatter(
            attn_gain_grad.astype(jnp.bfloat16), "wshard", scatter_dimension=0, tiled=True
        ).astype(jnp.float32),
        lax.psum_scatter(
            attn_shift_grad.astype(jnp.bfloat16), "wshard", scatter_dimension=0, tiled=True
        ).astype(jnp.float32),
        lax.psum_scatter(
            mlp_gain_grad.astype(jnp.bfloat16), "wshard", scatter_dimension=0, tiled=True
        ).astype(jnp.float32),
        lax.psum_scatter(
            mlp_shift_grad.astype(jnp.bfloat16), "wshard", scatter_dimension=0, tiled=True
        ).astype(jnp.float32),
    )
    shards = (
        lax.psum(shards[0].astype(jnp.bfloat16), "ctx").astype(jnp.float32),
        lax.psum(shards[1].astype(jnp.bfloat16), "ctx").astype(jnp.float32),
        lax.psum(shards[2].astype(jnp.bfloat16), "ctx").astype(jnp.float32),
        lax.psum(shards[3].astype(jnp.bfloat16), "ctx").astype(jnp.float32),
        lax.psum(shards[4].astype(jnp.bfloat16), "ctx").astype(jnp.float32),
        lax.psum(shards[5].astype(jnp.bfloat16), "ctx").astype(jnp.float32),
        lax.psum(shards[6].astype(jnp.bfloat16), "ctx").astype(jnp.float32),
        lax.psum(shards[7].astype(jnp.bfloat16), "ctx").astype(jnp.float32),
        lax.psum(shards[8].astype(jnp.bfloat16), "ctx").astype(jnp.float32),
        lax.psum(shards[9].astype(jnp.bfloat16), "ctx").astype(jnp.float32),
        lax.psum(shards[10].astype(jnp.bfloat16), "ctx").astype(jnp.float32),
        lax.psum(shards[11].astype(jnp.bfloat16), "ctx").astype(jnp.float32),
        lax.psum(shards[12].astype(jnp.bfloat16), "ctx").astype(jnp.float32),
        lax.psum(shards[13].astype(jnp.bfloat16), "ctx").astype(jnp.float32),
        lax.psum(shards[14].astype(jnp.bfloat16), "ctx").astype(jnp.float32),
    )
    factor = thresholds / jnp.maximum(maxima, thresholds)
    root = jnp.sqrt(factor)
    columns = w_query.shape[1]
    column_ids = lax.axis_index("wshard") * columns + jnp.arange(columns, dtype=jnp.int32)
    onehot = column_ids[:, None] // head_dim == jnp.arange(heads, dtype=jnp.int32)[None, :]
    column_scale = jnp.sum(jnp.where(onehot, root[None, :], 0.0), axis=1)
    return (
        layer_output[None],
        input_grad[None],
        shards[0],
        shards[1],
        shards[2],
        shards[3],
        shards[4],
        shards[5],
        shards[6],
        shards[7],
        shards[8],
        shards[9],
        shards[10],
        shards[11],
        shards[12],
        shards[13],
        shards[14],
        w_query * column_scale[None, :],
        w_key * column_scale[None, :],
        maxima,
    )


def solution(mesh):
    in_specs = (
        P("wshard", "ctx", None),
        P("wshard", None),
        P("wshard", None),
        P(),
        P(),
        P(None, "wshard"),
        P(None, "wshard"),
        P(None, "wshard"),
        P(None, "wshard"),
        P(None, "wshard"),
        P(None, "wshard"),
        P("wshard"),
        P("wshard"),
        P("wshard"),
        P("wshard"),
        P("wshard"),
        P("wshard"),
        P("wshard"),
        P("wshard"),
        P("wshard"),
        P("wshard", "ctx", None),
    )
    out_specs = (
        P("wshard", "ctx", None),
        P("wshard", "ctx", None),
        P(None, "wshard"),
        P(None, "wshard"),
        P(None, "wshard"),
        P(None, "wshard"),
        P(None, "wshard"),
        P(None, "wshard"),
        P("wshard"),
        P("wshard"),
        P("wshard"),
        P("wshard"),
        P("wshard"),
        P("wshard"),
        P("wshard"),
        P("wshard"),
        P("wshard"),
        P(None, "wshard"),
        P(None, "wshard"),
        P(),
    )
    return jax.shard_map(
        per_device, mesh=mesh, in_specs=in_specs, out_specs=out_specs, check_vma=False
    )
```

profile of v0, /device:TPU:1, one launch (start us, length us, event | category | flops | bytes accessed | tf_op | source)
XLA Modules:
  0.0 1409.5 jit_solution(553393293131802215)
XLA Ops:
  20.5 31.4 %all-reduce.18 = (bf16[768]{0:T(1024)(128)(2,1)S(1)}, bf16[768]{0:T(1024)(128)(2,1)S(1)}, bf16[768]{0:T(1024)(128)(2,1)S(1)}, bf16[768]{0:T(1024)(128)(2,1)S(1)}...) all-reduce(bf16[768]{0:T(1024)(128)(2,1)S(1)} %dynamic-update-slice, ...), channel_id=1, replica_groups=mesh['ctx'=4,'wshard'=8] {'wshard'}, use_global_device_ids=true, to_apply=%add | all-reduce | flops 5376 | bytes 21504
  53.4 3.2 add_convert_fusion.1
  56.7 38.9 %all-gather.16.cloned.1.call-done = bf16[768,768]{0,1:T(8,128)(2,1)} async-done(((bf16[768,96]{0,1:T(8,128)(2,1)}), bf16[768,768]{0,1:T(8,128)(2,1)}) %all-gather.16.cloned.1.call-update) | async-done | bytes 1179664 | tf_op jit(solution)/shard_map/all_gather | solution.py:103
  95.6 3.0 convolution_convert_fusion.7
  112.7 22.3 %all-gather = bf16[8,1,384]{2,1,0:T(2,128)(2,1)S(1)} all-gather(bf16[1,1,384]{2,1,0:T(2,128)(2,1)S(1)} %reshape.600), channel_id=1, replica_groups=mesh['ctx'=4,'wshard'=8] {'wshard'}, dimensions={0}, use_global_device_ids=true | all-gather | bytes 6912 | tf_op jit(solution)/shard_map/all_gather | solution.py:111
  143.8 25.5 %all-gather.12.cloned.1.call-done = bf16[2048,768]{1,0:T(8,128)(2,1)} async-done(((bf16[512,768]{1,0:T(8,128)(2,1)}), bf16[2048,768]{1,0:T(8,128)(2,1)}) %all-gather.12.cloned.1.call-update) | async-done | bytes 3145744 | tf_op jit(solution)/shard_map/all_gather | solution.py:134
  169.3 10.6 reshape.619
  179.9 7.6 copy.193
  187.6 12.3 all-gather.18.cloned.1.call-done
  199.9 3.2 copy.188
  217.8 3.4 copy.185
  221.1 4.7 convolution_bitcast_fusion
  227.5 10.6 reshape.620
  238.1 7.6 copy.201
  245.8 11.4 gather_fusion
  257.2 11.8 gather_fusion.2
  269.0 10.6 fusion.84
  279.6 6.6 fusion
  286.2 11.4 fusion.13
  300.1 3.5 convert_element_type.294
  307.5 17.0 %all-gather.22.cloned.1.call-done = bf16[768,3072]{1,0:T(8,128)(2,1)} async-done(((bf16[768,384]{1,0:T(8,128)(2,1)}), bf16[768,3072]{1,0:T(8,128)(2,1)}) %all-gather.22.cloned.1.call-update) | async-done | bytes 4718608 | tf_op jit(solution)/shard_map/all_gather | solution.py:106
  324.6 8.1 fusion.74
  332.7 72.2 %all-gather.24.cloned.1.call-done = bf16[3072,768]{0,1:T(8,128)(2,1)} async-done(((bf16[3072,96]{0,1:T(8,128)(2,1)}), bf16[3072,768]{0,1:T(8,128)(2,1)}) %all-gather.24.cloned.1.call-update) | async-done | bytes 4718608 | tf_op jit(solution)/shard_map/all_gather | solution.py:107
  404.9 7.9 fusion.86
  417.4 7.6 fusion.87
  425.0 3.6 multiply_reduce_fusion.3
  441.5 15.1 %select_reduce_fusion = (f32[12]{0:T(128)}, f32[8,12,64]{2,1,0:T(8,128)S(1)}, f32[8,12,64,512]{3,2,1,0:T(8,128)}) fusion(f32[8,12,64,512]{3,2,1,0:T(8,128)} %get-tuple-element.122, pred[8]{0:T(512)(128)(4,1)S(1)} %get-tuple-element.97, f32[8,12,64]{2,1,0:T(8,128)S(1)} %log_add_fusion, bf16[8,12,512,64]{3,2,1,0:T(8,128)(2,1)} %bitcast.223, ...), kind=kOutput, calls=%fused_computation.5 | convolution fusion | flops 418375680 | bytes 32292920 | tf_op jit(solution)/shard_map/qahd,qhkd->qhak/dot_general | solution.py:236
  456.6 9.6 multiply_convert_fusion
  468.8 6.2 broadcast_multiply_fusion
  475.1 17.7 %copy.241 = f32[8,12,512,64]{3,2,1,0:T(8,128)} copy(f32[8,12,512,64]{2,3,1,0:T(8,128)} %broadcast_multiply_fusion) | data formatting | bytes 25165824 | tf_op jit(solution)/shard_map/reshape | solution.py:255
  492.8 6.1 broadcast.396.clone.1
  498.8 122.0 %scatter_fusion = f32[32,64,12,64]{3,1,2,0:T(8,128)} fusion(f32[32,64,12,64]{3,1,2,0:T(8,128)} %broadcast.396.clone.1, s32[768]{0:T(1024)S(1)} %copy-done.4, f32[768,64,64]{2,1,0:T(8,128)} %bitcast.217), kind=kCustom, calls=%fused_computation.3 | custom fusion | flops 3145728 | bytes 37754880 | tf_op jit(solution)/shard_map/scatter-add | solution.py:255
  620.8 13.3 copy.218
  634.1 11.9 reshape.535
  646.0 5.1 fusion.77
  651.1 3.8 multiply_convert_fusion.2
  660.7 3.5 fusion.9
  665.0 15.0 %fusion.22 = f32[8,12,512,64]{3,2,1,0:T(8,128)} fusion(bf16[8,64,12,64]{1,0,3,2:T(8,128)(2,1)} %broadcast_select_fusion, f32[8,12,64,512]{3,2,1,0:T(8,128)} %get-tuple-element.122, f32[8,12,64]{2,1,0:T(8,128)S(1)} %copy-done.44, f32[8,12,64]{2,1,0:T(8,128)S(1)} %get-tuple-element.121), kind=kOutput, calls=%fused_computation.85 | convolution fusion | flops 412090368 | bytes 26001408 | tf_op jit(solution)/shard_map/reshape | solution.py:260
  680.0 6.1 broadcast.396.clone
  686.0 121.9 %scatter_fusion.1 = f32[32,64,12,64]{3,1,2,0:T(8,128)} fusion(f32[32,64,12,64]{3,1,2,0:T(8,128)} %broadcast.396.clone, s32[768]{0:T(1024)S(1)} %copy-done.4, f32[768,64,64]{2,1,0:T(8,128)} %bitcast.228), kind=kCustom, calls=%fused_computation.4 | custom fusion | flops 3145728 | bytes 37754880 | tf_op jit(solution)/shard_map/scatter-add | solution.py:260
  808.0 13.3 copy.224
  821.3 11.7 reshape.537
  833.0 3.2 fusion.39
  837.8 2.7 fusion.8
  841.2 7.4 convolution_convert_fusion.1
  848.6 6.9 copy.247
  856.8 9.3 convolution_multiply_fusion
  874.5 3.6 convert_element_type.322
  878.0 3.0 fusion.15
  881.1 3.1 convolution_convert_fusion.2
  884.2 2.9 fusion.16
  887.3 3.3 fusion.17
  890.6 8.1 convolution_convert_fusion
  901.9 41.2 %pmax.7 = f32[12]{0:T(128)S(1)} all-reduce(f32[12]{0:T(128)S(1)} %fusion.58), channel_id=1, replica_groups=mesh['ctx'=4,'wshard'=8] {'ctx','wshard'}, use_global_device_ids=true, to_apply=%region_66.67 | all-reduce | flops 12 | bytes 96 | tf_op jit(solution)/shard_map/pmax | solution.py:205
  945.2 3.5 fusion.88
  950.3 30.3 %all-reduce.17 = (bf16[768]{0:T(1024)(128)(2,1)S(1)}, bf16[768]{0:T(1024)(128)(2,1)S(1)}, bf16[768]{0:T(1024)(128)(2,1)S(1)}, bf16[768]{0:T(1024)(128)(2,1)S(1)}...) all-reduce(bf16[768]{0:T(1024)(128)(2,1)S(1)} %dynamic-update-slice, ...), channel_id=1, replica_groups=mesh['ctx'=4,'wshard'=8] {'wshard'}, use_global_device_ids=true, to_apply=%add.7 | all-reduce | flops 9984 | bytes 39936
  982.7 62.3 %reduce-scatter.15.cloned.1.call-done = bf16[768,96]{0,1:T(8,128)(2,1)} async-done(((bf16[768,768]{0,1:T(8,128)(2,1)}), bf16[768,96]{0,1:T(8,128)(2,1)}) %reduce-scatter.15.cloned.1.call-update) | async-done | bytes 147472 | tf_op jit(solution)/shard_map/reduce_scatter | solution.py:318
  1045.0 66.4 %reduce-scatter.21.cloned.1.call-done = bf16[768,96]{0,1:T(8,128)(2,1)} async-done(((bf16[768,768]{0,1:T(8,128)(2,1)}), bf16[768,96]{0,1:T(8,128)(2,1)}) %reduce-scatter.21.cloned.1.call-update) | async-done | bytes 147472 | tf_op jit(solution)/shard_map/reduce_scatter | solution.py:327
  1111.5 66.8 %reduce-scatter.17.cloned.1.call-done = bf16[768,96]{0,1:T(8,128)(2,1)} async-done(((bf16[768,768]{0,1:T(8,128)(2,1)}), bf16[768,96]{0,1:T(8,128)(2,1)}) %reduce-scatter.17.cloned.1.call-update) | async-done | bytes 147472 | tf_op jit(solution)/shard_map/reduce_scatter | solution.py:321
  1178.3 66.2 %reduce-scatter.19.cloned.1.call-done = bf16[768,96]{0,1:T(8,128)(2,1)} async-done(((bf16[768,768]{0,1:T(8,128)(2,1)}), bf16[768,96]{0,1:T(8,128)(2,1)}) %reduce-scatter.19.cloned.1.call-update) | async-done | bytes 147472 | tf_op jit(solution)/shard_map/reduce_scatter | solution.py:324
  1244.4 99.3 %reduce-scatter.23.cloned.1.call-done = bf16[3072,96]{0,1:T(8,128)(2,1)} async-done(((bf16[3072,768]{0,1:T(8,128)(2,1)}), bf16[3072,96]{0,1:T(8,128)(2,1)}) %reduce-scatter.23.cloned.1.call-update) | async-done | bytes 589840 | tf_op jit(solution)/shard_map/reduce_scatter | solution.py:333
  1345.9 5.8 all-reduce.19
  1358.8 3.4 add_bitcast_fusion
  1362.2 30.7 %all-reduce.23.cloned.1.call-done = (bf16[768,96]{0,1:T(8,128)(2,1)}, bf16[768,96]{0,1:T(8,128)(2,1)}, bf16[768,96]{0,1:T(8,128)(2,1)}, bf16[768,96]{0,1:T(8,128...) async-done(((bf16[768,96]{0,1:T(8,128)(2,1)}, bf16[768,96]{0,1:T(8,128)(2,1)}, bf16[768,96]{0,1:T(8,128)(2,1)}, bf16[768,96]{0,1:T(8,128)(2,1)}, ...) | async-done | bytes 1769488 | tf_op jit(solution)/shard_map/psum | solution.py:365
  (379 shorter events, 122.0 us)
Async XLA Ops:
  7.2 99.2 %copy-start = (s32[32,12,3]{0,2,1:T(4,128)S(1)}, s32[32,12,3]{0,2,1:T(4,128)}, u32[]{:S(2)}) copy-start(s32[32,12,3]{0,2,1:T(4,128)} %param.28) | copy-start | bytes 13828
  7.2 46.2 %all-gather.10.cloned.1.call-start = ((), (), s32[]{:S(2)}) async-start(), calls=%async_computation.8 | async-start | bytes 1327104 | tf_op jit(solution)/shard_map/all_gather | solution.py:104
  8.9 86.7 %all-gather.16.cloned.1.call-start = ((), (), s32[]{:S(2)}) async-start(), calls=%async_computation.11 | async-start | bytes 1327104 | tf_op jit(solution)/shard_map/all_gather | solution.py:103
  10.6 127.7 %all-gather.14.cloned.1.call-start = ((), (), s32[]{:S(2)}) async-start(), calls=%async_computation.10 | async-start | bytes 1327104 | tf_op jit(solution)/shard_map/all_gather | solution.py:102
  12.3 157.0 %all-gather.12.cloned.1.call-start = ((), (), s32[]{:S(2)}) async-start(), calls=%async_computation.9 | async-start | bytes 3932160 | tf_op jit(solution)/shard_map/all_gather | solution.py:134
  53.4 85.0 %copy-start.38 = (bf16[512,768]{1,0:T(8,128)(2,1)}, bf16[512,768]{1,0:T(8,128)(2,1)S(1)}, u32[]{:S(2)}) copy-start(bf16[512,768]{1,0:T(8,128)(2,1)S(1)} %bitcast_convert_fusion) | copy-start | bytes 2359300
  56.6 42.0 %copy-start.42 = (f32[768,96]{0,1:T(8,128)S(1)}, f32[768,96]{0,1:T(8,128)}, u32[]{:S(2)}) copy-start(f32[768,96]{0,1:T(8,128)} %param.33) | copy-start | bytes 884740
  56.6 42.8 %copy-start.35 = (f32[768,384]{1,0:T(8,128)S(1)}, f32[768,384]{1,0:T(8,128)}, u32[]{:S(2)}) copy-start(f32[768,384]{1,0:T(8,128)} %param.34) | copy-start | bytes 3538948
  56.7 43.7 %copy-start.36 = (f32[3072,96]{0,1:T(8,128)S(1)}, f32[3072,96]{0,1:T(8,128)}, u32[]{:S(2)}) copy-start(f32[3072,96]{0,1:T(8,128)} %param.35) | copy-start | bytes 3538948
  56.7 143.2 %all-gather.18.cloned.1.call-start = ((), (), s32[]{:S(2)}) async-start(), calls=%async_computation.12 | async-start | bytes 3932160 | tf_op jit(solution)/shard_map/all_gather | solution.py:133
  98.6 8.6 copy-start.49
  98.6 204.9 %all-gather.20.cloned.1.call-start = ((), (), s32[]{:S(2)}) async-start(), calls=%async_computation.13 | async-start | bytes 1327104 | tf_op jit(solution)/shard_map/all_gather | solution.py:105
  99.4 225.2 %all-gather.22.cloned.1.call-start = ((), (), s32[]{:S(2)}) async-start(), calls=%async_computation.14 | async-start | bytes 5308416 | tf_op jit(solution)/shard_map/all_gather | solution.py:106
  100.3 304.6 %all-gather.24.cloned.1.call-start = ((), (), s32[]{:S(2)}) async-start(), calls=%async_computation.15 | async-start | bytes 5308416 | tf_op jit(solution)/shard_map/all_gather | solution.py:107
  101.3 11.4 copy-start.69
  101.3 782.9 %reduce-scatter.11.cloned.1.call-start = ((), (), s32[]{:S(2)}) async-start(), calls=%async_computation.16 | async-start | bytes 3932160 | tf_op jit(solution)/shard_map/reduce_scatter | solution.py:290
  112.7 292.2 %copy-start.64 = (f32[768]{0:T(1024)}, f32[768]{0:T(1024)S(1)}, u32[]{:S(2)}) copy-start(f32[768]{0:T(1024)S(1)} %convert_element_type.301) | copy-start | bytes 9220
  112.7 315.9 %copy-start.54 = (f32[768]{0:T(1024)}, f32[768]{0:T(1024)S(1)}, u32[]{:S(2)}) copy-start(f32[768]{0:T(1024)S(1)} %convert_element_type.299) | copy-start | bytes 9220
  135.1 280.5 %copy-start.56 = (f32[8,1,384]{2,1,0:T(1,128)}, f32[8,1,384]{2,1,0:T(1,128)S(1)}, u32[]{:S(2)}) copy-start(f32[8,1,384]{2,1,0:T(1,128)S(1)} %convert_element_type.357) | copy-start | bytes 36868
  135.1 279.4 %copy-start.45 = (f32[768]{0:T(1024)}, f32[768]{0:T(1024)S(1)}, u32[]{:S(2)}) copy-start(f32[768]{0:T(1024)S(1)} %convert_element_type.311) | copy-start | bytes 9220
  141.6 38.4 %copy-start.15 = (bf16[8,64,12,64]{1,0,3,2:T(8,128)(2,1)}, bf16[8,64,12,64]{1,0,3,2:T(8,128)(2,1)S(1)}, u32[]{:S(2)}) copy-start(bf16[8,64,12,64]{1,0,3,2:T(8,128)(2,1)S(1)} %reshape.525) | copy-start | bytes 2359300
  143.8 67.1 %copy-start.28 = (bf16[1,64,12,64]{3,1,2,0:T(8,128)(2,1)}, bf16[1,64,12,64]{3,1,2,0:T(8,128)(2,1)S(1)}, u32[]{:S(2)}) copy-start(bf16[1,64,12,64]{3,1,2,0:T(8,128)(2,1)S(1)} %copy.187) | copy-start | bytes 294916
  203.0 7.9 copy-start.5
  257.2 11.8 copy-start.16
  257.2 11.8 copy-start.31
  257.2 11.8 copy-start.41
  279.6 6.6 copy-start.72
  279.6 6.6 copy-start.78
  279.6 6.6 copy-start.79
  286.2 21.3 %copy-start.43 = (f32[8,12,64]{2,1,0:T(8,128)}, f32[8,12,64]{2,1,0:T(8,128)S(1)}, u32[]{:S(2)}) copy-start(f32[8,12,64]{2,1,0:T(8,128)S(1)} %fusion) | copy-start | bytes 73732
  297.7 5.9 copy-start.23
  306.0 122.6 %copy-start.52 = (f32[512]{0:T(512)}, f32[512]{0:T(512)S(1)}, u32[]{:S(2)}) copy-start(f32[512]{0:T(512)S(1)} %broadcast_multiply_fusion.8) | copy-start | bytes 6148
  307.4 121.2 %copy-start.60 = (f32[512]{0:T(512)}, f32[512]{0:T(512)S(1)}, u32[]{:S(2)}) copy-start(f32[512]{0:T(512)S(1)} %add_rsqrt_fusion.1) | copy-start | bytes 6148
  307.5 97.4 %copy-start.26 = (f32[512,768]{1,0:T(8,128)S(1)}, f32[512,768]{1,0:T(8,128)}, u32[]{:S(2)}) copy-start(f32[512,768]{1,0:T(8,128)} %copy-done.25) | copy-start | bytes 4718596
  404.9 8.3 copy-start.17
  404.9 10.7 copy-start.80
  414.5 10.5 slice-start.4
  415.6 9.4 copy-start.32
  417.4 7.6 slice-start.5
  492.8 6.1 copy-start.4
  634.1 11.9 copy-start.9
  646.0 10.6 slice-start
  651.1 5.5 slice-start.1
  655.0 5.7 slice-start.2
  664.2 223.1 %reduce-scatter.13.cloned.1.call-start = ((), (), s32[]{:S(2)}) async-start(), calls=%async_computation.17 | async-start | bytes 3932160 | tf_op jit(solution)/shard_map/reduce_scatter | solution.py:296
  840.5 140.1 %reduce-scatter.25.cloned.1.call-start = ((), (), s32[]{:S(2)}) async-start(), calls=%async_computation.23 | async-start | bytes 5308416
  855.4 189.6 %reduce-scatter.15.cloned.1.call-start = ((), (), s32[]{:S(2)}) async-start(), calls=%async_computation.18 | async-start | bytes 1327104 | tf_op jit(solution)/shard_map/reduce_scatter | solution.py:318
  874.5 6.6 copy-start.20
  881.0 230.5 %reduce-scatter.21.cloned.1.call-start = ((), (), s32[]{:S(2)}) async-start(), calls=%async_computation.21 | async-start | bytes 1327104 | tf_op jit(solution)/shard_map/reduce_scatter | solution.py:327
  884.2 294.1 %reduce-scatter.17.cloned.1.call-start = ((), (), s32[]{:S(2)}) async-start(), calls=%async_computation.19 | async-start | bytes 1327104 | tf_op jit(solution)/shard_map/reduce_scatter | solution.py:321
  887.2 357.3 %reduce-scatter.19.cloned.1.call-start = ((), (), s32[]{:S(2)}) async-start(), calls=%async_computation.20 | async-start | bytes 1327104 | tf_op jit(solution)/shard_map/reduce_scatter | solution.py:324
  890.6 453.2 %reduce-scatter.23.cloned.1.call-start = ((), (), s32[]{:S(2)}) async-start(), calls=%async_computation.22 | async-start | bytes 5308416 | tf_op jit(solution)/shard_map/reduce_scatter | solution.py:333
  898.7 44.5 %copy-start.76 = (f32[12]{0:T(128)S(1)}, f32[12]{0:T(128)}, u32[]{:S(2)}) copy-start(f32[12]{0:T(128)} %param.29) | copy-start | bytes 148
  898.7 44.6 %copy-start.37 = (f32[768,96]{0,1:T(8,128)S(1)}, f32[768,96]{0,1:T(8,128)}, u32[]{:S(2)}) copy-start(f32[768,96]{0,1:T(8,128)} %param.31) | copy-start | bytes 884740
  898.8 494.1 %all-reduce.23.cloned.1.call-start = ((), (), s32[]{:S(2)}) async-start(), calls=%async_computation.24 | async-start | bytes 3538944 | tf_op jit(solution)/shard_map/psum | solution.py:365
  943.1 5.6 copy-start.77
  948.7 395.0 %copy-start.13 = (f32[512,768]{1,0:T(8,128)S(1)}, f32[512,768]{1,0:T(8,128)}, u32[]{:S(2)}) copy-start(f32[512,768]{1,0:T(8,128)} %copy-done.12) | copy-start | bytes 4718596
  948.7 395.0 %copy-start.46 = (f32[768]{0:T(1024)S(1)}, f32[768]{0:T(1024)}, u32[]{:S(2)}) copy-start(f32[768]{0:T(1024)} %copy-done.45) | copy-start | bytes 9220
  948.7 395.1 %copy-start.48 = (f32[512]{0:T(512)S(1)}, f32[512]{0:T(512)}, u32[]{:S(2)}) copy-start(f32[512]{0:T(512)} %copy-done.47) | copy-start | bytes 6148
  948.7 395.1 %copy-start.51 = (f32[512]{0:T(512)S(1)}, f32[512]{0:T(512)}, u32[]{:S(2)}) copy-start(f32[512]{0:T(512)} %copy-done.50) | copy-start | bytes 6148
  1345.3 13.5 copy-start.27
  1351.7 7.1 copy-start.34
  1358.8 44.0 %copy-start.1 = (s32[32,12,3]{0,2,1:T(4,128)S(1)}, s32[32,12,3]{0,2,1:T(4,128)}, u32[]{:S(2)}) copy-start(s32[32,12,3]{0,2,1:T(4,128)} %param.28) | copy-start | bytes 13828
  1392.9 8.8 copy-start.40
  (41 other events, 118.4 us)
Sparse Core Ops, SparseCore 0:
  10.8 42.1 all-gather.9
  55.8 39.7 all-gather.15
  98.4 39.9 all-gather.13
  140.4 28.8 all-gather.11
  171.3 28.5 all-gather.17
  202.5 39.3 all-gather.19
  244.0 80.5 all-gather.21
  327.3 77.5 all-gather.23
  664.3 37.1 reduce-scatter.10
  840.7 37.7 reduce-scatter.12
  882.1 96.7 reduce-scatter.24
  982.7 62.2 reduce-scatter.14
  1048.4 62.9 reduce-scatter.20
  1115.3 62.9 reduce-scatter.16
  1181.5 62.9 reduce-scatter.18
  1247.9 95.7 reduce-scatter.22
  1346.4 46.4 all-reduce.22
where the time goes:
time: 1420 us; the launch traced here: 1410 us
  waiting for transfers between devices  560 us (39%)
  other arithmetic  316 us (22%)
  local copies, waits for them, and re-layouts  206 us (15%)
  matrix products  175 us (12%)
  blocking collectives  131 us (9%)
  between operations  20 us (1%)
    scatter-add x1, other arithmetic, per_device(): dkey_full = jnp.zeros((nblocks, BLK, heads, head_dim), jnp.float32).at[li...  122 us
    scatter-add x1, other arithmetic, per_device(): dvalue_full = jnp.zeros((nblocks, BLK, heads, head_dim), jnp.float32).at[...  122 us
    reduce_scatter x1, waiting for transfers between devices, per_device(): lax.psum_scatter(outer_weight_grad.astype(jnp.bfloat16), 'wshard', scatte...  99.3 us
    all_gather x1, waiting for transfers between devices, per_device(): lax.all_gather(w_outer.astype(jnp.bfloat16), 'wshard', axis=1, tiled=True)  72.2 us
    reduce_scatter x1, waiting for transfers between devices, per_device(): lax.psum_scatter(key_weight_grad.astype(jnp.bfloat16), 'wshard', scatter_...  66.8 us
    reduce_scatter x1, waiting for transfers between devices, per_device(): lax.psum_scatter(output_weight_grad.astype(jnp.bfloat16), 'wshard', scatt...  66.4 us
    reduce_scatter x1, waiting for transfers between devices, per_device(): lax.psum_scatter(value_weight_grad.astype(jnp.bfloat16), 'wshard', scatte...  66.2 us
    reduce_scatter x1, waiting for transfers between devices, per_device(): lax.psum_scatter(query_weight_grad.astype(jnp.bfloat16), 'wshard', scatte...  62.3 us
  transfers between devices with their start and end apart: 17, of which 12 were waited for; matrix products, arithmetic and copies ran while one was open for 30% of the time, Pallas kernels for 0%

commit v1 on v0

v1 whole, which is shorter than its diff:
```python
import functools

import jax
import jax.numpy as jnp
from jax import lax
from jax.experimental import pallas as pl
from jax.experimental.pallas import tpu as pltpu
from jax.sharding import PartitionSpec as P

BLK = 64
EPSILON = 1e-05
NEG = -1e30
UNROLL = 4
LOW = jnp.bfloat16
F32 = jnp.float32


def dot_nn(left, right):
    return lax.dot_general(left, right, (((1,), (0,)), ((), ())), preferred_element_type=F32)


def dot_tn(left, right):
    return lax.dot_general(left, right, (((0,), (0,)), ((), ())), preferred_element_type=F32)


def dot_nt(left, right):
    return lax.dot_general(left, right, (((1,), (1,)), ((), ())), preferred_element_type=F32)


def norm_forward(values, gain, shift):
    centre = values - jnp.mean(values, axis=-1, keepdims=True)
    inverse = lax.rsqrt(jnp.mean(centre * centre, axis=-1, keepdims=True) + EPSILON)
    normed = centre * inverse
    return (normed * gain + shift, normed, inverse)


def norm_backward(upstream, normed, inverse, gain):
    scaled = upstream * gain
    mean_one = jnp.mean(scaled, axis=-1, keepdims=True)
    mean_two = jnp.mean(scaled * normed, axis=-1, keepdims=True)
    result = inverse * (scaled - mean_one - normed * mean_two)
    return (result, jnp.sum(upstream * normed, axis=0), jnp.sum(upstream, axis=0))


def gelu_and_slope(v):
    c = 0.7978845608028654
    t = jnp.tanh(c * (v + 0.044715 * v * v * v))
    half = 0.5 * (1.0 + t)
    slope = half + 0.5 * v * (1.0 - t * t) * (c * (1.0 + 3 * 0.044715 * v * v))
    return v * half, slope


def halves():
    lane = lax.broadcasted_iota(jnp.int32, (BLK, 2 * BLK), 1)
    return lane < BLK


def stack_pair(tile):
    low = jnp.where(halves(), 1.0, 0.0).astype(tile.dtype)
    high = jnp.where(halves(), 0.0, 1.0).astype(tile.dtype)
    return jnp.concatenate([tile * low, tile * high], axis=0)


def unstack_pair(rows):
    return jnp.where(halves(), rows[:BLK], rows[BLK:])


def rows_of(ref, block, count=1):
    return ref[pl.ds(pl.multiple_of(block * BLK, BLK), count * BLK), :]


def shared_rows(ref, index, base):
    return jnp.concatenate([rows_of(ref, index[base], 3), rows_of(ref, index[base + 3])], axis=0)


def own_rows(ref, index, base):
    return jnp.concatenate([rows_of(ref, index[base + j]) for j in range(4, 8)], axis=0)


def attend_kernel(index, active, flags, q_ref, k_ref, v_ref, seg_q, seg_k, seg_row, o_ref, p_ref, og_ref, pg_ref, top_ref, score, *, heads):
    pair = pl.program_id(0)
    step = pl.program_id(1)
    wide = lax.broadcasted_iota(jnp.int32, (1, 2 * BLK), 1) < BLK
    length = k_ref.shape[0]

    @pl.when(step == 0)
    def _():
        top_ref[...] = jnp.full(top_ref.shape, NEG, F32)

        @pl.when(flags[1] == 0)
        def _():
            og_ref[...] = jnp.zeros(og_ref.shape, og_ref.dtype)
            pg_ref[...] = jnp.zeros(pg_ref.shape, pg_ref.dtype)

        @pl.when(flags[1] != 0)
        def _():
            place = flags[0]
            q2 = stack_pair(rows_of(q_ref, place))
            sq = rows_of(seg_q, place)
            sq = jnp.concatenate([sq, sq], axis=0)
            top = jnp.full((2 * BLK, 1), NEG, F32)
            cut = 512
            for j in range(length // cut):
                raw = dot_nt(q2, k_ref[j * cut : (j + 1) * cut, :])
                raw = jnp.where(seg_row[:, j * cut : (j + 1) * cut] == sq, raw, NEG)
                score[:, j * cut : (j + 1) * cut] = raw
                top = jnp.maximum(top, jnp.max(raw, axis=1, keepdims=True))
            total = jnp.zeros((2 * BLK, 1), F32)
            for j in range(length // cut):
                power = jnp.exp(score[:, j * cut : (j + 1) * cut] - top)
                score[:, j * cut : (j + 1) * cut] = power
                total = total + jnp.sum(power, axis=1, keepdims=True)
            scale = 1.0 / total
            acc = jnp.zeros((2 * BLK, 2 * BLK), F32)
            for j in range(length // cut):
                prob = (score[:, j * cut : (j + 1) * cut] * scale).astype(LOW)
                pg_ref[0, :, j * cut : (j + 1) * cut] = prob
                acc = acc + dot_nn(prob, v_ref[j * cut : (j + 1) * cut, :])
            og_ref[...] = unstack_pair(acc).astype(LOW)
            top_ref[0] = jnp.maximum(top_ref[0], jnp.broadcast_to(top, top_ref.shape[1:]))

    for u in range(UNROLL):
        b = step * UNROLL + u
        place = flags[2] + b
        q2 = stack_pair(rows_of(q_ref, place))
        sq = rows_of(seg_q, place)
        sq = jnp.concatenate([sq, sq], axis=0)
        base = (b * heads + 2 * pair) * 8
        shared = dot_nt(q2, shared_rows(k_ref, index, base))
        own = jnp.concatenate(
            [dot_nt(q2[h * BLK : (h + 1) * BLK], own_rows(k_ref, index, base + 8 * h)) for h in range(2)],
            axis=0,
        )

        def seg_of(at, j):
            first = seg_k[pl.ds(active[at + j], 1), :]
            second = seg_k[pl.ds(active[at + j + 1], 1), :]
            return jnp.where(wide, first, second)

        raw_s = jnp.where(jnp.concatenate([seg_of(base, 0), seg_of(base, 2)], axis=1) == sq, shared, NEG)
        seg_own = [
            jnp.broadcast_to(
                jnp.concatenate([seg_of(base + 8 * h, 4), seg_of(base + 8 * h, 6)], axis=1), (BLK, 4 * BLK)
            )
            for h in range(2)
        ]
        raw_o = jnp.where(jnp.concatenate(seg_own, axis=0) == sq, own, NEG)
        top = jnp.maximum(jnp.max(raw_s, axis=1, keepdims=True), jnp.max(raw_o, axis=1, keepdims=True))
        power_s = jnp.exp(raw_s - top)
        power_o = jnp.exp(raw_o - top)
        scale = 1.0 / (jnp.sum(power_s, axis=1, keepdims=True) + jnp.sum(power_o, axis=1, keepdims=True))
        prob_s = (power_s * scale).astype(LOW)
        prob_o = (power_o * scale).astype(LOW)
        p_ref[0, u, :, : 4 * BLK] = prob_s
        p_ref[0, u, :, 4 * BLK :] = prob_o
        out = dot_nn(prob_s, shared_rows(v_ref, index, base))
        out = out + jnp.concatenate(
            [
                dot_nn(prob_o[h * BLK : (h + 1) * BLK], own_rows(v_ref, index, base + 8 * h))
                for h in range(2)
            ],
            axis=0,
        )
        o_ref[u * BLK : (u + 1) * BLK, :] = unstack_pair(out).astype(LOW)
        used = jnp.where(flags[3 + b] != 0, jnp.full_like(top, NEG), top)
        top_ref[0] = jnp.maximum(top_ref[0], jnp.broadcast_to(used, top_ref.shape[1:]))


def pull_kernel(index, active, flags, q_ref, k_ref, v_ref, do_ref, dog_ref, p_ref, pg_ref, dq_ref, dk_ref, dv_ref, dk, dv, score, *, heads):
    del active
    pair = pl.program_id(0)
    step = pl.program_id(1)
    steps = pl.num_programs(1)
    length = k_ref.shape[0]

    @pl.when(step == 0)
    def _():
        dk[...] = jnp.zeros(dk.shape, F32)
        dv[...] = jnp.zeros(dv.shape, F32)
        dq_ref[...] = jnp.zeros(dq_ref.shape, dq_ref.dtype)

    def add(ref, block, value):
        at = pl.ds(pl.multiple_of(block * BLK, BLK), value.shape[0])
        ref[at, :] += value

    for u in range(UNROLL):
        b = step * UNROLL + u
        place = flags[2] + b
        q2 = stack_pair(rows_of(q_ref, place))
        keep = jnp.where(flags[3 + b] != 0, 0.0, 1.0).astype(LOW)
        do2 = stack_pair(do_ref[u * BLK : (u + 1) * BLK, :] * keep)
        base = (b * heads + 2 * pair) * 8
        ks = shared_rows(k_ref, index, base)
        ko = [own_rows(k_ref, index, base + 8 * h) for h in range(2)]
        vs = shared_rows(v_ref, index, base)
        vo = [own_rows(v_ref, index, base + 8 * h) for h in range(2)]
        prob_s = p_ref[0, u, :, : 4 * BLK]
        prob_o = p_ref[0, u, :, 4 * BLK :]
        dp_s = dot_nt(do2, vs)
        dp_o = jnp.concatenate([dot_nt(do2[h * BLK : (h + 1) * BLK], vo[h]) for h in range(2)], axis=0)
        ps = prob_s.astype(F32)
        po = prob_o.astype(F32)
        ts = ps * dp_s
        to = po * dp_o
        total = jnp.sum(ts, axis=1, keepdims=True) + jnp.sum(to, axis=1, keepdims=True)
        ds_s = (ts - ps * total).astype(LOW)
        ds_o = (to - po * total).astype(LOW)
        dq = dot_nn(ds_s, ks) + jnp.concatenate(
            [dot_nn(ds_o[h * BLK : (h + 1) * BLK], ko[h]) for h in range(2)], axis=0
        )
        at = pl.ds(pl.multiple_of(place * BLK, BLK), BLK)
        dq_ref[at, :] = (unstack_pair(dq) * 0.125).astype(LOW)
        dks = dot_tn(ds_s, q2)
        dvs = dot_tn(prob_s, do2)
        add(dk, index[base], dks[: 3 * BLK])
        add(dk, index[base + 3], dks[3 * BLK :])
        add(dv, index[base], dvs[: 3 * BLK])
        add(dv, index[base + 3], dvs[3 * BLK :])
        for h in range(2):
            part = slice(h * BLK, (h + 1) * BLK)
            dko = dot_tn(ds_o[part], q2[part])
            dvo = dot_tn(prob_o[part], do2[part])
            for j in range(4):
                add(dk, index[base + 8 * h + 4 + j], dko[j * BLK : (j + 1) * BLK])
                add(dv, index[base + 8 * h + 4 + j], dvo[j * BLK : (j + 1) * BLK])

    @pl.when((step == steps - 1) & (flags[1] != 0))
    def _():
        place = flags[0]
        q2 = stack_pair(rows_of(q_ref, place))
        do2 = stack_pair(dog_ref[...])
        cut = 512
        total = jnp.zeros((2 * BLK, 1), F32)
        for j in range(length // cut):
            part = slice(j * cut, (j + 1) * cut)
            dp = dot_nt(do2, v_ref[part, :])
            score[:, part] = dp
            total = total + jnp.sum(pg_ref[0, :, part].astype(F32) * dp, axis=1, keepdims=True)
        acc = jnp.zeros((2 * BLK, 2 * BLK), F32)
        for j in range(length // cut):
            part = slice(j * cut, (j + 1) * cut)
            prob = pg_ref[0, :, part]
            ds = (prob.astype(F32) * (score[:, part] - total)).astype(LOW)
            acc = acc + dot_nn(ds, k_ref[part, :])
            dk[part, :] += dot_tn(ds, q2)
            dv[part, :] += dot_tn(prob, do2)
        at = pl.ds(pl.multiple_of(place * BLK, BLK), BLK)
        dq_ref[at, :] = (unstack_pair(acc) * 0.125).astype(LOW)

    @pl.when(step == steps - 1)
    def _():
        dk_ref[...] = dk[...].astype(LOW)
        dv_ref[...] = dv[...].astype(LOW)


def attend(index, active, flags, query, key, value, seg_col, seg_rep, seg_row, blocks, heads):
    length, width = key.shape
    pairs = width // (2 * BLK)
    steps = blocks // UNROLL
    column = pl.BlockSpec((length, 2 * BLK), lambda p, s, *_: (0, p))
    whole = lambda shape: pl.BlockSpec(shape, lambda p, s, *_: (0,) * len(shape))
    grid = pltpu.PrefetchScalarGridSpec(
        num_scalar_prefetch=3,
        grid=(pairs, steps),
        in_specs=[column, column, column, whole(seg_col.shape), whole(seg_rep.shape), whole(seg_row.shape)],
        out_specs=[
            pl.BlockSpec((UNROLL * BLK, 2 * BLK), lambda p, s, *_: (s, p)),
            pl.BlockSpec((1, UNROLL, 2 * BLK, 8 * BLK), lambda p, s, *_: (p, s, 0, 0)),
            pl.BlockSpec((BLK, 2 * BLK), lambda p, s, *_: (0, p)),
            pl.BlockSpec((1, 2 * BLK, length), lambda p, s, *_: (p, 0, 0)),
            pl.BlockSpec((1, 2 * BLK, 2 * BLK), lambda p, s, *_: (p, 0, 0)),
        ],
        scratch_shapes=[pltpu.VMEM((2 * BLK, length), F32)],
    )
    work = pairs * (blocks * 8 + length // BLK) * 2 * BLK * BLK
    return pl.pallas_call(
        functools.partial(attend_kernel, heads=heads),
        grid_spec=grid,
        out_shape=[
            jax.ShapeDtypeStruct((blocks * BLK, width), LOW),
            jax.ShapeDtypeStruct((pairs, blocks, 2 * BLK, 8 * BLK), LOW),
            jax.ShapeDtypeStruct((BLK, width), LOW),
            jax.ShapeDtypeStruct((pairs, 2 * BLK, length), LOW),
            jax.ShapeDtypeStruct((pairs, 2 * BLK, 2 * BLK), F32),
        ],
        compiler_params=pltpu.CompilerParams(vmem_limit_bytes=48 << 20),
        cost_estimate=pl.CostEstimate(flops=work * 512 * 4, bytes_accessed=20 << 20, transcendentals=work),
        name="attend",
    )(index, active, flags, query, key, value, seg_col, seg_rep, seg_row)


def pull(index, active, flags, query, key, value, grad, grad_glob, probs, probs_glob, heads):
    length, width = key.shape
    blocks = grad.shape[0] // BLK
    pairs = width // (2 * BLK)
    steps = blocks // UNROLL
    column = pl.BlockSpec((length, 2 * BLK), lambda p, s, *_: (0, p))
    grid = pltpu.PrefetchScalarGridSpec(
        num_scalar_prefetch=3,
        grid=(pairs, steps),
        in_specs=[
            column,
            column,
            column,
            pl.BlockSpec((UNROLL * BLK, 2 * BLK), lambda p, s, *_: (s, p)),
            pl.BlockSpec((BLK, 2 * BLK), lambda p, s, *_: (0, p)),
            pl.BlockSpec((1, UNROLL, 2 * BLK, 8 * BLK), lambda p, s, *_: (p, s, 0, 0)),
            pl.BlockSpec((1, 2 * BLK, length), lambda p, s, *_: (p, 0, 0)),
        ],
        out_specs=[column, column, column],
        scratch_shapes=[
            pltpu.VMEM((length, 2 * BLK), F32),
            pltpu.VMEM((length, 2 * BLK), F32),
            pltpu.VMEM((2 * BLK, length), F32),
        ],
    )
    work = pairs * (blocks * 8 + length // BLK) * 2 * BLK * BLK
    return pl.pallas_call(
        functools.partial(pull_kernel, heads=heads),
        grid_spec=grid,
        out_shape=[jax.ShapeDtypeStruct((length, width), LOW)] * 3,
        compiler_params=pltpu.CompilerParams(vmem_limit_bytes=48 << 20),
        cost_estimate=pl.CostEstimate(flops=work * 512 * 8, bytes_accessed=24 << 20, transcendentals=0),
        name="pull",
    )(index, active, flags, query, key, value, grad, grad_glob, probs, probs_glob)


class Moves:
    def __init__(self, ctx, wshard):
        self.ctx, self.wshard, self.chips = ctx, wshard, ctx // 2
        self.order = list(range(0, wshard, 2)) + list(range(wshard - 1, 0, -2))
        places = [self.order.index(i) for i in range(wshard)]
        self.up_perm = [(self.order[i], self.order[(i + 1) % wshard]) for i in range(wshard)]
        self.down_perm = [(b, a) for a, b in self.up_perm]
        self.shard = lax.axis_index("wshard")
        self.place = jnp.asarray(places, jnp.int32)[self.shard]
        self.table = jnp.asarray(self.order, jnp.int32)
        here = lax.axis_index("ctx")
        self.core, self.chip = here % 2, here // 2

    def up(self, value):
        return lax.ppermute(value, "wshard", self.up_perm)

    def down(self, value):
        return lax.ppermute(value, "wshard", self.down_perm)

    def swap(self, value):
        return lax.ppermute(value, "ctx", [(c, c ^ 1) for c in range(self.ctx)])

    def chip_shift(self, value, j):
        return lax.ppermute(value, "ctx", [(c, (c + 2 * j) % self.ctx) for c in range(self.ctx)])

    def chip_flip(self, value, bit):
        return lax.ppermute(value, "ctx", [(c, c ^ (2 * bit)) for c in range(self.ctx)])

    def shard_at(self, delta):
        return self.table[(self.place + delta) % self.wshard]

    def gather(self, piece):
        rows = piece.shape[0]
        half = self.wshard // 2
        whole = jnp.zeros((self.wshard * rows,) + piece.shape[1:], piece.dtype)

        def put(whole, part, delta, offset=0):
            return lax.dynamic_update_slice_in_dim(whole, part, self.shard_at(delta) * rows + offset, 0)

        whole = put(whole, piece, 0)
        above = below = piece
        for step in range(1, half):
            above, below = self.up(above), self.down(below)
            whole = put(put(whole, above, -step), below, step)
        cut = (rows // 2) // 8 * 8
        above, below = self.up(above[:cut]), self.down(below[cut:])
        return put(put(whole, above, -half), below, half, cut)

    def scatter(self, parts):
        half = self.wshard // 2
        rows = parts.shape[1]
        cut = (rows // 2) // 8 * 8

        def own(delta, begin, end):
            part = lax.dynamic_index_in_dim(parts, self.shard_at(delta), 0, keepdims=False)
            return part[begin:end]

        above = self.up(own(half, 0, cut).astype(LOW))
        below = self.down(own(-half, cut, rows).astype(LOW))
        for step in range(half - 1, 0, -1):
            up_part, down_part = own(step, 0, rows), own(-step, 0, rows)
            if step == half - 1:
                up_part = jnp.concatenate([up_part[:cut] + above.astype(F32), up_part[cut:].astype(F32)], axis=0)
                down_part = jnp.concatenate([down_part[:cut].astype(F32), down_part[cut:] + below.astype(F32)], axis=0)
            else:
                up_part = up_part + above.astype(F32)
                down_part = down_part + below.astype(F32)
            above, below = self.up(up_part.astype(LOW)), self.down(down_part.astype(LOW))
        return own(0, 0, rows).astype(F32) + above.astype(F32) + below.astype(F32)

    def chip_sum(self, value):
        bit = 1
        while bit < self.chips:
            low = value.astype(LOW)
            value = low.astype(F32) + self.chip_flip(low, bit).astype(F32)
            bit *= 2
        return value.astype(LOW)

    def both(self, value, axis):
        other = self.swap(value)
        return jnp.where(
            self.core == 0,
            jnp.concatenate([value, other], axis=axis),
            jnp.concatenate([other, value], axis=axis),
        )

    def mine(self, value, axis, which=0):
        size = value.shape[axis] // 2
        core = self.core if which == 0 else 1 - self.core
        return lax.dynamic_slice_in_dim(value, core * size, size, axis)


def slot_lists(first, count, nblocks, glob, random_rows, heads):
    blocks = first + jnp.arange(count, dtype=jnp.int32)
    offsets = jnp.arange(-1, 2, dtype=jnp.int32)
    start = jnp.clip(blocks - 1, 0, nblocks - 3)
    window = start[:, None] + jnp.arange(3, dtype=jnp.int32)[None, :]
    near = jnp.abs(window - blocks[:, None]) <= 1
    slide = jnp.clip(blocks[:, None] + offsets[None, :], 0, nblocks - 1)
    spread = lambda a: jnp.broadcast_to(a[:, None, :], (count, heads, a.shape[-1]))
    rest = jnp.concatenate(
        [jnp.broadcast_to(glob[None, None, :], (count, heads, glob.shape[0])), random_rows], axis=2
    )
    lists = jnp.concatenate([spread(slide), rest], axis=2)
    slots = lists.shape[2]
    equal = lists[..., :, None] == lists[..., None, :]
    earlier = jnp.arange(slots)[:, None] < jnp.arange(slots)[None, :]
    fresh = jnp.logical_not(jnp.any(equal & earlier[None, None], axis=-2))
    on = jnp.concatenate([spread(near), fresh[..., 3:]], axis=2)
    index = jnp.concatenate([spread(window), rest], axis=2)
    return blocks, index, jnp.where(on, index, nblocks)


def per_device(ctx, wshard, layer_input, segments, global_blocks, random_blocks, thresholds, w_query, w_key, w_value, w_output, w_inner, w_outer, query_bias, value_bias, output_bias, inner_bias, outer_bias, gain_attn, shift_attn, gain_mlp, shift_mlp, out_grad):
    m = Moves(ctx, wshard)
    chips = m.chips
    tokens = layer_input[0]
    rows_here, width = tokens.shape
    seg_all = segments[0]
    length = seg_all.shape[0]
    glob = global_blocks[0]
    nglob = glob.shape[0]
    heads = thresholds.shape[0]
    head_dim = width // heads
    nblocks = length // BLK
    chip_rows = 2 * rows_here
    count = chip_rows // BLK
    first = m.chip * count
    half = width // 2
    own_heads = heads // 2
    hidden_width = w_inner.shape[1] * wshard
    cols = w_query.shape[1]

    inputs_low = tokens.astype(LOW)
    from_chips = [inputs_low] + [m.chip_shift(inputs_low, j) for j in range(1, chips)]
    mine = jnp.concatenate(from_chips, axis=0)
    theirs = m.swap(mine)
    inputs_all = jnp.zeros((length, width), LOW)
    for j in range(chips):
        source = (m.chip - j) % chips
        cut = slice(j * rows_here, (j + 1) * rows_here)
        inputs_all = lax.dynamic_update_slice_in_dim(
            inputs_all, mine[cut], (2 * source + m.core) * rows_here, 0
        )
        inputs_all = lax.dynamic_update_slice_in_dim(
            inputs_all, theirs[cut], (2 * source + 1 - m.core) * rows_here, 0
        )

    small = jnp.concatenate(
        [query_bias, value_bias, output_bias, outer_bias, gain_attn, shift_attn, gain_mlp, shift_mlp, inner_bias]
    ).astype(LOW)
    small_rows = -(-small.shape[0] // (8 * half)) * 8
    small_piece = jnp.pad(small, (0, small_rows * half - small.shape[0])).reshape(small_rows, half)
    projections = [m.mine(w.astype(LOW).T, 1) for w in (w_query, w_key, w_value)]
    first_rows = 3 * cols + small_rows
    got = m.gather(jnp.concatenate(projections + [small_piece], axis=0)).reshape(wshard, first_rows, half)
    small_all = got[:, 3 * cols :].reshape(wshard, small_rows * half)
    vectors = [small_all[:, i * cols : (i + 1) * cols].reshape(width).astype(F32) for i in range(8)]
    bias_query, bias_value, bias_output, bias_outer, attn_gain, attn_shift, mlp_gain, mlp_shift = vectors
    inner_cols = w_inner.shape[1]
    bias_inner = small_all[:, 8 * cols : 8 * cols + inner_cols].reshape(hidden_width).astype(F32)
    halves_all = jnp.stack([got[:, i * cols : (i + 1) * cols].reshape(width, half) for i in range(3)])
    received = m.swap(m.mine(halves_all, 1, 1))
    kept = m.mine(halves_all, 1)
    head_weights = jnp.where(
        m.core == 0,
        jnp.concatenate([kept, received], axis=2),
        jnp.concatenate([received, kept], axis=2),
    )
    wq, wk, wv = head_weights[0], head_weights[1], head_weights[2]

    full_output = m.both(m.gather(m.mine(w_output.astype(LOW).T, 1)), 1)
    full_inner = m.both(m.gather(m.mine(w_inner.astype(LOW).T, 1)), 1)
    full_outer = m.both(m.gather(m.mine(w_outer.astype(LOW).T, 1)), 1)

    query = ((dot_nt(inputs_all, wq) + m.mine(bias_query, 0)).astype(LOW) * 0.125).astype(LOW)
    key = dot_nt(inputs_all, wk).astype(LOW)
    value = (dot_nt(inputs_all, wv) + m.mine(bias_value, 0)).astype(LOW)

    random_own = lax.dynamic_slice(
        random_blocks, (first, m.core * own_heads, 0), (count, own_heads, random_blocks.shape[2])
    )
    blocks, index, active = slot_lists(first, count, nblocks, glob, random_own, own_heads)
    is_global = jnp.any(blocks[:, None] == glob[None, :], axis=1)
    distinct = jnp.array([True] + [False] * (nglob - 1))
    for n in range(1, nglob):
        distinct = distinct.at[n].set(jnp.all(glob[:n] != glob[n]))
    glob_ext = jnp.concatenate([glob, jnp.zeros((max(0, chips - nglob),), jnp.int32)])
    on_ext = jnp.concatenate([distinct, jnp.zeros((max(0, chips - nglob),), bool)])
    my_glob = glob_ext[m.chip]
    my_on = on_ext[m.chip]
    flags = jnp.concatenate(
        [jnp.stack([my_glob, my_on.astype(jnp.int32), first.astype(jnp.int32)]), is_global.astype(jnp.int32)]
    )
    seg_rep = seg_all.reshape(nblocks, BLK)
    seg_rep = jnp.concatenate([seg_rep, seg_rep], axis=1)
    seg_rep = jnp.concatenate([seg_rep, jnp.full((8, 2 * BLK), -1, jnp.int32)], axis=0)
    index, active = index.reshape(-1), active.reshape(-1)
    attended, probs, attended_glob, probs_glob, top = attend(
        index, active, flags, query, key, value, seg_all[:, None], seg_rep, seg_all[None, :], count, own_heads
    )
    pairs = own_heads // 2
    local_top = jnp.max(top.reshape(pairs, 2, BLK, 2 * BLK), axis=(2, 3)).reshape(own_heads)
    glob_rows = [attended_glob] + [m.chip_shift(attended_glob, j) for j in range(1, chips)]
    attended = attended.reshape(count, BLK, half)
    for j in range(chips):
        number = (m.chip - j) % chips
        here = (blocks == glob_ext[number]) & on_ext[number]
        attended = jnp.where(here[:, None, None], glob_rows[j][None], attended)
    attended = attended.reshape(chip_rows, half)
    attn_low = m.mine(attended, 0)
    attn_other = m.swap(m.mine(attended, 0, 1))
    attn_low = jnp.where(
        m.core == 0,
        jnp.concatenate([attn_low, attn_other], axis=1),
        jnp.concatenate([attn_other, attn_low], axis=1),
    )
    spot = jnp.arange(heads, dtype=jnp.int32) // own_heads == m.core
    maxima = jnp.where(spot, jnp.concatenate([local_top, local_top]), NEG)
    maxima = jnp.pad(maxima, (0, 128 - heads))[None]
    maxima = jnp.maximum(maxima, m.swap(maxima))
    bit = 1
    while bit < chips:
        maxima = jnp.maximum(maxima, m.chip_flip(maxima, bit))
        bit *= 2
    bit = 1
    while bit < wshard:
        flipped = lax.ppermute(maxima, "wshard", [(i, i ^ bit) for i in range(wshard)])
        maxima = jnp.maximum(maxima, flipped)
        bit *= 2
    maxima = maxima[0, :heads]

    mixed = dot_nt(attn_low, full_output) + bias_output
    hidden, normed_one, inverse_one = norm_forward(tokens + mixed, attn_gain, attn_shift)
    hidden_low = hidden.astype(LOW)
    inner = dot_nt(hidden_low, full_inner) + bias_inner
    activation, slope = gelu_and_slope(inner)
    activation_low = activation.astype(LOW)
    outer = dot_nt(activation_low, full_outer) + bias_outer
    layer_output, normed_two, inverse_two = norm_forward(hidden + outer, mlp_gain, mlp_shift)
    resid_two, mlp_gain_grad, mlp_shift_grad = norm_backward(out_grad[0], normed_two, inverse_two, mlp_gain)
    outer_grad = resid_two.astype(LOW)
    outer_bias_grad = jnp.sum(outer_grad.astype(F32), axis=0)
    inner_grad = (dot_nn(outer_grad, full_outer) * slope).astype(LOW)
    inner_bias_grad = jnp.sum(inner_grad.astype(F32), axis=0)
    hidden_grad = resid_two + dot_nn(inner_grad, full_inner)
    resid_one, attn_gain_grad, attn_shift_grad = norm_backward(hidden_grad, normed_one, inverse_one, attn_gain)
    mixed_grad = resid_one.astype(LOW)
    output_bias_grad = jnp.sum(mixed_grad.astype(F32), axis=0)

    def finish(left, right):
        keep = dot_tn(left, m.mine(right, 1))
        give = dot_tn(left, m.mine(right, 1, 1)).astype(LOW)
        total = (keep + m.swap(give).astype(F32)).astype(LOW)
        total = m.scatter(total.reshape(wshard, total.shape[0] // wshard, total.shape[1]))
        return m.both(m.chip_sum(total), 1).astype(F32).T

    grad_outer = finish(outer_grad, activation_low)
    grad_inner = finish(inner_grad, hidden_low)
    grad_output = finish(mixed_grad, attn_low)

    attn_grad = dot_nn(mixed_grad, full_output).astype(LOW)
    grad_other = m.swap(m.mine(attn_grad, 1, 1))
    grad_mine = m.mine(attn_grad, 1)
    heads_grad = jnp.where(
        m.core == 0,
        jnp.concatenate([grad_mine, grad_other], axis=0),
        jnp.concatenate([grad_other, grad_mine], axis=0),
    )
    blocks_grad = heads_grad.reshape(count, BLK, half)
    glob_grad = None
    for j in range(chips):
        number = (m.chip + j) % chips
        offset = glob_ext[number] - first
        owned = (offset >= 0) & (offset < count)
        rows = lax.dynamic_index_in_dim(blocks_grad, jnp.clip(offset, 0, count - 1), 0, keepdims=False)
        rows = jnp.where(owned, rows, jnp.zeros_like(rows))
        rows = rows if j == 0 else m.chip_shift(rows, j)
        glob_grad = rows if j == 0 else glob_grad + rows
    dquery, dkey, dvalue = pull(
        index, active, flags, query, key, value, heads_grad, glob_grad, probs, probs_glob, own_heads
    )
    weight_grads = jnp.stack([dot_tn(d, inputs_all).astype(LOW) for d in (dquery, dkey, dvalue)])
    give = m.swap(m.mine(weight_grads, 2, 1))
    keep = m.mine(weight_grads, 2)
    weight_grads = jnp.where(
        m.core == 0, jnp.concatenate([keep, give], axis=1), jnp.concatenate([give, keep], axis=1)
    )
    zeros = jnp.zeros((half,), F32)

    def spread(vector):
        return jnp.where(
            m.core == 0, jnp.concatenate([vector, zeros]), jnp.concatenate([zeros, vector])
        )

    vector_grads = [
        spread(jnp.sum(dquery.astype(F32), axis=0)),
        spread(jnp.sum(dvalue.astype(F32), axis=0)),
        output_bias_grad,
        outer_bias_grad,
        attn_gain_grad,
        attn_shift_grad,
        mlp_gain_grad,
        mlp_shift_grad,
        inner_bias_grad,
    ]
    packed = jnp.concatenate([v.reshape(wshard, -1) for v in vector_grads], axis=1)
    packed = jnp.pad(packed, ((0, 0), (0, small_rows * half - packed.shape[1])))
    packed = packed.reshape(wshard, small_rows, half).astype(LOW)
    pieces = [weight_grads[i].reshape(wshard, cols, half) for i in range(3)]
    tail = m.chip_sum(m.scatter(jnp.concatenate(pieces + [packed], axis=1)))
    weight_tail = m.both(tail[: 3 * cols], 1).astype(F32)
    grad_query, grad_key, grad_value = [weight_tail[i * cols : (i + 1) * cols].T for i in range(3)]
    vector_tail = tail[3 * cols :]
    vector_tail = (vector_tail.astype(F32) + m.swap(vector_tail).astype(F32)).reshape(-1)
    vector_out = [vector_tail[i * cols : (i + 1) * cols] for i in range(8)]
    inner_out = vector_tail[8 * cols : 8 * cols + inner_cols]

    partial = dot_nn(dquery, wq) + dot_nn(dkey, wk) + dot_nn(dvalue, wv)
    partial = partial.astype(LOW).reshape(chips, 2, rows_here, width)
    passed = m.swap(m.mine(partial, 1, 1))
    summed = m.mine(partial, 1).astype(F32) + passed.astype(F32)
    summed = summed.reshape(chips, rows_here, width)
    input_grad = resid_one + lax.dynamic_index_in_dim(summed, m.chip, 0, keepdims=False)
    summed_low = summed.astype(LOW)
    for j in range(1, chips):
        send = lax.dynamic_index_in_dim(summed_low, (m.chip + j) % chips, 0, keepdims=False)
        input_grad = input_grad + m.chip_shift(send, j).astype(F32)

    root = jnp.sqrt(thresholds / jnp.maximum(maxima, thresholds))
    column_ids = m.shard * cols + jnp.arange(cols, dtype=jnp.int32)
    onehot = column_ids[:, None] // head_dim == jnp.arange(heads, dtype=jnp.int32)[None, :]
    column_scale = jnp.sum(jnp.where(onehot, root[None, :], 0.0), axis=1)
    return (
        layer_output[None],
        input_grad[None],
        grad_query,
        grad_key,
        grad_value,
        grad_output,
        grad_inner,
        grad_outer,
        vector_out[0],
        vector_out[1],
        vector_out[2],
        inner_out,
        vector_out[3],
        vector_out[4],
        vector_out[5],
        vector_out[6],
        vector_out[7],
        w_query * column_scale[None, :],
        w_key * column_scale[None, :],
        maxima,
    )


def solution(mesh):
    tokens = P("wshard", "ctx", None)
    sequence = P("wshard", None)
    matrix = P(None, "wshard")
    vector = P("wshard")
    in_specs = (tokens, sequence, sequence, P(), P()) + (matrix,) * 6 + (vector,) * 9 + (tokens,)
    out_specs = (tokens, tokens) + (matrix,) * 6 + (vector,) * 9 + (matrix, matrix, P())
    return jax.shard_map(
        functools.partial(per_device, mesh.shape["ctx"], mesh.shape["wshard"]),
        mesh=mesh,
        in_specs=in_specs,
        out_specs=out_specs,
        check_vma=False,
    )
```

time: 1420 us -> 482 us (0.34)
  waiting for transfers between devices: 560 us -> 66.9 us
  other arithmetic: 316 us -> 48 us
  blocking collectives: 131 us -> 0 us
  local copies, waits for them, and re-layouts: 206 us -> 75.5 us
  starting transfers between devices: 1.28 us -> 107 us
  matrix products: 175 us -> 69.8 us
  Pallas kernels: 0 us -> 57.1 us
  between operations: 20 us -> 48.7 us
    reduce_scatter x7 -> x0, waiting for transfers between devices: 361 us -> none  [the longest x1 99.3 us: per_device(): lax.psum_scatter(outer_weight_grad.astype(jnp.bfloat16), 'wshard', scatte...]
    scatter-add x2 -> x0, other arithmetic: 244 us -> none  [the longest x1 122 us: per_device(): dkey_full = jnp.zeros((nblocks, BLK, heads, head_dim), jnp.float32).at[li...]
    all_gather x8 -> x0, waiting for transfers between devices: 168 us -> none  [the longest x1 72.2 us: per_device(): lax.all_gather(w_outer.astype(jnp.bfloat16), 'wshard', axis=1, tiled=True)]
    ppermute x0 -> x94, starting transfers between devices: none -> 107 us  [the longest x18 39.3 us: swap(): return lax.ppermute(value, 'ctx', [(c, c ^ 1) for c in range(self.ctx)])]
    dot_general x35 -> x21, matrix products: 160 us -> 69.8 us  [the longest x6 25.3 us: dot_nn(): lax.dot_general(left, right, (((1,), (0,)), ((), ())), preferred_element_...]
    reshape x10 -> x13, local copies, waits for them, and re-layouts: 81.2 us -> 1.49 us  [the longest x9 0.7 us: per_device(): v.reshape(wshard, -1)]
    ppermute x0 -> x94, waiting for transfers between devices: none -> 66.9 us  [the longest x32 37.3 us: up(): return lax.ppermute(value, 'wshard', self.up_perm)]
    unnamed x2 -> x0, blocking collectives: 61.7 us -> none
  transfers between devices with their start and end apart: 17 -> 94, of which waited for: 12 -> 27; matrix products, arithmetic and copies ran while one was open for 30% -> 31% of each run, Pallas kernels for 0% -> 12%
where the time goes in v1:
time: 482 us; the launch traced here: 473 us
  starting transfers between devices  107 us (22%)
  local copies, waits for them, and re-layouts  75.5 us (16%)
  matrix products  69.8 us (14%)
  waiting for transfers between devices  66.9 us (14%)
  Pallas kernels  57.1 us (12%)
  between operations  48.7 us (10%)
  other arithmetic  48 us (10%)
    ppermute x18, starting transfers between devices, swap(): return lax.ppermute(value, 'ctx', [(c, c ^ 1) for c in range(self.ctx)])  39.3 us
    ppermute x32, waiting for transfers between devices, up(): return lax.ppermute(value, 'wshard', self.up_perm)  37.3 us
    ppermute x32, starting transfers between devices, up(): return lax.ppermute(value, 'wshard', self.up_perm)  36.5 us
    dynamic_update_slice x35, local copies, waits for them, and re-layouts, put(): lax.dynamic_update_slice_in_dim(whole, part, self.shard_at(delta) * rows...  31 us
    pallas_call x1, Pallas kernels, pull(): pl.pallas_call(functools.partial(pull_kernel, heads=heads), grid_spec=gri...  30 us
    pallas_call x1, Pallas kernels, attend(): pl.pallas_call(functools.partial(attend_kernel, heads=heads), grid_spec=g...  27 us
    dot_general x6, matrix products, dot_nn(): lax.dot_general(left, right, (((1,), (0,)), ((), ())), preferred_element_...  25.3 us
    ppermute x32, waiting for transfers between devices, down(): return lax.ppermute(value, 'wshard', self.down_perm)  24.2 us
  transfers between devices with their start and end apart: 94, of which 27 were waited for; matrix products, arithmetic and copies ran while one was open for 31% of the time, Pallas kernels for 12%

profile of v1, /device:TPU:1, one launch (start us, length us, event | category | flops | bytes accessed | tf_op | source)
XLA Modules:
  0.0 472.5 jit_solution(779872151120964254)
XLA Ops:
  21.0 2.1 collective-permute-start.2
  27.0 1.7 broadcast_in_dim.167
  28.7 2.0 constant_dynamic-update-slice_fusion.15
  66.8 2.6 compare_and_fusion
  83.9 2.1 collective-permute-done.17
  93.7 5.6 %collective-permute-done.20 = bf16[48,384]{1,0:T(8,128)(2,1)S(1)} collective-permute-done((bf16[48,384]{1,0:T(8,128)(2,1)S(1)}, bf16[48,384]{1,0:T(8,128)(2,1)S(1)}, u32[]{:S(2)}, u32[]{:S(2)}) %collective-permute-start.20) | collective-permute-done | bytes 36896 | tf_op jit(solution)/shard_map/ppermute | solution.py:345
  103.7 1.8 constant_dynamic-update-slice_fusion.14
  110.4 1.7 constant_dynamic-update-slice_fusion.12
  112.3 1.7 constant_dynamic-update-slice_fusion.11
  117.9 2.3 collective-permute-done.6
  126.2 8.9 %collective-permute-done.8 = bf16[144,384]{1,0:T(8,128)(2,1)S(1)} collective-permute-done((bf16[144,384]{1,0:T(8,128)(2,1)S(1)}, bf16[144,384]{1,0:T(8,128)(2,1)S(1)}, u32[]{:S(2)}, u32[]{:S(2)}) %collective-permute-start.8) | collective-permute-done | bytes 110624 | tf_op jit(solution)/shard_map/ppermute | solution.py:342
  135.1 6.2 %collective-permute-start.1 = (bf16[1024,768]{1,0:T(8,128)(2,1)}, bf16[1024,768]{1,0:T(8,128)(2,1)}, u32[]{:S(2)}, u32[]{:S(2)}) collective-permute-start(bf16[1024,768]{1,0:T(8,128)(2,1)} %pad_maximum_fusion.3), channel_id=1, source_target_pairs={{0,8},{8,0},{16,24},{24,16},{1,9},{9,1},{17,25},{25,17},{2,10},{10... | collective-permute-start | bytes 4718600 | tf_op jit(solution)/shard_map/ppermute | solution.py:348
  152.3 1.9 maximum_select_fusion.2
  158.3 3.0 convolution_convert_fusion.2.k_ref
  161.3 1.8 fusion.8.q_ref
  163.1 3.0 add_convert_fusion.3.v_ref
  166.1 27.0 %attend.1 = (bf16[1024,384]{1,0:T(8,128)(2,1)S(1)}, bf16[3,16,128,512]{3,2,1,0:T(8,128)(2,1)}, bf16[64,384]{1,0:T(8,128)(2,1)S(1)}, bf16[3,128,2048]{2,1,0:T(8,128)(2,1)S(1)}, f32[3,128,128]{2,1,0:T(8,128)S(1)}) custom-call(s32[768]{0:T(1024)S(1)} %reshape.521.index, s32[768]{0:T(1024)S(1)} %broadcast_select_fusion.active, s32[19]{0:T(128)S(1)} %pad_add_fusion.4.flags, ...), custom_call_target="tpu_custom_call" | custom-call | flops 8053063680 | bytes 20971520 | tf_op jit(solution)/shard_map/attend/pallas_call | solution.py:276
  200.2 1.8 collective-permute-start.38
  202.0 3.3 dynamic_update_slice.149
  205.2 3.0 dynamic_update_slice.150
  208.3 2.0 collective-permute-start.30
  213.1 1.9 collective-permute-start.93
  218.1 2.8 fusion.99
  221.7 8.1 %multiply_convert_fusion = (bf16[512,3072]{1,0:T(8,128)(2,1)S(1)}, f32[512,3072]{1,0:T(8,128)}) fusion(f32[3072]{0:T(1024)S(1)} %reshape.545, bf16[512,768]{1,0:T(8,128)(2,1)S(1)} %fusion.17, bf16[3072,384]{0,1:T(8,128)(2,1)S(1)} %collective-permute-done.30, bf16[3072,384]{0,1:T(8,128)(2,1)} %dynamic_update_slice.150, pred[]{:T(512)S(6)} %eq.161), kind=kOutput, calls=%fused_computation.11 | convolution fusion | flops 2452881408 | bytes 14954497 | tf_op jit(solution)/shard_map/dot_general | solution.py:27
  229.8 2.9 fusion.100
  234.2 2.0 fusion.11
  236.7 10.5 %fusion.101 = (bf16[3072]{0:T(1024)(128)(2,1)S(1)}, bf16[512,3072]{1,0:T(8,128)(2,1)S(1)}) fusion(f32[512,3072]{1,0:T(8,128)} %get-tuple-element.165, f32[3072]{0:T(1024)S(1)} %reshape.545, bf16[512,768]{1,0:T(8,128)(2,1)S(1)} %get-tuple-element.58, bf16[768,1536]{1,0:T(8,128)(2,1)S(1)} %collective-permute-done.39, ...), kind=kOutput, calls=%fused_computation.347 | convolution fusion | flops 2470179840 | bytes 14960641 | tf_op jit(solution)/shard_map/dot_general | solution.py:19
  247.3 6.8 %multiply_reduce_fusion = (bf16[768]{0:T(1024)(128)(2,1)S(1)}, f32[512]{0:T(512)S(1)}, f32[512]{0:T(512)S(1)}, bf16[768]{0:T(1024)(128)(2,1)S(1)}, f32[512,768]{1,0:T(8,128)S(1)}) fusion(f32[512,768]{1,0:T(8,128)S(1)} %get-tuple-element.163, f32[512]{0:T(512)S(1)} %add_rsqrt_fusion.1, f32[512]{0:T(512)S(1)} %broadcast_multiply_fusion.7, ...), kind=kOutput, calls=%fused_computation.44 | convolution fusion | flops 2441082368 | bytes 12597249 | tf_op jit(solution)/shard_map/dot_general | solution.py:19
  254.1 1.7 fusion.90
  255.8 2.4 convolution_convert_fusion.3
  261.8 5.4 %convolution_convert_fusion = bf16[3072,384]{1,0:T(8,128)(2,1)} fusion(bf16[512,3072]{1,0:T(8,128)(2,1)} %copy-done.47, bf16[512,768]{1,0:T(8,128)(2,1)S(1)} %fusion.17, s32[]{:T(128)S(6)} %select_n.718), kind=kOutput, calls=%fused_computation.17 | convolution fusion | flops 1209139200 | bytes 5898244 | tf_op jit(solution)/shard_map/dot_general | solution.py:23
  270.4 2.8 convolution_convert_fusion.1
  273.5 30.0 %pull.1 = (bf16[2048,384]{1,0:T(8,128)(2,1)S(1)}, bf16[2048,384]{1,0:T(8,128)(2,1)S(1)}, bf16[2048,384]{1,0:T(8,128)(2,1)S(1)}) custom-call(s32[768]{0:T(1024)S(1)} %reshape.521.index, s32[768]{0:T(1024)S(1)} %broadcast_select_fusion.active, s32[19]{0:T(128)S(1)} %pad_add_fusion.4.flags, bf16[2048,384]{1,0:T(8,128)(2,1)} %copy-done.3, ...), custom_call_target="tpu_custom_call" | custom-call | flops 16106127360 | bytes 25165824 | tf_op jit(solution)/shard_map/pull/pallas_call | solution.py:318
  303.6 1.8 fusion.38
  312.2 1.8 fusion.39
  314.0 1.7 fusion.19
  317.9 2.0 add_convert_fusion
  321.6 1.7 collective-permute-done.57
  330.8 1.7 collective-permute-start.63
  332.7 4.7 %collective-permute-start.42 = (bf16[2,1,512,768]{3,2,1,0:T(8,128)(2,1)}, bf16[2,1,512,768]{3,2,1,0:T(8,128)(2,1)S(1)}, u32[]{:S(2)}, u32[]{:S(2)}) collective-permute-start(bf16[2,1,512,768]{3,2,1,0:T(8,128)(2,1)} %constant_dynamic-slice_fusion.13), channel_id=1, source_target_pairs={{0,8},{8,0},{16,24},{24,16},{1,9},{9,1},{17,25},{25,17},{2,10},{10... | collective-permute-start | bytes 4718600 | tf_op jit(solution)/shard_map/ppermute | solution.py:348
  338.9 2.6 maximum_select_fusion.3
  342.5 3.6 collective-permute-done.45
  347.6 2.1 collective-permute-done.49
  350.4 4.2 collective-permute-done.46
  356.3 3.5 collective-permute-done.50
  359.8 8.7 %collective-permute-start.65 = (bf16[96,384]{1,0:T(8,128)(2,1)S(1)}, bf16[96,384]{1,0:T(8,128)(2,1)S(1)}, u32[]{:S(2)}, u32[]{:S(2)}) collective-permute-start(bf16[96,384]{1,0:T(8,128)(2,1)S(1)} %add_convert_fusion.8), channel_id=1, source_target_pairs={{0,8},{8,0},{16,24},{24,16},{1,9},{9,1},{17,25},{25,17},{2,10},{10... | collective-permute-start | bytes 221192 | tf_op jit(solution)/shard_map/ppermute | solution.py:348
  372.1 1.7 collective-permute-done.51
  373.9 2.4 collective-permute-start.52
  380.2 2.0 collective-permute-done.52
  384.0 3.6 add_convert_fusion.2
  392.2 1.7 copy.103
  394.0 1.7 copy.102
  397.1 1.7 copy.100
  400.2 3.8 add_convert_fusion.1
  414.2 4.2 collective-permute-start.88
  423.5 1.9 collective-permute-start.54
  431.7 3.5 collective-permute-done.80
  439.1 2.4 collective-permute-done.69
  445.4 4.6 collective-permute-done.74
  450.8 4.8 %collective-permute-done.81 = bf16[96,1536]{1,0:T(8,128)(2,1)S(1)} collective-permute-done((bf16[96,1536]{1,0:T(8,128)(2,1)S(1)}, bf16[96,1536]{1,0:T(8,128)(2,1)S(1)}, u32[]{:S(2)}, u32[]{:S(2)}) %collective-permute-start.81) | collective-permute-done | bytes 294944 | tf_op jit(solution)/shard_map/ppermute | solution.py:342
  458.2 3.7 collective-permute-start.76
  461.8 3.2 collective-permute-done.86
  465.2 2.0 collective-permute-start.87
  467.2 2.6 fusion.10
  (496 shorter events, 169.1 us)
Async XLA Ops:
  21.0 67.5 %collective-permute-start.2 = (bf16[296,384]{1,0:T(8,128)(2,1)}, bf16[296,384]{1,0:T(8,128)(2,1)}, u32[]{:S(2)}, u32[]{:S(2)}) collective-permute-start(bf16[296,384]{1,0:T(8,128)(2,1)} %get-tuple-element.122), channel_id=1, source_target_pairs={{0,2},{2,4},{4,6},{6,7},{7,5},{5,3},{3,1},{1,0},{8,10},{10,12},{12... | collective-permute-start | bytes 681992 | tf_op jit(solution)/shard_map/ppermute | solution.py:342
  23.1 67.3 %collective-permute-start.3 = (bf16[296,384]{1,0:T(8,128)(2,1)}, bf16[296,384]{1,0:T(8,128)(2,1)}, u32[]{:S(2)}, u32[]{:S(2)}) collective-permute-start(bf16[296,384]{1,0:T(8,128)(2,1)} %get-tuple-element.122), channel_id=1, source_target_pairs={{2,0},{4,2},{6,4},{7,6},{5,7},{3,5},{1,3},{0,1},{10,8},{12,10},{14... | collective-permute-start | bytes 681992 | tf_op jit(solution)/shard_map/ppermute | solution.py:345
  24.8 54.2 %collective-permute-start.13 = (bf16[96,384]{1,0:T(8,128)(2,1)S(1)}, bf16[96,384]{1,0:T(8,128)(2,1)}, u32[]{:S(2)}, u32[]{:S(2)}) collective-permute-start(bf16[96,384]{1,0:T(8,128)(2,1)S(1)} %get-tuple-element.70), channel_id=1, source_target_pairs={{0,2},{2,4},{4,6},{6,7},{7,5},{5,3},{3,1},{1,0},{8,10},{10,12},{12... | collective-permute-start | bytes 221192 | tf_op jit(solution)/shard_map/ppermute | solution.py:342
  26.3 54.0 %collective-permute-start.14 = (bf16[96,384]{1,0:T(8,128)(2,1)S(1)}, bf16[96,384]{1,0:T(8,128)(2,1)S(1)}, u32[]{:S(2)}, u32[]{:S(2)}) collective-permute-start(bf16[96,384]{1,0:T(8,128)(2,1)S(1)} %get-tuple-element.70), channel_id=1, source_target_pairs={{2,0},{4,2},{6,4},{7,6},{5,7},{3,5},{1,3},{0,1},{10,8},{12,10},{14... | collective-permute-start | bytes 221192 | tf_op jit(solution)/shard_map/ppermute | solution.py:345
  30.6 71.3 %collective-permute-start.22 = (bf16[384,384]{0,1:T(8,128)(2,1)}, bf16[384,384]{0,1:T(8,128)(2,1)}, u32[]{:S(2)}, u32[]{:S(2)}) collective-permute-start(bf16[384,384]{0,1:T(8,128)(2,1)} %get-tuple-element.66), channel_id=1, source_target_pairs={{0,2},{2,4},{4,6},{6,7},{7,5},{5,3},{3,1},{1,0},{8,10},{10,12},{12... | collective-permute-start | bytes 884744 | tf_op jit(solution)/shard_map/ppermute | solution.py:342
  86.0 16.1 %collective-permute-start.23 = (bf16[384,384]{0,1:T(8,128)(2,1)}, bf16[384,384]{0,1:T(8,128)(2,1)S(1)}, u32[]{:S(2)}, u32[]{:S(2)}) collective-permute-start(bf16[384,384]{0,1:T(8,128)(2,1)} %get-tuple-element.66), channel_id=1, source_target_pairs={{2,0},{4,2},{6,4},{7,6},{5,7},{3,5},{1,3},{0,1},{10,8},{12,10},{14... | collective-permute-start | bytes 884744 | tf_op jit(solution)/shard_map/ppermute | solution.py:345
  87.1 13.4 %collective-permute-start.31 = (bf16[96,1536]{1,0:T(8,128)(2,1)S(1)}, bf16[96,1536]{1,0:T(8,128)(2,1)S(1)}, u32[]{:S(2)}, u32[]{:S(2)}) collective-permute-start(bf16[96,1536]{1,0:T(8,128)(2,1)S(1)} %get-tuple-element.64), channel_id=1, source_target_pairs={{0,2},{2,4},{4,6},{6,7},{7,5},{5,3},{3,1},{1,0},{8,10},{10,12},{12... | collective-permute-start | bytes 884744 | tf_op jit(solution)/shard_map/ppermute | solution.py:342
  88.5 15.0 %collective-permute-start.32 = (bf16[96,1536]{1,0:T(8,128)(2,1)S(1)}, bf16[96,1536]{1,0:T(8,128)(2,1)S(1)}, u32[]{:S(2)}, u32[]{:S(2)}) collective-permute-start(bf16[96,1536]{1,0:T(8,128)(2,1)S(1)} %get-tuple-element.64), channel_id=1, source_target_pairs={{2,0},{4,2},{6,4},{7,6},{5,7},{3,5},{1,3},{0,1},{10,8},{12,10},{14... | collective-permute-start | bytes 884744 | tf_op jit(solution)/shard_map/ppermute | solution.py:345
  99.3 24.7 %collective-permute-start = (bf16[512,768]{1,0:T(8,128)(2,1)S(1)}, bf16[512,768]{1,0:T(8,128)(2,1)S(1)}, u32[]{:S(2)}, u32[]{:S(2)}) collective-permute-start(bf16[512,768]{1,0:T(8,128)(2,1)S(1)} %get-tuple-element.68), channel_id=1, source_target_pairs={{0,16},{8,24},{16,0},{24,8},{1,17},{9,25},{17,1},{25,9},{2,18},{10... | collective-permute-start | bytes 2359304 | tf_op jit(solution)/shard_map/ppermute | solution.py:351
  101.9 6.3 %collective-permute-start.5 = (bf16[296,384]{1,0:T(8,128)(2,1)}, bf16[296,384]{1,0:T(8,128)(2,1)S(1)}, u32[]{:S(2)}, u32[]{:S(2)}) collective-permute-start(bf16[296,384]{1,0:T(8,128)(2,1)} %collective-permute-done.3), channel_id=1, source_target_pairs={{2,0},{4,2},{6,4},{7,6},{5,7},{3,5},{1,3},{0,1},{10,8},{12,10},{14... | collective-permute-start | bytes 681992 | tf_op jit(solution)/shard_map/ppermute | solution.py:345
  102.2 7.0 %collective-permute-start.24 = (bf16[384,384]{0,1:T(8,128)(2,1)}, bf16[384,384]{0,1:T(8,128)(2,1)}, u32[]{:S(2)}, u32[]{:S(2)}) collective-permute-start(bf16[384,384]{0,1:T(8,128)(2,1)} %collective-permute-done.22), channel_id=1, source_target_pairs={{0,2},{2,4},{4,6},{6,7},{7,5},{5,3},{3,1},{1,0},{8,10},{10,12},{12... | collective-permute-start | bytes 884744 | tf_op jit(solution)/shard_map/ppermute | solution.py:342
  103.5 8.7 %collective-permute-start.25 = (bf16[384,384]{0,1:T(8,128)(2,1)S(1)}, bf16[384,384]{0,1:T(8,128)(2,1)}, u32[]{:S(2)}, u32[]{:S(2)}) collective-permute-start(bf16[384,384]{0,1:T(8,128)(2,1)S(1)} %collective-permute-done.23), channel_id=1, source_target_pairs={{2,0},{4,2},{6,4},{7,6},{5,7},{3,5},{1,3},{0,1},{10,8},{12,10},{14... | collective-permute-start | bytes 884744 | tf_op jit(solution)/shard_map/ppermute | solution.py:345
  106.3 9.1 %collective-permute-start.33 = (bf16[96,1536]{1,0:T(8,128)(2,1)S(1)}, bf16[96,1536]{1,0:T(8,128)(2,1)}, u32[]{:S(2)}, u32[]{:S(2)}) collective-permute-start(bf16[96,1536]{1,0:T(8,128)(2,1)S(1)} %collective-permute-done.31), channel_id=1, source_target_pairs={{0,2},{2,4},{4,6},{6,7},{7,5},{5,3},{3,1},{1,0},{8,10},{10,12},{12... | collective-permute-start | bytes 884744 | tf_op jit(solution)/shard_map/ppermute | solution.py:342
  108.2 9.2 %collective-permute-start.34 = (bf16[96,1536]{1,0:T(8,128)(2,1)S(1)}, bf16[96,1536]{1,0:T(8,128)(2,1)S(1)}, u32[]{:S(2)}, u32[]{:S(2)}) collective-permute-start(bf16[96,1536]{1,0:T(8,128)(2,1)S(1)} %collective-permute-done.32), channel_id=1, source_target_pairs={{2,0},{4,2},{6,4},{7,6},{5,7},{3,5},{1,3},{0,1},{10,8},{12,10},{14... | collective-permute-start | bytes 884744 | tf_op jit(solution)/shard_map/ppermute | solution.py:345
  109.1 11.1 %collective-permute-start.6 = (bf16[296,384]{1,0:T(8,128)(2,1)S(1)}, bf16[296,384]{1,0:T(8,128)(2,1)S(1)}, u32[]{:S(2)}, u32[]{:S(2)}) collective-permute-start(bf16[296,384]{1,0:T(8,128)(2,1)S(1)} %collective-permute-done.4), channel_id=1, source_target_pairs={{0,2},{2,4},{4,6},{6,7},{7,5},{5,3},{3,1},{1,0},{8,10},{10,12},{12... | collective-permute-start | bytes 681992 | tf_op jit(solution)/shard_map/ppermute | solution.py:342
  112.2 9.8 %collective-permute-start.7 = (bf16[296,384]{1,0:T(8,128)(2,1)S(1)}, bf16[296,384]{1,0:T(8,128)(2,1)S(1)}, u32[]{:S(2)}, u32[]{:S(2)}) collective-permute-start(bf16[296,384]{1,0:T(8,128)(2,1)S(1)} %collective-permute-done.5), channel_id=1, source_target_pairs={{2,0},{4,2},{6,4},{7,6},{5,7},{3,5},{1,3},{0,1},{10,8},{12,10},{14... | collective-permute-start | bytes 681992 | tf_op jit(solution)/shard_map/ppermute | solution.py:345
  115.3 31.9 %collective-permute-start.26 = (bf16[384,384]{0,1:T(8,128)(2,1)}, bf16[384,384]{0,1:T(8,128)(2,1)S(1)}, u32[]{:S(2)}, u32[]{:S(2)}) collective-permute-start(bf16[384,384]{0,1:T(8,128)(2,1)} %collective-permute-done.24), channel_id=1, source_target_pairs={{0,2},{2,4},{4,6},{6,7},{7,5},{5,3},{3,1},{1,0},{8,10},{10,12},{12... | collective-permute-start | bytes 884744 | tf_op jit(solution)/shard_map/ppermute | solution.py:342
  117.4 31.1 %collective-permute-start.27 = (bf16[384,384]{0,1:T(8,128)(2,1)}, bf16[384,384]{0,1:T(8,128)(2,1)S(1)}, u32[]{:S(2)}, u32[]{:S(2)}) collective-permute-start(bf16[384,384]{0,1:T(8,128)(2,1)} %collective-permute-done.25), channel_id=1, source_target_pairs={{2,0},{4,2},{6,4},{7,6},{5,7},{3,5},{1,3},{0,1},{10,8},{12,10},{14... | collective-permute-start | bytes 884744 | tf_op jit(solution)/shard_map/ppermute | solution.py:345
  120.2 29.2 %collective-permute-start.35 = (bf16[96,1536]{1,0:T(8,128)(2,1)}, bf16[96,1536]{1,0:T(8,128)(2,1)S(1)}, u32[]{:S(2)}, u32[]{:S(2)}) collective-permute-start(bf16[96,1536]{1,0:T(8,128)(2,1)} %collective-permute-done.33), channel_id=1, source_target_pairs={{0,2},{2,4},{4,6},{6,7},{7,5},{5,3},{3,1},{1,0},{8,10},{10,12},{12... | collective-permute-start | bytes 884744 | tf_op jit(solution)/shard_map/ppermute | solution.py:342
  122.0 13.1 %collective-permute-start.8 = (bf16[144,384]{1,0:T(8,128)(2,1)S(1)}, bf16[144,384]{1,0:T(8,128)(2,1)S(1)}, u32[]{:S(2)}, u32[]{:S(2)}) collective-permute-start(bf16[144,384]{1,0:T(8,128)(2,1)S(1)} %slice.351), channel_id=1, source_target_pairs={{0,2},{2,4},{4,6},{6,7},{7,5},{5,3},{3,1},{1,0},{8,10},{10,12},{12... | collective-permute-start | bytes 331784 | tf_op jit(solution)/shard_map/ppermute | solution.py:342
  124.0 18.0 %collective-permute-start.9 = (bf16[152,384]{1,0:T(8,128)(2,1)S(1)}, bf16[152,384]{1,0:T(8,128)(2,1)S(1)}, u32[]{:S(2)}, u32[]{:S(2)}) collective-permute-start(bf16[152,384]{1,0:T(8,128)(2,1)S(1)} %slice.352), channel_id=1, source_target_pairs={{2,0},{4,2},{6,4},{7,6},{5,7},{3,5},{1,3},{0,1},{10,8},{12,10},{14... | collective-permute-start | bytes 350216 | tf_op jit(solution)/shard_map/ppermute | solution.py:345
  135.1 19.2 %collective-permute-start.1 = (bf16[1024,768]{1,0:T(8,128)(2,1)}, bf16[1024,768]{1,0:T(8,128)(2,1)}, u32[]{:S(2)}, u32[]{:S(2)}) collective-permute-start(bf16[1024,768]{1,0:T(8,128)(2,1)} %pad_maximum_fusion.3), channel_id=1, source_target_pairs={{0,8},{8,0},{16,24},{24,16},{1,9},{9,1},{17,25},{25,17},{2,10},{10... | collective-permute-start | bytes 4718600 | tf_op jit(solution)/shard_map/ppermute | solution.py:348
  145.6 6.6 %collective-permute-start.10 = (bf16[3,384,384]{2,1,0:T(8,128)(2,1)}, bf16[3,384,384]{2,1,0:T(8,128)(2,1)}, u32[]{:S(2)}, u32[]{:S(2)}) collective-permute-start(bf16[3,384,384]{2,1,0:T(8,128)(2,1)} %get-tuple-element.105), channel_id=1, source_target_pairs={{0,8},{8,0},{16,24},{24,16},{1,9},{9,1},{17,25},{25,17},{2,10},{10... | collective-permute-start | bytes 2654216 | tf_op jit(solution)/shard_map/ppermute | solution.py:348
  147.3 70.2 %collective-permute-start.21 = (bf16[768,384]{1,0:T(8,128)(2,1)}, bf16[768,384]{1,0:T(8,128)(2,1)}, u32[]{:S(2)}, u32[]{:S(2)}) collective-permute-start(bf16[768,384]{1,0:T(8,128)(2,1)} %copy-done.36), channel_id=1, source_target_pairs={{0,8},{8,0},{16,24},{24,16},{1,9},{9,1},{17,25},{25,17},{2,10},{10... | collective-permute-start | bytes 1769480 | tf_op jit(solution)/shard_map/ppermute | solution.py:348
  148.5 46.4 %collective-permute-start.36 = (bf16[96,1536]{1,0:T(8,128)(2,1)}, bf16[96,1536]{1,0:T(8,128)(2,1)S(1)}, u32[]{:S(2)}, u32[]{:S(2)}) collective-permute-start(bf16[96,1536]{1,0:T(8,128)(2,1)} %copy-done.40), channel_id=1, source_target_pairs={{2,0},{4,2},{6,4},{7,6},{5,7},{3,5},{1,3},{0,1},{10,8},{12,10},{14... | collective-permute-start | bytes 884744 | tf_op jit(solution)/shard_map/ppermute | solution.py:345
  149.4 50.8 %collective-permute-start.28 = (bf16[192,384]{0,1:T(8,128)(2,1)}, bf16[192,384]{0,1:T(8,128)(2,1)}, u32[]{:S(2)}, u32[]{:S(2)}) collective-permute-start(bf16[192,384]{0,1:T(8,128)(2,1)} %slice.367), channel_id=1, source_target_pairs={{0,2},{2,4},{4,6},{6,7},{7,5},{5,3},{3,1},{1,0},{8,10},{10,12},{12... | collective-permute-start | bytes 442376 | tf_op jit(solution)/shard_map/ppermute | solution.py:342
  152.2 53.1 %collective-permute-start.29 = (bf16[192,384]{0,1:T(8,128)(2,1)}, bf16[192,384]{0,1:T(8,128)(2,1)S(1)}, u32[]{:S(2)}, u32[]{:S(2)}) collective-permute-start(bf16[192,384]{0,1:T(8,128)(2,1)} %slice.368), channel_id=1, source_target_pairs={{2,0},{4,2},{6,4},{7,6},{5,7},{3,5},{1,3},{0,1},{10,8},{12,10},{14... | collective-permute-start | bytes 442376 | tf_op jit(solution)/shard_map/ppermute | solution.py:345
  154.3 56.3 %collective-permute-start.37 = (bf16[48,1536]{1,0:T(8,128)(2,1)}, bf16[48,1536]{1,0:T(8,128)(2,1)}, u32[]{:S(2)}, u32[]{:S(2)}) collective-permute-start(bf16[48,1536]{1,0:T(8,128)(2,1)} %slice.370), channel_id=1, source_target_pairs={{0,2},{2,4},{4,6},{6,7},{7,5},{5,3},{3,1},{1,0},{8,10},{10,12},{12... | collective-permute-start | bytes 442376 | tf_op jit(solution)/shard_map/ppermute | solution.py:342
  199.2 11.1 %collective-permute-start.91 = (f32[1,128]{1,0:T(1,128)S(1)}, f32[1,128]{1,0:T(1,128)S(1)}, u32[]{:S(2)}, u32[]{:S(2)}) collective-permute-start(f32[1,128]{1,0:T(1,128)S(1)} %max.42), channel_id=1, source_target_pairs={{0,1},{1,0},{2,3},{3,2},{4,5},{5,4},{6,7},{7,6},{8,9},{9,8},{10,11... | collective-permute-start | bytes 1544 | tf_op jit(solution)/shard_map/ppermute | solution.py:555
  200.2 16.6 %collective-permute-start.38 = (bf16[48,1536]{1,0:T(8,128)(2,1)S(1)}, bf16[48,1536]{1,0:T(8,128)(2,1)S(1)}, u32[]{:S(2)}, u32[]{:S(2)}) collective-permute-start(bf16[48,1536]{1,0:T(8,128)(2,1)S(1)} %slice.371), channel_id=1, source_target_pairs={{2,0},{4,2},{6,4},{7,6},{5,7},{3,5},{1,3},{0,1},{10,8},{12,10},{14... | collective-permute-start | bytes 442376 | tf_op jit(solution)/shard_map/ppermute | solution.py:345
  208.3 13.5 %collective-permute-start.30 = (bf16[3072,384]{0,1:T(8,128)(2,1)}, bf16[3072,384]{0,1:T(8,128)(2,1)S(1)}, u32[]{:S(2)}, u32[]{:S(2)}) collective-permute-start(bf16[3072,384]{0,1:T(8,128)(2,1)} %dynamic_update_slice.150), channel_id=1, source_target_pairs={{0,8},{8,0},{16,24},{24,16},{1,9},{9,1},{17,25},{25,17},{2,10},{10... | collective-permute-start | bytes 7077896 | tf_op jit(solution)/shard_map/ppermute | solution.py:348
  216.8 13.1 %collective-permute-start.39 = (bf16[768,1536]{1,0:T(8,128)(2,1)S(1)}, bf16[768,1536]{1,0:T(8,128)(2,1)S(1)}, u32[]{:S(2)}, u32[]{:S(2)}) collective-permute-start(bf16[768,1536]{1,0:T(8,128)(2,1)S(1)} %constant_dynamic-update-slice_fusion), channel_id=1, source_target_pairs={{0,8},{8,0},{16,24},{24,16},{1,9},{9,1},{17,25},{25,17},{2,10},{10... | collective-permute-start | bytes 7077896 | tf_op jit(solution)/shard_map/ppermute | solution.py:348
  258.3 9.4 %collective-permute-start.40 = (bf16[512,384]{1,0:T(8,128)(2,1)S(1)}, bf16[512,384]{1,0:T(8,128)(2,1)}, u32[]{:S(2)}, u32[]{:S(2)}) collective-permute-start(bf16[512,384]{1,0:T(8,128)(2,1)S(1)} %get-tuple-element.111), channel_id=1, source_target_pairs={{0,8},{8,0},{16,24},{24,16},{1,9},{9,1},{17,25},{25,17},{2,10},{10... | collective-permute-start | bytes 1179656 | tf_op jit(solution)/shard_map/ppermute | solution.py:348
  261.7 52.3 %collective-permute-start.55 = (bf16[768,384]{1,0:T(8,128)(2,1)}, bf16[768,384]{1,0:T(8,128)(2,1)}, u32[]{:S(2)}, u32[]{:S(2)}) collective-permute-start(bf16[768,384]{1,0:T(8,128)(2,1)} %convolution_convert_fusion.7), channel_id=1, source_target_pairs={{0,8},{8,0},{16,24},{24,16},{1,9},{9,1},{17,25},{25,17},{2,10},{10... | collective-permute-start | bytes 1769480 | tf_op jit(solution)/shard_map/ppermute | solution.py:348
  267.1 116.8 %collective-permute-start.66 = (bf16[3072,384]{1,0:T(8,128)(2,1)}, bf16[3072,384]{1,0:T(8,128)(2,1)}, u32[]{:S(2)}, u32[]{:S(2)}) collective-permute-start(bf16[3072,384]{1,0:T(8,128)(2,1)} %convolution_convert_fusion), channel_id=1, source_target_pairs={{0,8},{8,0},{16,24},{24,16},{1,9},{9,1},{17,25},{25,17},{2,10},{10... | collective-permute-start | bytes 7077896 | tf_op jit(solution)/shard_map/ppermute | solution.py:348
  273.2 127.0 %collective-permute-start.77 = (bf16[768,1536]{1,0:T(8,128)(2,1)}, bf16[768,1536]{1,0:T(8,128)(2,1)}, u32[]{:S(2)}, u32[]{:S(2)}) collective-permute-start(bf16[768,1536]{1,0:T(8,128)(2,1)} %convolution_convert_fusion.1), channel_id=1, source_target_pairs={{0,8},{8,0},{16,24},{24,16},{1,9},{9,1},{17,25},{25,17},{2,10},{10... | collective-permute-start | bytes 7077896 | tf_op jit(solution)/shard_map/ppermute | solution.py:348
  311.7 27.2 %collective-permute-start.44 = (bf16[3,384,384]{2,1,0:T(8,128)(2,1)}, bf16[3,384,384]{2,1,0:T(8,128)(2,1)}, u32[]{:S(2)}, u32[]{:S(2)}) collective-permute-start(bf16[3,384,384]{2,1,0:T(8,128)(2,1)} %get-tuple-element.103), channel_id=1, source_target_pairs={{0,8},{8,0},{16,24},{24,16},{1,9},{9,1},{17,25},{25,17},{2,10},{10... | collective-permute-start | bytes 2654216 | tf_op jit(solution)/shard_map/ppermute | solution.py:348
  330.8 6.7 %collective-permute-start.63 = (bf16[96,384]{1,0:T(8,128)(2,1)S(1)}, bf16[96,384]{1,0:T(8,128)(2,1)}, u32[]{:S(2)}, u32[]{:S(2)}) collective-permute-start(bf16[96,384]{1,0:T(8,128)(2,1)S(1)} %fusion.64), channel_id=1, source_target_pairs={{2,0},{4,2},{6,4},{7,6},{5,7},{3,5},{1,3},{0,1},{10,8},{12,10},{14... | collective-permute-start | bytes 221192 | tf_op jit(solution)/shard_map/ppermute | solution.py:345
  332.7 43.6 %collective-permute-start.42 = (bf16[2,1,512,768]{3,2,1,0:T(8,128)(2,1)}, bf16[2,1,512,768]{3,2,1,0:T(8,128)(2,1)S(1)}, u32[]{:S(2)}, u32[]{:S(2)}) collective-permute-start(bf16[2,1,512,768]{3,2,1,0:T(8,128)(2,1)} %constant_dynamic-slice_fusion.13), channel_id=1, source_target_pairs={{0,8},{8,0},{16,24},{24,16},{1,9},{9,1},{17,25},{25,17},{2,10},{10... | collective-permute-start | bytes 4718600 | tf_op jit(solution)/shard_map/ppermute | solution.py:348
  338.4 17.8 %collective-permute-start.64 = (bf16[96,384]{1,0:T(8,128)(2,1)S(1)}, bf16[96,384]{1,0:T(8,128)(2,1)S(1)}, u32[]{:S(2)}, u32[]{:S(2)}) collective-permute-start(bf16[96,384]{1,0:T(8,128)(2,1)S(1)} %fusion.68), channel_id=1, source_target_pairs={{0,16},{8,24},{16,0},{24,8},{1,17},{9,25},{17,1},{25,9},{2,18},{10... | collective-permute-start | bytes 221192 | tf_op jit(solution)/shard_map/ppermute | solution.py:354
  356.2 12.3 %collective-permute-start.47 = (bf16[296,384]{1,0:T(8,128)(2,1)S(1)}, bf16[296,384]{1,0:T(8,128)(2,1)S(1)}, u32[]{:S(2)}, u32[]{:S(2)}) collective-permute-start(bf16[296,384]{1,0:T(8,128)(2,1)S(1)} %fusion.43), channel_id=1, source_target_pairs={{0,2},{2,4},{4,6},{6,7},{7,5},{5,3},{3,1},{1,0},{8,10},{10,12},{12... | collective-permute-start | bytes 681992 | tf_op jit(solution)/shard_map/ppermute | solution.py:342
  359.8 11.2 %collective-permute-start.65 = (bf16[96,384]{1,0:T(8,128)(2,1)S(1)}, bf16[96,384]{1,0:T(8,128)(2,1)S(1)}, u32[]{:S(2)}, u32[]{:S(2)}) collective-permute-start(bf16[96,384]{1,0:T(8,128)(2,1)S(1)} %add_convert_fusion.8), channel_id=1, source_target_pairs={{0,8},{8,0},{16,24},{24,16},{1,9},{9,1},{17,25},{25,17},{2,10},{10... | collective-permute-start | bytes 221192 | tf_op jit(solution)/shard_map/ppermute | solution.py:348
  371.7 8.4 %collective-permute-start.48 = (bf16[296,384]{1,0:T(8,128)(2,1)S(1)}, bf16[296,384]{1,0:T(8,128)(2,1)S(1)}, u32[]{:S(2)}, u32[]{:S(2)}) collective-permute-start(bf16[296,384]{1,0:T(8,128)(2,1)S(1)} %get-tuple-element.90), channel_id=1, source_target_pairs={{0,2},{2,4},{4,6},{6,7},{7,5},{5,3},{3,1},{1,0},{8,10},{10,12},{12... | collective-permute-start | bytes 681992 | tf_op jit(solution)/shard_map/ppermute | solution.py:342
  373.9 8.3 %collective-permute-start.52 = (bf16[296,384]{1,0:T(8,128)(2,1)S(1)}, bf16[296,384]{1,0:T(8,128)(2,1)S(1)}, u32[]{:S(2)}, u32[]{:S(2)}) collective-permute-start(bf16[296,384]{1,0:T(8,128)(2,1)S(1)} %fusion.42), channel_id=1, source_target_pairs={{2,0},{4,2},{6,4},{7,6},{5,7},{3,5},{1,3},{0,1},{10,8},{12,10},{14... | collective-permute-start | bytes 681992 | tf_op jit(solution)/shard_map/ppermute | solution.py:345
  379.3 87.8 %collective-permute-start.43 = (bf16[512,768]{1,0:T(8,128)(2,1)}, bf16[512,768]{1,0:T(8,128)(2,1)}, u32[]{:S(2)}, u32[]{:S(2)}) collective-permute-start(bf16[512,768]{1,0:T(8,128)(2,1)} %fusion.24), channel_id=1, source_target_pairs={{0,16},{8,24},{16,0},{24,8},{1,17},{9,25},{17,1},{25,9},{2,18},{10... | collective-permute-start | bytes 2359304 | tf_op jit(solution)/shard_map/ppermute | solution.py:351
  382.9 30.2 %collective-permute-start.53 = (bf16[296,384]{1,0:T(8,128)(2,1)}, bf16[296,384]{1,0:T(8,128)(2,1)}, u32[]{:S(2)}, u32[]{:S(2)}) collective-permute-start(bf16[296,384]{1,0:T(8,128)(2,1)} %fusion.46), channel_id=1, source_target_pairs={{0,16},{8,24},{16,0},{24,8},{1,17},{9,25},{17,1},{25,9},{2,18},{10... | collective-permute-start | bytes 681992 | tf_op jit(solution)/shard_map/ppermute | solution.py:354
  389.2 16.5 %collective-permute-start.71 = (bf16[192,384]{0,1:T(8,128)(2,1)}, bf16[192,384]{0,1:T(8,128)(2,1)}, u32[]{:S(2)}, u32[]{:S(2)}) collective-permute-start(bf16[192,384]{0,1:T(8,128)(2,1)} %bitcast.89), channel_id=1, source_target_pairs={{2,0},{4,2},{6,4},{7,6},{5,7},{3,5},{1,3},{0,1},{10,8},{12,10},{14... | collective-permute-start | bytes 442376 | tf_op jit(solution)/shard_map/ppermute | solution.py:345
  395.7 11.8 %collective-permute-start.67 = (bf16[192,384]{0,1:T(8,128)(2,1)}, bf16[192,384]{0,1:T(8,128)(2,1)}, u32[]{:S(2)}, u32[]{:S(2)}) collective-permute-start(bf16[192,384]{0,1:T(8,128)(2,1)} %bitcast.83), channel_id=1, source_target_pairs={{0,2},{2,4},{4,6},{6,7},{7,5},{5,3},{3,1},{1,0},{8,10},{10,12},{12... | collective-permute-start | bytes 442376 | tf_op jit(solution)/shard_map/ppermute | solution.py:342
  407.5 18.9 %collective-permute-start.72 = (bf16[384,384]{0,1:T(8,128)(2,1)}, bf16[384,384]{0,1:T(8,128)(2,1)}, u32[]{:S(2)}, u32[]{:S(2)}) collective-permute-start(bf16[384,384]{0,1:T(8,128)(2,1)} %pad_maximum_fusion.5), channel_id=1, source_target_pairs={{2,0},{4,2},{6,4},{7,6},{5,7},{3,5},{1,3},{0,1},{10,8},{12,10},{14... | collective-permute-start | bytes 884744 | tf_op jit(solution)/shard_map/ppermute | solution.py:345
  409.4 19.7 %collective-permute-start.68 = (bf16[384,384]{0,1:T(8,128)(2,1)}, bf16[384,384]{0,1:T(8,128)(2,1)}, u32[]{:S(2)}, u32[]{:S(2)}) collective-permute-start(bf16[384,384]{0,1:T(8,128)(2,1)} %pad_maximum_fusion.4), channel_id=1, source_target_pairs={{0,2},{2,4},{4,6},{6,7},{7,5},{5,3},{3,1},{1,0},{8,10},{10,12},{12... | collective-permute-start | bytes 884744 | tf_op jit(solution)/shard_map/ppermute | solution.py:342
  411.6 11.8 %collective-permute-start.79 = (bf16[96,1536]{1,0:T(8,128)(2,1)}, bf16[96,1536]{1,0:T(8,128)(2,1)}, u32[]{:S(2)}, u32[]{:S(2)}) collective-permute-start(bf16[96,1536]{1,0:T(8,128)(2,1)} %pad_maximum_fusion.6), channel_id=1, source_target_pairs={{0,2},{2,4},{4,6},{6,7},{7,5},{5,3},{3,1},{1,0},{8,10},{10,12},{12... | collective-permute-start | bytes 884744 | tf_op jit(solution)/shard_map/ppermute | solution.py:342
  419.9 10.2 %collective-permute-start.83 = (bf16[96,1536]{1,0:T(8,128)(2,1)}, bf16[96,1536]{1,0:T(8,128)(2,1)}, u32[]{:S(2)}, u32[]{:S(2)}) collective-permute-start(bf16[96,1536]{1,0:T(8,128)(2,1)} %pad_maximum_fusion.7), channel_id=1, source_target_pairs={{2,0},{4,2},{6,4},{7,6},{5,7},{3,5},{1,3},{0,1},{10,8},{12,10},{14... | collective-permute-start | bytes 884744 | tf_op jit(solution)/shard_map/ppermute | solution.py:345
  423.5 21.7 %collective-permute-start.54 = (bf16[288,384]{1,0:T(8,128)(2,1)}, bf16[288,384]{1,0:T(8,128)(2,1)S(1)}, u32[]{:S(2)}, u32[]{:S(2)}) collective-permute-start(bf16[288,384]{1,0:T(8,128)(2,1)} %slice.378), channel_id=1, source_target_pairs={{0,8},{8,0},{16,24},{24,16},{1,9},{9,1},{17,25},{25,17},{2,10},{10... | collective-permute-start | bytes 663560 | tf_op jit(solution)/shard_map/ppermute | solution.py:348
  426.5 8.7 %collective-permute-start.80 = (bf16[96,1536]{1,0:T(8,128)(2,1)S(1)}, bf16[96,1536]{1,0:T(8,128)(2,1)S(1)}, u32[]{:S(2)}, u32[]{:S(2)}) collective-permute-start(bf16[96,1536]{1,0:T(8,128)(2,1)S(1)} %fusion.28), channel_id=1, source_target_pairs={{0,2},{2,4},{4,6},{6,7},{7,5},{5,3},{3,1},{1,0},{8,10},{10,12},{12... | collective-permute-start | bytes 884744 | tf_op jit(solution)/shard_map/ppermute | solution.py:342
  429.0 8.5 %collective-permute-start.73 = (bf16[384,384]{0,1:T(8,128)(2,1)S(1)}, bf16[384,384]{0,1:T(8,128)(2,1)S(1)}, u32[]{:S(2)}, u32[]{:S(2)}) collective-permute-start(bf16[384,384]{0,1:T(8,128)(2,1)S(1)} %fusion.32), channel_id=1, source_target_pairs={{2,0},{4,2},{6,4},{7,6},{5,7},{3,5},{1,3},{0,1},{10,8},{12,10},{14... | collective-permute-start | bytes 884744 | tf_op jit(solution)/shard_map/ppermute | solution.py:345
  430.2 11.3 %collective-permute-start.69 = (bf16[384,384]{0,1:T(8,128)(2,1)S(1)}, bf16[384,384]{0,1:T(8,128)(2,1)S(1)}, u32[]{:S(2)}, u32[]{:S(2)}) collective-permute-start(bf16[384,384]{0,1:T(8,128)(2,1)S(1)} %fusion.34), channel_id=1, source_target_pairs={{0,2},{2,4},{4,6},{6,7},{7,5},{5,3},{3,1},{1,0},{8,10},{10,12},{12... | collective-permute-start | bytes 884744 | tf_op jit(solution)/shard_map/ppermute | solution.py:342
  436.3 7.4 %collective-permute-start.84 = (bf16[96,1536]{1,0:T(8,128)(2,1)S(1)}, bf16[96,1536]{1,0:T(8,128)(2,1)S(1)}, u32[]{:S(2)}, u32[]{:S(2)}) collective-permute-start(bf16[96,1536]{1,0:T(8,128)(2,1)S(1)} %get-tuple-element.72), channel_id=1, source_target_pairs={{2,0},{4,2},{6,4},{7,6},{5,7},{3,5},{1,3},{0,1},{10,8},{12,10},{14... | collective-permute-start | bytes 884744 | tf_op jit(solution)/shard_map/ppermute | solution.py:345
  437.6 12.4 %collective-permute-start.74 = (bf16[384,384]{0,1:T(8,128)(2,1)S(1)}, bf16[384,384]{0,1:T(8,128)(2,1)S(1)}, u32[]{:S(2)}, u32[]{:S(2)}) collective-permute-start(bf16[384,384]{0,1:T(8,128)(2,1)S(1)} %fusion.33), channel_id=1, source_target_pairs={{2,0},{4,2},{6,4},{7,6},{5,7},{3,5},{1,3},{0,1},{10,8},{12,10},{14... | collective-permute-start | bytes 884744 | tf_op jit(solution)/shard_map/ppermute | solution.py:345
  441.6 8.4 %collective-permute-start.70 = (bf16[384,384]{0,1:T(8,128)(2,1)S(1)}, bf16[384,384]{0,1:T(8,128)(2,1)S(1)}, u32[]{:S(2)}, u32[]{:S(2)}) collective-permute-start(bf16[384,384]{0,1:T(8,128)(2,1)S(1)} %fusion.35), channel_id=1, source_target_pairs={{0,2},{2,4},{4,6},{6,7},{7,5},{5,3},{3,1},{1,0},{8,10},{10,12},{12... | collective-permute-start | bytes 884744 | tf_op jit(solution)/shard_map/ppermute | solution.py:342
  443.7 12.0 %collective-permute-start.81 = (bf16[96,1536]{1,0:T(8,128)(2,1)S(1)}, bf16[96,1536]{1,0:T(8,128)(2,1)S(1)}, u32[]{:S(2)}, u32[]{:S(2)}) collective-permute-start(bf16[96,1536]{1,0:T(8,128)(2,1)S(1)} %get-tuple-element.71), channel_id=1, source_target_pairs={{0,2},{2,4},{4,6},{6,7},{7,5},{5,3},{3,1},{1,0},{8,10},{10,12},{12... | collective-permute-start | bytes 884744 | tf_op jit(solution)/shard_map/ppermute | solution.py:342
  445.2 11.1 %collective-permute-start.85 = (bf16[96,1536]{1,0:T(8,128)(2,1)S(1)}, bf16[96,1536]{1,0:T(8,128)(2,1)S(1)}, u32[]{:S(2)}, u32[]{:S(2)}) collective-permute-start(bf16[96,1536]{1,0:T(8,128)(2,1)S(1)} %fusion.27), channel_id=1, source_target_pairs={{2,0},{4,2},{6,4},{7,6},{5,7},{3,5},{1,3},{0,1},{10,8},{12,10},{14... | collective-permute-start | bytes 884744 | tf_op jit(solution)/shard_map/ppermute | solution.py:345
  450.1 8.0 %collective-permute-start.75 = (bf16[384,384]{0,1:T(8,128)(2,1)S(1)}, bf16[384,384]{0,1:T(8,128)(2,1)S(1)}, u32[]{:S(2)}, u32[]{:S(2)}) collective-permute-start(bf16[384,384]{0,1:T(8,128)(2,1)S(1)} %fusion.37), channel_id=1, source_target_pairs={{0,16},{8,24},{16,0},{24,8},{1,17},{9,25},{17,1},{25,9},{2,18},{10... | collective-permute-start | bytes 884744 | tf_op jit(solution)/shard_map/ppermute | solution.py:354
  456.4 8.6 %collective-permute-start.86 = (bf16[96,1536]{1,0:T(8,128)(2,1)S(1)}, bf16[96,1536]{1,0:T(8,128)(2,1)S(1)}, u32[]{:S(2)}, u32[]{:S(2)}) collective-permute-start(bf16[96,1536]{1,0:T(8,128)(2,1)S(1)} %fusion.31), channel_id=1, source_target_pairs={{0,16},{8,24},{16,0},{24,8},{1,17},{9,25},{17,1},{25,9},{2,18},{10... | collective-permute-start | bytes 884744 | tf_op jit(solution)/shard_map/ppermute | solution.py:354
  458.2 11.7 %collective-permute-start.76 = (bf16[384,384]{0,1:T(8,128)(2,1)S(1)}, bf16[384,384]{0,1:T(8,128)(2,1)S(1)}, u32[]{:S(2)}, u32[]{:S(2)}) collective-permute-start(bf16[384,384]{0,1:T(8,128)(2,1)S(1)} %add_convert_fusion.6), channel_id=1, source_target_pairs={{0,8},{8,0},{16,24},{24,16},{1,9},{9,1},{17,25},{25,17},{2,10},{10... | collective-permute-start | bytes 884744 | tf_op jit(solution)/shard_map/ppermute | solution.py:348
  (79 other events, 800.7 us)

commit v2 on v1

v2 whole, which is shorter than its diff:
```python
import functools

import jax
import jax.numpy as jnp
from jax import lax
from jax.experimental import pallas as pl
from jax.experimental.pallas import tpu as pltpu
from jax.sharding import PartitionSpec as P

BLK = 64
EPSILON = 1e-05
NEG = -1e30
UNROLL = 4
LOW = jnp.bfloat16
F32 = jnp.float32


def dot_nn(left, right):
    return lax.dot_general(left, right, (((1,), (0,)), ((), ())), preferred_element_type=F32)


def dot_tn(left, right):
    return lax.dot_general(left, right, (((0,), (0,)), ((), ())), preferred_element_type=F32)


def dot_nt(left, right):
    return lax.dot_general(left, right, (((1,), (1,)), ((), ())), preferred_element_type=F32)


def normalise(values):
    centre = values - jnp.mean(values, axis=-1, keepdims=True)
    inverse = lax.rsqrt(jnp.mean(centre * centre, axis=-1, keepdims=True) + EPSILON)
    return centre * inverse, inverse


def norm_backward(upstream, normed, inverse, gain):
    scaled = upstream * gain
    mean_one = jnp.mean(scaled, axis=-1, keepdims=True)
    mean_two = jnp.mean(scaled * normed, axis=-1, keepdims=True)
    return inverse * (scaled - mean_one - normed * mean_two)


def gelu_and_slope(v):
    c = 0.7978845608028654
    t = jnp.tanh(c * (v + 0.044715 * v * v * v))
    half = 0.5 * (1.0 + t)
    slope = half + 0.5 * v * (1.0 - t * t) * (c * (1.0 + 3 * 0.044715 * v * v))
    return v * half, slope


def global_of(glob, number):
    block = glob[jnp.minimum(number, glob.shape[0] - 1)]
    on = number < glob.shape[0]
    for i in range(glob.shape[0]):
        on = on & ((i >= number) | (glob[i] != block))
    return block, on


def in_global(glob, place):
    found = glob[0] == place
    for i in range(1, glob.shape[0]):
        found = found | (glob[i] == place)
    return found


def halves():
    lane = lax.broadcasted_iota(jnp.int32, (BLK, 2 * BLK), 1)
    return lane < BLK


def stack_pair(tile):
    low = jnp.where(halves(), 1.0, 0.0).astype(tile.dtype)
    high = jnp.where(halves(), 0.0, 1.0).astype(tile.dtype)
    return jnp.concatenate([tile * low, tile * high], axis=0)


def unstack_pair(rows):
    return jnp.where(halves(), rows[:BLK], rows[BLK:])


def rows_of(ref, block, count=1):
    return ref[pl.ds(pl.multiple_of(block * BLK, BLK), count * BLK), :]


def shared_rows(ref, index, base):
    return jnp.concatenate([rows_of(ref, index[base], 3), rows_of(ref, index[base + 3])], axis=0)


def own_rows(ref, index, base):
    return jnp.concatenate([rows_of(ref, index[base + j]) for j in range(4, 8)], axis=0)


def attend_kernel(index, active, glob, where, q_ref, k_ref, v_ref, seg_q, seg_k, seg_row, o_ref, p_ref, og_ref, pg_ref, top_ref, score, *, heads, pair, shards, blocks):
    chip = where[shards + 1]
    my_glob, my_on = global_of(glob, chip)
    step = pl.program_id(0)
    wide = lax.broadcasted_iota(jnp.int32, (1, 2 * BLK), 1) < BLK
    length = k_ref.shape[0]

    @pl.when(step == 0)
    def _():
        top_ref[...] = jnp.full(top_ref.shape, NEG, F32)

        @pl.when(jnp.logical_not(my_on))
        def _():
            og_ref[...] = jnp.zeros(og_ref.shape, og_ref.dtype)
            pg_ref[...] = jnp.zeros(pg_ref.shape, pg_ref.dtype)

        @pl.when(my_on)
        def _():
            place = my_glob
            q2 = stack_pair(rows_of(q_ref, place))
            sq = rows_of(seg_q, place)
            sq = jnp.concatenate([sq, sq], axis=0)
            top = jnp.full((2 * BLK, 1), NEG, F32)
            cut = 512
            for j in range(length // cut):
                raw = dot_nt(q2, k_ref[j * cut : (j + 1) * cut, :])
                raw = jnp.where(seg_row[:, j * cut : (j + 1) * cut] == sq, raw, NEG)
                score[:, j * cut : (j + 1) * cut] = raw
                top = jnp.maximum(top, jnp.max(raw, axis=1, keepdims=True))
            total = jnp.zeros((2 * BLK, 1), F32)
            for j in range(length // cut):
                power = jnp.exp(score[:, j * cut : (j + 1) * cut] - top)
                score[:, j * cut : (j + 1) * cut] = power
                total = total + jnp.sum(power, axis=1, keepdims=True)
            scale = 1.0 / total
            acc = jnp.zeros((2 * BLK, 2 * BLK), F32)
            for j in range(length // cut):
                prob = (score[:, j * cut : (j + 1) * cut] * scale).astype(LOW)
                pg_ref[:, j * cut : (j + 1) * cut] = prob
                acc = acc + dot_nn(prob, v_ref[j * cut : (j + 1) * cut, :])
            og_ref[...] = unstack_pair(acc).astype(LOW)
            top_ref[...] = jnp.maximum(top_ref[...], jnp.broadcast_to(top, top_ref.shape))

    for u in range(UNROLL):
        b = step * UNROLL + u
        place = chip * blocks + b
        q2 = stack_pair(rows_of(q_ref, place))
        sq = rows_of(seg_q, place)
        sq = jnp.concatenate([sq, sq], axis=0)
        base = (b * heads + 2 * pair) * 8
        shared = dot_nt(q2, shared_rows(k_ref, index, base))
        own = jnp.concatenate(
            [dot_nt(q2[h * BLK : (h + 1) * BLK], own_rows(k_ref, index, base + 8 * h)) for h in range(2)],
            axis=0,
        )

        def seg_of(at, j):
            first = seg_k[pl.ds(active[at + j], 1), :]
            second = seg_k[pl.ds(active[at + j + 1], 1), :]
            return jnp.where(wide, first, second)

        raw_s = jnp.where(jnp.concatenate([seg_of(base, 0), seg_of(base, 2)], axis=1) == sq, shared, NEG)
        seg_own = [
            jnp.broadcast_to(
                jnp.concatenate([seg_of(base + 8 * h, 4), seg_of(base + 8 * h, 6)], axis=1), (BLK, 4 * BLK)
            )
            for h in range(2)
        ]
        raw_o = jnp.where(jnp.concatenate(seg_own, axis=0) == sq, own, NEG)
        top = jnp.maximum(jnp.max(raw_s, axis=1, keepdims=True), jnp.max(raw_o, axis=1, keepdims=True))
        power_s = jnp.exp(raw_s - top)
        power_o = jnp.exp(raw_o - top)
        scale = 1.0 / (jnp.sum(power_s, axis=1, keepdims=True) + jnp.sum(power_o, axis=1, keepdims=True))
        prob_s = (power_s * scale).astype(LOW)
        prob_o = (power_o * scale).astype(LOW)
        p_ref[u, :, : 4 * BLK] = prob_s
        p_ref[u, :, 4 * BLK :] = prob_o
        out = dot_nn(prob_s, shared_rows(v_ref, index, base))
        out = out + jnp.concatenate(
            [
                dot_nn(prob_o[h * BLK : (h + 1) * BLK], own_rows(v_ref, index, base + 8 * h))
                for h in range(2)
            ],
            axis=0,
        )
        o_ref[u * BLK : (u + 1) * BLK, :] = unstack_pair(out).astype(LOW)
        used = jnp.where(in_global(glob, place), jnp.full_like(top, NEG), top)
        top_ref[...] = jnp.maximum(top_ref[...], jnp.broadcast_to(used, top_ref.shape))


def pull_kernel(index, active, glob, where, q_ref, k_ref, v_ref, do_ref, p_ref, pg_ref, *refs, heads, pair, shards, blocks):
    *dog_refs, dq_ref, dk_ref, dv_ref, dk, dv, score = refs
    chip = where[shards + 1]
    my_glob, my_on = global_of(glob, chip)
    del active
    step = pl.program_id(0)
    steps = pl.num_programs(0)
    length = k_ref.shape[0]

    @pl.when(step == 0)
    def _():
        dk[...] = jnp.zeros(dk.shape, F32)
        dv[...] = jnp.zeros(dv.shape, F32)
        dq_ref[...] = jnp.zeros(dq_ref.shape, dq_ref.dtype)

    def add(ref, block, value):
        at = pl.ds(pl.multiple_of(block * BLK, BLK), value.shape[0])
        ref[at, :] += value

    for u in range(UNROLL):
        b = step * UNROLL + u
        place = chip * blocks + b
        q2 = stack_pair(rows_of(q_ref, place))
        keep = jnp.where(in_global(glob, place), 0.0, 1.0).astype(LOW)
        do2 = stack_pair(do_ref[u * BLK : (u + 1) * BLK, :] * keep)
        base = (b * heads + 2 * pair) * 8
        ks = shared_rows(k_ref, index, base)
        ko = [own_rows(k_ref, index, base + 8 * h) for h in range(2)]
        vs = shared_rows(v_ref, index, base)
        vo = [own_rows(v_ref, index, base + 8 * h) for h in range(2)]
        prob_s = p_ref[u, :, : 4 * BLK]
        prob_o = p_ref[u, :, 4 * BLK :]
        dp_s = dot_nt(do2, vs)
        dp_o = jnp.concatenate([dot_nt(do2[h * BLK : (h + 1) * BLK], vo[h]) for h in range(2)], axis=0)
        ps = prob_s.astype(F32)
        po = prob_o.astype(F32)
        ts = ps * dp_s
        to = po * dp_o
        total = jnp.sum(ts, axis=1, keepdims=True) + jnp.sum(to, axis=1, keepdims=True)
        ds_s = (ts - ps * total).astype(LOW)
        ds_o = (to - po * total).astype(LOW)
        dq = dot_nn(ds_s, ks) + jnp.concatenate(
            [dot_nn(ds_o[h * BLK : (h + 1) * BLK], ko[h]) for h in range(2)], axis=0
        )
        at = pl.ds(pl.multiple_of(place * BLK, BLK), BLK)
        dq_ref[at, :] = (unstack_pair(dq) * 0.125).astype(LOW)
        dks = dot_tn(ds_s, q2)
        dvs = dot_tn(prob_s, do2)
        add(dk, index[base], dks[: 3 * BLK])
        add(dk, index[base + 3], dks[3 * BLK :])
        add(dv, index[base], dvs[: 3 * BLK])
        add(dv, index[base + 3], dvs[3 * BLK :])
        for h in range(2):
            part = slice(h * BLK, (h + 1) * BLK)
            dko = dot_tn(ds_o[part], q2[part])
            dvo = dot_tn(prob_o[part], do2[part])
            for j in range(4):
                add(dk, index[base + 8 * h + 4 + j], dko[j * BLK : (j + 1) * BLK])
                add(dv, index[base + 8 * h + 4 + j], dvo[j * BLK : (j + 1) * BLK])

    @pl.when((step == steps - 1) & my_on)
    def _():
        place = my_glob
        q2 = stack_pair(rows_of(q_ref, place))
        dog = dog_refs[0][...].astype(F32)
        for ref in dog_refs[1:]:
            dog = dog + ref[...].astype(F32)
        do2 = stack_pair(dog.astype(LOW))
        cut = 512
        total = jnp.zeros((2 * BLK, 1), F32)
        for j in range(length // cut):
            part = slice(j * cut, (j + 1) * cut)
            dp = dot_nt(do2, v_ref[part, :])
            score[:, part] = dp
            total = total + jnp.sum(pg_ref[:, part].astype(F32) * dp, axis=1, keepdims=True)
        acc = jnp.zeros((2 * BLK, 2 * BLK), F32)
        for j in range(length // cut):
            part = slice(j * cut, (j + 1) * cut)
            prob = pg_ref[:, part]
            ds = (prob.astype(F32) * (score[:, part] - total)).astype(LOW)
            acc = acc + dot_nn(ds, k_ref[part, :])
            dk[part, :] += dot_tn(ds, q2)
            dv[part, :] += dot_tn(prob, do2)
        at = pl.ds(pl.multiple_of(place * BLK, BLK), BLK)
        dq_ref[at, :] = (unstack_pair(acc) * 0.125).astype(LOW)

    @pl.when(step == steps - 1)
    def _():
        dk_ref[...] = dk[...].astype(LOW)
        dv_ref[...] = dv[...].astype(LOW)


def attend(index, active, glob, where, query, key, value, seg_col, seg_rep, seg_row, blocks, heads, pair, shards):
    length = key.shape[0]
    column = pl.BlockSpec((length, 2 * BLK), lambda s, *_: (0, pair))
    whole = lambda shape: pl.BlockSpec(shape, lambda s, *_: (0,) * len(shape))
    grid = pltpu.PrefetchScalarGridSpec(
        num_scalar_prefetch=4,
        grid=(blocks // UNROLL,),
        in_specs=[column, column, column, whole(seg_col.shape), whole(seg_rep.shape), whole(seg_row.shape)],
        out_specs=[
            pl.BlockSpec((UNROLL * BLK, 2 * BLK), lambda s, *_: (s, 0)),
            pl.BlockSpec((UNROLL, 2 * BLK, 8 * BLK), lambda s, *_: (s, 0, 0)),
            whole((BLK, 2 * BLK)),
            whole((2 * BLK, length)),
            whole((2 * BLK, 2 * BLK)),
        ],
        scratch_shapes=[pltpu.VMEM((2 * BLK, length), F32)],
    )
    work = (blocks * 8 + length // BLK) * 2 * BLK * BLK
    return pl.pallas_call(
        functools.partial(attend_kernel, heads=heads, pair=pair, shards=shards, blocks=blocks),
        grid_spec=grid,
        out_shape=[
            jax.ShapeDtypeStruct((blocks * BLK, 2 * BLK), LOW),
            jax.ShapeDtypeStruct((blocks, 2 * BLK, 8 * BLK), LOW),
            jax.ShapeDtypeStruct((BLK, 2 * BLK), LOW),
            jax.ShapeDtypeStruct((2 * BLK, length), LOW),
            jax.ShapeDtypeStruct((2 * BLK, 2 * BLK), F32),
        ],
        compiler_params=pltpu.CompilerParams(vmem_limit_bytes=32 << 20),
        cost_estimate=pl.CostEstimate(flops=work * 8192, bytes_accessed=6 << 20, transcendentals=work),
        name="attend",
    )(index, active, glob, where, query, key, value, seg_col, seg_rep, seg_row)


def pull(index, active, glob, where, query, key, value, grad, grad_glob, probs, probs_glob, heads, pair, shards):
    length = key.shape[0]
    blocks = grad.shape[0] // BLK
    column = pl.BlockSpec((length, 2 * BLK), lambda s, *_: (0, pair))
    whole = lambda shape: pl.BlockSpec(shape, lambda s, *_: (0,) * len(shape))
    grid = pltpu.PrefetchScalarGridSpec(
        num_scalar_prefetch=4,
        grid=(blocks // UNROLL,),
        in_specs=[
            column,
            column,
            column,
            pl.BlockSpec((UNROLL * BLK, 2 * BLK), lambda s, *_: (s, pair)),
            pl.BlockSpec((UNROLL, 2 * BLK, 8 * BLK), lambda s, *_: (s, 0, 0)),
            whole((2 * BLK, length)),
        ]
        + [pl.BlockSpec((BLK, 2 * BLK), lambda s, *_: (0, pair))] * len(grad_glob),
        out_specs=[whole((length, 2 * BLK))] * 3,
        scratch_shapes=[
            pltpu.VMEM((length, 2 * BLK), F32),
            pltpu.VMEM((length, 2 * BLK), F32),
            pltpu.VMEM((2 * BLK, length), F32),
        ],
    )
    work = (blocks * 8 + length // BLK) * 2 * BLK * BLK
    return pl.pallas_call(
        functools.partial(pull_kernel, heads=heads, pair=pair, shards=shards, blocks=blocks),
        grid_spec=grid,
        out_shape=[jax.ShapeDtypeStruct((length, 2 * BLK), LOW)] * 3,
        compiler_params=pltpu.CompilerParams(vmem_limit_bytes=32 << 20),
        cost_estimate=pl.CostEstimate(flops=work * 8192, bytes_accessed=8 << 20, transcendentals=0),
        name="pull",
    )(index, active, glob, where, query, key, value, grad, probs, probs_glob, *grad_glob)


def eye(size):
    row = lax.broadcasted_iota(jnp.int32, (size, size), 0)
    column = lax.broadcasted_iota(jnp.int32, (size, size), 1)
    return jnp.where(row == column, 1.0, 0.0).astype(LOW)


def lanes(start, size):
    return pl.ds(pl.multiple_of(start, 128), size)


def simple_call(kernel, out_shape, args, scalars, name, cost, scratch=(), anywhere=0, limit=32):
    smem = pl.BlockSpec(memory_space=pltpu.SMEM)
    vmem = pl.BlockSpec(memory_space=pltpu.VMEM)
    free = pl.BlockSpec(memory_space=pl.ANY)
    specs = [smem] * len(scalars) + [free] * anywhere + [vmem] * (len(args) - anywhere)
    return pl.pallas_call(
        kernel,
        in_specs=specs,
        out_specs=jax.tree.map(lambda _: vmem, out_shape),
        out_shape=out_shape,
        scratch_shapes=list(scratch),
        compiler_params=pltpu.CompilerParams(vmem_limit_bytes=limit << 20),
        cost_estimate=pl.CostEstimate(flops=cost[0], bytes_accessed=cost[1], transcendentals=0),
        name=name,
    )(*scalars, *args)


def pack_heads_kernel(where, wq, wk, wv, *refs, shards):
    *vectors, out, rows_ref = refs
    half, cols = wq.shape[0] // 2, wq.shape[1]
    core = where[shards]
    unit = eye(cols)
    for i, ref in enumerate((wq, wk, wv)):
        rows = ref[pl.ds(pl.multiple_of(core * half, 128), half), :].astype(LOW)
        out[i * cols : (i + 1) * cols, :] = dot_nt(unit, rows).astype(LOW)
    rows_ref[...] = jnp.zeros(rows_ref.shape, F32)
    for v, ref in enumerate(vectors[:-1]):
        at = v % 3 * 128
        rows_ref[v // 3 : v // 3 + 1, at : at + cols] = ref[...]
    rows_ref[3:4, : vectors[-1].shape[1]] = vectors[-1][...]
    out[3 * cols :, :] = rows_ref[...].astype(LOW)


def pack_rest_kernel(where, inner, output, outer, out_one, out_two, *, shards):
    half, cols = output.shape[0] // 2, output.shape[1]
    wide = inner.shape[1]
    unit, unit_wide = eye(cols), eye(wide)
    core = where[shards]
    rows = inner[pl.ds(pl.multiple_of(core * half, 128), half), :].astype(LOW)
    out_one[...] = dot_nt(unit_wide, rows).astype(LOW)
    rows = output[pl.ds(pl.multiple_of(core * half, 128), half), :].astype(LOW)
    out_two[:cols, :] = dot_nt(unit, rows).astype(LOW)
    count = outer.shape[0] // 2 // half
    for j in range(count):
        start = (core * count + j) * half
        rows = outer[pl.ds(pl.multiple_of(start, 128), half), :].astype(LOW)
        at = cols * (1 + j)
        out_two[at : at + cols, :] = dot_nt(unit, rows).astype(LOW)


def project_kernel(
    where, got, passed, mine, theirs, q_ref, k_ref, v_ref, wh, vec, bias_inner, pieces, sem, *, rows, chips, cols, wide
):
    shards, half = pieces.shape[1], pieces.shape[3]
    core, chip = where[shards], where[shards + 1]
    copies = []
    for side, ref in enumerate((got, passed)):
        for i in range(shards):
            copies.append(pltpu.make_async_copy(ref.at[i], pieces.at[side, where[i]], sem.at[side, i]))
    for copy in copies:
        copy.start()
    for copy in copies:
        copy.wait()
    for side in range(2):
        for t in range(3):
            part = pieces[side, pl.ds(core * (shards // 2), shards // 2), t * cols : (t + 1) * cols, :]
            wh[side, t] = part.reshape(half, half)
    for i in range(shards):
        small = pieces[0, i, 3 * cols :, :].astype(F32)
        for v in range(8):
            at = v % 3 * 128
            vec[v : v + 1, i * cols : (i + 1) * cols] = small[v // 3 : v // 3 + 1, at : at + cols]
        unit, at = i * wide // half, i * wide % half
        bias_inner[unit : unit + 1, at : at + wide] = small[3:4, :wide]
    own_lanes, other_lanes = lanes(core * half, half), lanes((1 - core) * half, half)
    for j in range(chips):
        source = lax.rem(chip - j + chips, chips)
        for side, ref in enumerate((mine, theirs)):
            place = (2 * source + (core if side == 0 else 1 - core)) * rows
            at = pl.ds(pl.multiple_of(place, rows), rows)
            left = ref[j * rows : (j + 1) * rows, own_lanes]
            right = ref[j * rows : (j + 1) * rows, other_lanes]
            for t, out in enumerate((q_ref, k_ref, v_ref)):
                value = dot_nt(left, wh[0, t]) + dot_nt(right, wh[1, t])
                if t == 0:
                    value = (value + vec[0:1, own_lanes]).astype(LOW).astype(F32) * 0.125
                if t == 2:
                    value = value + vec[1:2, own_lanes]
                out[at, :] = value.astype(LOW)


def merge_kernel(where, glob, *refs, shards, chips, rows):
    outs = refs[-2:]
    parts, globs = refs[: -2 - chips], refs[-2 - chips : -2]
    core, chip = where[shards], where[shards + 1]
    full = jnp.concatenate
    for side, out in enumerate(outs):
        start = (core if side == 0 else 1 - core) * rows
        out[...] = full([p[pl.ds(pl.multiple_of(start, rows), rows), :] for p in parts], axis=1)
    per = 2 * rows // BLK
    for j in range(chips):
        number = lax.rem(chip - j + chips, chips)
        block, on = global_of(glob, number)
        local = block - chip * per
        for side, out in enumerate(outs):
            start = local - (core if side == 0 else 1 - core) * (per // 2)

            @pl.when(on & (start >= 0) & (start < per // 2))
            def _(out=out, start=start, j=j):
                out[pl.ds(pl.multiple_of(start * BLK, BLK), BLK), :] = globs[j][...]


def spread_kernel(where, glob, own, other, heads_grad, *sends, shards, chips, rows):
    core, chip = where[shards], where[shards + 1]
    heads_grad[pl.ds(pl.multiple_of(core * rows, rows), rows), :] = own[...]
    heads_grad[pl.ds(pl.multiple_of((1 - core) * rows, rows), rows), :] = other[...]
    per = 2 * rows // BLK
    for j, send in enumerate(sends):
        number = lax.rem(chip + j, chips)
        block, on = global_of(glob, number)
        local = block - chip * per
        send[...] = jnp.zeros(send.shape, send.dtype)

        @pl.when(on & (local >= 0) & (local < per))
        def _(send=send, local=local):
            send[...] = heads_grad[pl.ds(pl.multiple_of(local * BLK, BLK), BLK), :]


def weight_grad_kernel(
    where, *refs, rows, chips, pairs, cols, wide, shards, devices
):
    grads = refs[: 3 * pairs]
    tops = refs[3 * pairs : 4 * pairs]
    mine, theirs, vec_grad, inner_bias, layout, keep, give, small, vec = refs[4 * pairs :]
    core, chip = where[shards], where[shards + 1]
    half = mine.shape[1] // 2
    vec[...] = vec_grad[...]
    vec[0:2, :] = jnp.zeros((2, vec.shape[1]), F32)
    for t in range(3):
        whole = [jnp.zeros((half, half), F32)] * 2
        total = jnp.zeros((1, half), F32)
        for j in range(chips):
            source = lax.rem(chip - j + chips, chips)
            for side, ref in enumerate((mine, theirs)):
                place = (2 * source + (core if side == 0 else 1 - core)) * rows
                at = pl.ds(pl.multiple_of(place, rows), rows)
                part = jnp.concatenate([g[at, :] for g in grads[t * pairs : (t + 1) * pairs]], axis=1)
                if t != 1:
                    total = total + jnp.sum(part.astype(F32), axis=0, keepdims=True)
                for s in range(2):
                    which = core if s == 0 else 1 - core
                    whole[s] = whole[s] + dot_tn(part, ref[j * rows : (j + 1) * rows, lanes(which * half, half)])
        for s, out in enumerate((keep, give)):
            out[:, t * cols : (t + 1) * cols, :] = whole[s].astype(LOW).reshape(shards // 2, cols, half)
        if t != 1:
            vec[t // 2 : t // 2 + 1, lanes(core * half, half)] = total
    head, part, slot = layout[0:1, :], layout[1:2, :], layout[2:3, :]
    value = jnp.full((1, half), NEG, F32)
    for p in range(pairs):
        for i in range(2):
            top = jnp.max(tops[p][i * BLK : (i + 1) * BLK, :], axis=0, keepdims=True)
            value = jnp.where(head == core * 2 * pairs + 2 * p + i, top[:, 0:1], value)
    first = value.astype(LOW).astype(F32)
    second = (value - first).astype(LOW).astype(F32)
    third = value - first - second
    value = jnp.where(part == 0, first, jnp.where(part == 1, second, jnp.where(part == 2, third, 0.0)))
    small[...] = jnp.zeros(small.shape, F32)
    device = where[shards + 3]
    value = jnp.where(slot == lax.rem(device, 8), value, 0.0)
    for r in range(devices // 8):
        line = jnp.where(device // 8 == r, value, 0.0)
        for i in range(shards):
            small[i, 4 + r : 5 + r, :] = line
    for i in range(shards):
        for v in range(8):
            at = v % 3 * 128
            small[i, v // 3 : v // 3 + 1, at : at + cols] = vec[v : v + 1, i * cols : (i + 1) * cols]
        unit, at = i * wide // half, i * wide % half
        small[i, 3:4, :wide] = inner_bias[unit : unit + 1, at : at + wide]


def token_grad_kernel(where, *refs, rows, chips, pairs, shards):
    grads, (wh, mine, theirs) = refs[: 3 * pairs], refs[3 * pairs :]
    core, chip = where[shards], where[shards + 1]
    half = mine.shape[1] // 2
    for j in range(chips):
        source = lax.rem(chip - j + chips, chips)
        for side, out in enumerate((mine, theirs)):
            place = (2 * source + (core if side == 0 else 1 - core)) * rows
            at = pl.ds(pl.multiple_of(place, rows), rows)
            parts = [
                jnp.concatenate([g[at, :] for g in grads[t * pairs : (t + 1) * pairs]], axis=1) for t in range(3)
            ]
            for s in range(2):
                which = core if s == 0 else 1 - core
                total = dot_nn(parts[0], wh[s, 0]) + dot_nn(parts[1], wh[s, 1]) + dot_nn(parts[2], wh[s, 2])
                out[j * rows : (j + 1) * rows, lanes(which * half, half)] = total.astype(LOW)


def finish_heads_kernel(where, own, other, limits, wq, wk, *outs, shards, devices, head_dim):
    grads, vectors, (inner, maxima, cut_q, cut_k) = outs[:3], outs[3:11], outs[11:]
    core, shard = where[shards], where[shards + 2]
    half, cols = own.shape[1], wq.shape[1]
    unit = eye(half)
    for t, out in enumerate(grads):
        for ref, which in ((own, core), (other, 1 - core)):
            value = dot_nt(unit, ref[t * cols : (t + 1) * cols, :])
            out[pl.ds(pl.multiple_of(which * half, 128), half), :] = value
    small = own[3 * cols :, :].astype(F32) + other[3 * cols :, :].astype(F32)
    for v, out in enumerate(vectors):
        at = v % 3 * 128
        out[...] = small[v // 3 : v // 3 + 1, at : at + cols]
    inner[...] = small[3:4, : inner.shape[1]]
    heads = limits.shape[1]
    value = jnp.full((1, half), NEG, F32)
    for r in range(devices // 8):
        line = jnp.broadcast_to(small[4 + r : 5 + r, :], (8, half))
        line = line + pltpu.roll(line, half - heads, 1) + pltpu.roll(line, half - 2 * heads, 1)
        value = jnp.maximum(value, line)
    step = half // 2
    while step >= 48:
        value = jnp.maximum(value, pltpu.roll(value, step, 1))
        step //= 2
    top = value[0:1, :heads]
    maxima[...] = top
    root = jnp.sqrt(limits[...] / jnp.maximum(top, limits[...]))
    column = lax.broadcasted_iota(jnp.int32, (1, cols), 1) + shard * cols
    scale = jnp.zeros((1, cols), F32)
    for h in range(heads):
        inside = (column >= h * head_dim) & (column < (h + 1) * head_dim)
        scale = jnp.where(inside, root[:, h : h + 1], scale)
    cut_q[...] = wq[...] * scale
    cut_k[...] = wk[...] * scale


def finish_rest_kernel(where, own_one, other_one, own_two, other_two, inner, output, outer, *, shards):
    half, cols = own_one.shape[1], output.shape[1]
    unit = eye(half)
    core = where[shards]
    for one, two, which in ((own_one, own_two, core), (other_one, other_two, 1 - core)):
        inner[pl.ds(pl.multiple_of(which * half, 128), half), :] = dot_nt(unit, one[...])
        output[pl.ds(pl.multiple_of(which * half, 128), half), :] = dot_nt(unit, two[:cols, :])
        count = outer.shape[0] // 2 // half
        for j in range(count):
            at = cols * (1 + j)
            start = (which * count + j) * half
            outer[pl.ds(pl.multiple_of(start, 128), half), :] = dot_nt(unit, two[at : at + cols, :])


def dense_kernel(
    where, one_a, one_b, one_c, one_d, two_a, two_b, two_c, two_d, att_own, att_other, tokens, cotangent, vec, bias_inner,
    layer_out, resid, grad_own, grad_other, keep_one, give_one, keep_two, give_two, vec_grad, inner_bias_grad,
    one, two, low, hidden, normed, inverse, act, slope, acc, outer_grad, sem,
):
    shards, wide, half = one.shape[1:]
    rows, width = tokens.shape
    cols = width // shards
    core = where[shards]
    copies = []
    for n, (packed, sources) in enumerate(
        ((two, ((two_a, two_b), (two_c, two_d))), (one, ((one_a, one_b), (one_c, one_d))))
    ):
        for side, pair in enumerate(sources):
            at = 0
            for ref in pair:
                for i in range(ref.shape[0]):
                    copies.append(pltpu.make_async_copy(ref.at[i], packed.at[side, where[at]], sem.at[n, side, at]))
                    at += 1
    for copy in copies:
        copy.start()
    for copy in copies:
        copy.wait()
    own, other = lanes(core * half, half), lanes((1 - core) * half, half)
    sides = (own, other)
    units = shards * wide // half
    each = half // wide
    step = 128

    def inner_weights(side, u):
        return one[side, u * each : (u + 1) * each].reshape(half, half)

    def outer_at(u):
        begin = cols * (1 + u % (units // 2))
        return slice(begin, begin + cols)

    def outer_weights(u):
        side = jnp.where(core == u // (units // 2), 0, 1)
        return two[side, :, outer_at(u), :].reshape(width, half)

    def output_weights(side):
        return two[side, :, :cols, :].reshape(width, half)

    acc[...] = dot_nt(att_own[...], output_weights(0)) + dot_nt(att_other[...], output_weights(1))
    for r in range(0, rows, step):
        at = slice(r, r + step)
        n, inv = normalise(tokens[at, :] + (acc[at, :] + vec[2:3, :]))
        normed[at, :] = n
        inverse[at, :] = inv
        h = n * vec[4:5, :] + vec[5:6, :]
        hidden[at, :] = h
        low[at, :] = h.astype(LOW)

    for u in range(units):
        inner = dot_nt(low[:, own], inner_weights(0, u)) + dot_nt(low[:, other], inner_weights(1, u))
        a, d = gelu_and_slope(inner + bias_inner[u : u + 1, :])
        act[u] = a.astype(LOW)
        slope[u] = d
        product = dot_nt(act[u], outer_weights(u))
        acc[...] = product if u == 0 else acc[...] + product

    sums = [jnp.zeros((1, width), F32)] * 3
    for r in range(0, rows, step):
        at = slice(r, r + step)
        n, inv = normalise(hidden[at, :] + (acc[at, :] + vec[3:4, :]))
        layer_out[at, :] = n * vec[6:7, :] + vec[7:8, :]
        e = cotangent[at, :]
        dv = norm_backward(e, n, inv, vec[6:7, :])
        acc[at, :] = dv
        dl = dv.astype(LOW)
        outer_grad[at, :] = dl
        sums = [
            sums[0] + jnp.sum(dl.astype(F32), axis=0, keepdims=True),
            sums[1] + jnp.sum(e * n, axis=0, keepdims=True),
            sums[2] + jnp.sum(e, axis=0, keepdims=True),
        ]
    vec_grad[3:4, :] = sums[0]
    vec_grad[6:7, :] = sums[1]
    vec_grad[7:8, :] = sums[2]

    turned = outer_grad[...].T
    for u in range(units):
        inner_grad = dot_nn(outer_grad[...], outer_weights(u)) * slope[u]
        inner_low = inner_grad.astype(LOW)
        inner_bias_grad[u : u + 1, :] = jnp.sum(inner_low.astype(F32), axis=0, keepdims=True)
        for side, at in enumerate(sides):
            acc[:, at] += dot_nn(inner_low, inner_weights(side, u))
        inner_turned = inner_low.T
        for out, at in ((keep_one, own), (give_one, other)):
            part = dot_nn(inner_turned, low[:, at]).astype(LOW)
            out[u * each : (u + 1) * each] = part.reshape(each, wide, half)
        part = dot_nn(turned, act[u]).astype(LOW).reshape(shards, cols, half)

        @pl.when(core == u // (units // 2))
        def _(u=u, part=part):
            keep_two[:, outer_at(u), :] = part

        @pl.when(core != u // (units // 2))
        def _(u=u, part=part):
            give_two[:, outer_at(u), :] = part

    sums = [jnp.zeros((1, width), F32)] * 3
    for r in range(0, rows, step):
        at = slice(r, r + step)
        e, n = acc[at, :], normed[at, :]
        dv = norm_backward(e, n, inverse[at, :], vec[4:5, :])
        resid[at, :] = dv
        dl = dv.astype(LOW)
        outer_grad[at, :] = dl
        sums = [
            sums[0] + jnp.sum(dl.astype(F32), axis=0, keepdims=True),
            sums[1] + jnp.sum(e * n, axis=0, keepdims=True),
            sums[2] + jnp.sum(e, axis=0, keepdims=True),
        ]
    vec_grad[0:2, :] = jnp.zeros((2, width), F32)
    vec_grad[2:3, :] = sums[0]
    vec_grad[4:5, :] = sums[1]
    vec_grad[5:6, :] = sums[2]
    grad_own[...] = dot_nn(outer_grad[...], output_weights(0)).astype(LOW)
    grad_other[...] = dot_nn(outer_grad[...], output_weights(1)).astype(LOW)
    turned = outer_grad[...].T
    for out, ref in ((keep_two, att_own), (give_two, att_other)):
        part = dot_nn(turned, ref[...]).astype(LOW)
        out[:, :cols, :] = part.reshape(shards, cols, half)


def ring_kernel(where, *refs, counts, kind, cut):
    refs = list(refs)
    parts = []
    for count in counts:
        total = refs.pop(0)[0].astype(F32)
        for _ in range(count - 1):
            total = total + refs.pop(0)[0].astype(F32)
        parts.append(total)
    if kind == "first":
        up, down = refs
        up[...] = parts[0][:cut].astype(LOW)
        down[...] = parts[0][cut:].astype(LOW)
    elif kind == "second":
        above, below, up, down = refs
        up[:cut, :] = (parts[0][:cut] + above[...].astype(F32)).astype(LOW)
        up[cut:, :] = parts[0][cut:].astype(LOW)
        down[:cut, :] = parts[1][:cut].astype(LOW)
        down[cut:, :] = (parts[1][cut:] + below[...].astype(F32)).astype(LOW)
    elif kind == "later":
        above, below, up, down = refs
        up[...] = (parts[0] + above[...].astype(F32)).astype(LOW)
        down[...] = (parts[1] + below[...].astype(F32)).astype(LOW)
    else:
        above, below, out = refs
        out[...] = (parts[0] + above[...].astype(F32) + below[...].astype(F32)).astype(LOW)


def ring_step(where, arrays, slots, received, kind, cut):
    rows, half = arrays[0].shape[1:]
    specs = [
        pl.BlockSpec((1, rows, half), lambda i, where, slot=slot: (where[slot], 0, 0)) for slot in slots for _ in arrays
    ]
    specs += [pl.BlockSpec(a.shape, lambda i, where: (0, 0)) for a in received]
    shapes = [(rows, half)] if kind == "last" else [(rows, half)] * 2
    if kind == "first":
        shapes = [(cut, half), (rows - cut, half)]
    return pl.pallas_call(
        functools.partial(ring_kernel, counts=[len(arrays)] * len(slots), kind=kind, cut=cut),
        grid_spec=pltpu.PrefetchScalarGridSpec(
            num_scalar_prefetch=1,
            grid=(1,),
            in_specs=specs,
            out_specs=[pl.BlockSpec(s, lambda i, where: (0, 0)) for s in shapes],
        ),
        out_shape=[struct(s) for s in shapes],
        compiler_params=pltpu.CompilerParams(vmem_limit_bytes=32 << 20),
        cost_estimate=pl.CostEstimate(flops=10**6, bytes_accessed=3 << 20, transcendentals=0),
        name="ring_" + kind,
    )(where, *[a for _ in slots for a in arrays], *received)


class Moves:
    def __init__(self, ctx, wshard):
        self.ctx, self.wshard, self.chips = ctx, wshard, ctx // 2
        self.half = half = wshard // 2
        order = list(range(0, wshard, 2)) + list(range(wshard - 1, 0, -2))
        self.up_perm = [(order[i], order[(i + 1) % wshard]) for i in range(wshard)]
        self.down_perm = [(b, a) for a, b in self.up_perm]
        deltas = [0]
        for step in range(1, half):
            deltas += [-step, step]
        deltas.append(half)
        sums = [half]
        for step in range(half - 1, 0, -1):
            sums += [step, -step]
        sums.append(0)
        table = []
        for c in range(ctx):
            for w in range(wshard):
                at = order.index(w)
                goes = [order[(at + d) % wshard] for d in sums]
                placed = [(s // half != c % 2) * half + s % half for s in goes]
                table.append(
                    [order[(at + d) % wshard] for d in deltas] + [c % 2, c // 2, w, c * wshard + w] + goes + placed
                )
        self.sums, self.placed = wshard + 4, wshard + 4 + len(sums)
        here = lax.axis_index("ctx") * wshard + lax.axis_index("wshard")
        table = jnp.asarray(table, jnp.int32)
        self.where = lax.dynamic_slice(table, (here, 0), (1, table.shape[1]), allow_negative_indices=False)[0]

    def up(self, value):
        return lax.ppermute(value, "wshard", self.up_perm)

    def down(self, value):
        return lax.ppermute(value, "wshard", self.down_perm)

    def swap(self, value):
        return lax.ppermute(value, "ctx", [(c, c ^ 1) for c in range(self.ctx)])

    def chip_shift(self, value, j):
        return lax.ppermute(value, "ctx", [(c, (c + 2 * j) % self.ctx) for c in range(self.ctx)])

    def chip_flip(self, value, bit):
        return lax.ppermute(value, "ctx", [(c, c ^ (2 * bit)) for c in range(self.ctx)])

    def gather(self, piece, cut):
        above = below = piece
        pieces = [piece]
        for _ in range(1, self.half):
            above, below = self.up(above), self.down(below)
            pieces += [above, below]
        pieces.append(jnp.concatenate([self.up(above[:cut]), self.down(below[cut:])], axis=0))
        return pieces

    def scatter(self, step, cut):
        up, down = step("first", [0], [])
        yield up
        for s in range(self.half - 1):
            above, below = self.up(up), self.down(down)
            up, down = step("second" if s == 0 else "later", [1 + 2 * s, 2 + 2 * s], [above, below])
            yield up
        above, below = self.up(up), self.down(down)
        [total] = step("last", [2 * self.half - 1], [above, below])
        yield total

    def chip_sum(self, value):
        bit = 1
        while bit < self.chips:
            other = self.chip_flip(value, bit)
            value = (value.astype(F32) + other.astype(F32)).astype(LOW)
            bit *= 2
        return value


def slot_lists(first, count, nblocks, glob, random_rows, heads):
    blocks = first + jnp.arange(count, dtype=jnp.int32)
    offsets = jnp.arange(-1, 2, dtype=jnp.int32)
    start = jnp.clip(blocks - 1, 0, nblocks - 3)
    window = start[:, None] + jnp.arange(3, dtype=jnp.int32)[None, :]
    near = jnp.abs(window - blocks[:, None]) <= 1
    slide = jnp.clip(blocks[:, None] + offsets[None, :], 0, nblocks - 1)
    spread = lambda a: jnp.broadcast_to(a[:, None, :], (count, heads, a.shape[-1]))
    rest = jnp.concatenate(
        [jnp.broadcast_to(glob[None, None, :], (count, heads, glob.shape[0])), random_rows], axis=2
    )
    lists = jnp.concatenate([spread(slide), rest], axis=2)
    slots = lists.shape[2]
    equal = lists[..., :, None] == lists[..., None, :]
    earlier = jnp.arange(slots)[:, None] < jnp.arange(slots)[None, :]
    fresh = jnp.logical_not(jnp.any(equal & earlier[None, None], axis=-2))
    on = jnp.concatenate([spread(near), fresh[..., 3:]], axis=2)
    index = jnp.concatenate([spread(window), rest], axis=2)
    return index, jnp.where(on, index, nblocks)


def struct(shape, dtype=LOW):
    return jax.ShapeDtypeStruct(tuple(shape), dtype)


def after(value, *others):
    return lax.optimization_barrier((value,) + others)[0]


def per_device(ctx, wshard, layer_input, segments, global_blocks, random_blocks, thresholds, w_query, w_key, w_value, w_output, w_inner, w_outer, query_bias, value_bias, output_bias, inner_bias, outer_bias, gain_attn, shift_attn, gain_mlp, shift_mlp, out_grad):
    m = Moves(ctx, wshard)
    chips, where, devices = m.chips, m.where, ctx * wshard
    tokens = layer_input[0]
    rows_here, width = tokens.shape
    seg_all = segments[0]
    length = seg_all.shape[0]
    glob = global_blocks[0]
    heads = thresholds.shape[0]
    head_dim = width // heads
    nblocks = length // BLK
    count = 2 * rows_here // BLK
    half = width // 2
    own_heads = heads // 2
    pairs = own_heads // 2
    cols, wide = w_query.shape[1], w_inner.shape[1]
    units = wide * wshard // half
    sizes = dict(shards=wshard, rows=rows_here, chips=chips)

    small_least = 4 + devices // 8
    head_rows = -(-(3 * cols + 4) // 16) * 16
    vectors = (query_bias, value_bias, output_bias, outer_bias, gain_attn, shift_attn, gain_mlp, shift_mlp, inner_bias)
    head_piece = simple_call(
        functools.partial(pack_heads_kernel, shards=wshard),
        struct((head_rows, half)),
        (w_query, w_key, w_value) + tuple(v[None] for v in vectors),
        (where,),
        "pack_heads",
        (10**8, 10**6),
        scratch=[pltpu.VMEM((head_rows - 3 * cols, half), F32)],
    )
    inputs_low = tokens.astype(LOW)
    mine = jnp.concatenate([inputs_low] + [m.chip_shift(inputs_low, j) for j in range(1, chips)], axis=0)
    theirs = m.swap(mine)
    head_pieces = m.gather(head_piece, head_rows // 2 // 16 * 16)
    got = jnp.stack(head_pieces)
    passed = m.swap(got)
    query, key, value, head_weights, vec, bias_inner = simple_call(
        functools.partial(project_kernel, rows=rows_here, chips=chips, cols=cols, wide=wide),
        [struct((length, half))] * 3
        + [struct((2, 3, half, half)), struct((8, width), F32), struct((units, half), F32)],
        (got, passed, mine, theirs),
        (where,),
        "project",
        (2 * length * width * 3 * half, 12 << 20),
        scratch=[pltpu.VMEM((2, wshard, head_rows, half), LOW), pltpu.SemaphoreType.DMA((2, wshard))],
        anywhere=2,
        limit=40,
    )

    piece_one, piece_two = simple_call(
        functools.partial(pack_rest_kernel, shards=wshard),
        [struct((wide, half)), struct((5 * cols, half))],
        (w_inner, w_output, w_outer),
        (where,),
        "pack_rest",
        (10**9, 4 * 10**6),
    )
    piece_one, piece_two = after((piece_one, piece_two), head_pieces[-1])
    pieces_one = m.gather(piece_one, wide // 2)
    pieces_two = m.gather(piece_two, 5 * cols // 2 // 8 * 8)
    rest = []
    for pieces in (pieces_one, pieces_two):
        early, late = jnp.stack(pieces[:-3]), jnp.stack(pieces[-3:])
        rest += [early, late, m.swap(early), m.swap(late)]

    chip, core = where[wshard + 1], where[wshard]
    random_own = lax.dynamic_slice(
        random_blocks,
        (chip * count, core * own_heads, 0),
        (count, own_heads, random_blocks.shape[2]),
        allow_negative_indices=False,
    )
    index, active = slot_lists(chip * count, count, nblocks, glob, random_own, own_heads)
    seg_rep = seg_all.reshape(nblocks, BLK)
    seg_rep = jnp.concatenate([seg_rep, seg_rep], axis=1)
    seg_rep = jnp.concatenate([seg_rep, jnp.full((8, 2 * BLK), -1, jnp.int32)], axis=0)
    scalars = (index.reshape(-1), active.reshape(-1), glob, where)
    seg_args = (seg_all[:, None], seg_rep, seg_all[None, :])
    done = []
    for pair in range(pairs):
        at = min(1 + 2 * pair, len(pieces_one) - 1)
        turn = (pieces_one[at - 1], pieces_two[at - 1]) if pair else ()
        q = after(query, *turn) if turn else query
        done.append(attend(*scalars, q, key, value, *seg_args, count, own_heads, pair, wshard))
    attended_glob = jnp.concatenate([d[2] for d in done], axis=1)
    glob_rows = [attended_glob] + [m.chip_shift(attended_glob, j) for j in range(1, chips)]
    att_own, att_give = simple_call(
        functools.partial(merge_kernel, **sizes),
        [struct((rows_here, half))] * 2,
        tuple(d[0] for d in done) + tuple(glob_rows),
        (where, glob),
        "merge",
        (10**6, 2 << 20),
    )
    att_other = m.swap(att_give)

    big = lambda *shape: pltpu.VMEM(shape, F32)
    low = lambda *shape: pltpu.VMEM(shape, LOW)
    layer_output, resid_one, grad_own, grad_other, keep_one, give_one, keep_two, give_two, vec_grad, inner_bias_grad = (
        simple_call(
            dense_kernel,
            [struct((rows_here, width), F32)] * 2
            + [struct((rows_here, half))] * 2
            + [struct((wshard, wide, half))] * 2
            + [struct((wshard, 5 * cols, half))] * 2
            + [struct((8, width), F32), struct((units, half), F32)],
            tuple(rest) + (att_own, att_other, tokens, out_grad[0], vec, bias_inner),
            (where,),
            "dense",
            (32 * rows_here * width * width, 30 << 20),
            scratch=[
                low(2, wshard, wide, half),
                low(2, wshard, 5 * cols, half),
                low(rows_here, width),
                big(rows_here, width),
                big(rows_here, width),
                big(rows_here, 1),
                low(units, rows_here, half),
                big(units, rows_here, half),
                big(rows_here, width),
                low(rows_here, width),
                pltpu.SemaphoreType.DMA((2, 2, wshard)),
            ],
            anywhere=8,
            limit=60,
        )
    )

    from_other = m.swap(grad_other)
    given_two, given_one = m.swap(give_two), m.swap(give_one)
    heads_grad, *glob_sends = simple_call(
        functools.partial(spread_kernel, **sizes),
        [struct((2 * rows_here, half))] + [struct((BLK, half))] * chips,
        (grad_own, from_other),
        (where, glob),
        "spread",
        (10**6, 2 << 20),
    )
    glob_grads = [glob_sends[0]] + [m.chip_shift(glob_sends[j], j) for j in range(1, chips)]

    def ring_of(arrays, cut, base):
        def step(kind, slots, received):
            return ring_step(where, arrays, [base + s for s in slots], received, kind, cut)

        return m.scatter(step, cut)

    ring_one = ring_of([keep_one, given_one], wide // 2 // 16 * 16, m.sums)
    ring_two = ring_of([keep_two, given_two], 5 * cols // 2 // 16 * 16, m.sums)
    rings = (ring_two, ring_one)
    turn = ()
    pulled = []
    for pair in range(pairs):
        q = after(query, *turn) if turn else query
        pulled.append(
            pull(*scalars, q, key, value, heads_grad, glob_grads, done[pair][1], done[pair][3], own_heads, pair, wshard)
        )
        turn = tuple(next(ring) for ring in rings)
    grads = tuple(pulled[pair][t] for t in range(3) for pair in range(pairs))
    dense_cost = (2 * length * width * 3 * half, 12 << 20)
    small_rows = -(-(3 * cols + small_least) // 16) * 16 - 3 * cols
    lane = [i % 48 for i in range(half)]
    layout = jnp.asarray(
        [[i % heads if i < 3 * heads else -1 for i in lane], [i // heads for i in lane], [i // 48 for i in range(half)]],
        jnp.int32,
    )
    layout = jnp.concatenate([layout, jnp.zeros((5, half), jnp.int32)], axis=0)
    grads = after(grads, *turn)
    head_keep, head_give, small_parts = simple_call(
        functools.partial(weight_grad_kernel, pairs=pairs, cols=cols, wide=wide, devices=devices, **sizes),
        [struct((wshard // 2, 3 * cols, half))] * 2 + [struct((wshard, small_rows, half), F32)],
        grads + tuple(d[4] for d in done) + (mine, theirs, vec_grad, inner_bias_grad, layout),
        (where,),
        "weight_grad",
        dense_cost,
        scratch=[big(8, width)],
    )
    head_given = m.swap(head_give)
    turn = tuple(next(ring) for ring in rings)
    grads = after(grads, *turn)
    part_mine, part_theirs = simple_call(
        functools.partial(token_grad_kernel, pairs=pairs, **sizes),
        [struct((chips * rows_here, width))] * 2,
        grads + (head_weights,),
        (where,),
        "token_grad",
        dense_cost,
    )
    head_parts = jnp.concatenate([head_keep, head_given], axis=0)

    def head_step(kind, slots, received):
        return head_ring_step(where, head_parts, small_parts, m, slots, received, kind)

    *_, head_tail = m.scatter(head_step, None)
    rest_tail = []
    for ring in rings:
        *_, total = ring
        rest_tail.append(m.chip_sum(total))
    tail_two, tail_one = rest_tail
    grad_inner, grad_output, grad_outer = simple_call(
        functools.partial(finish_rest_kernel, shards=wshard),
        [struct(w_inner.shape, F32), struct(w_output.shape, F32), struct(w_outer.shape, F32)],
        (tail_one, m.swap(tail_one), tail_two, m.swap(tail_two)),
        (where,),
        "finish_rest",
        (10**9, 6 << 20),
    )
    head_tail = m.chip_sum(head_tail)
    vector = struct((1, cols), F32)
    finished = simple_call(
        functools.partial(finish_heads_kernel, shards=wshard, devices=devices, head_dim=head_dim),
        [struct(w_query.shape, F32)] * 3
        + [vector] * 8
        + [struct((1, wide), F32), struct((1, heads), F32), struct(w_query.shape, F32), struct(w_query.shape, F32)],
        (head_tail, m.swap(head_tail), thresholds[None], w_query, w_key),
        (where,),
        "finish_heads",
        (10**8, 3 << 20),
    )
    grad_query, grad_key, grad_value = finished[:3]
    vector_out = [v[0] for v in finished[3:11]]
    inner_out, maxima, clipped_query, clipped_key = finished[11][0], finished[12][0], finished[13], finished[14]

    summed = part_mine.astype(F32) + m.swap(part_theirs).astype(F32)
    summed = summed.reshape(chips, rows_here, width)
    input_grad = resid_one + summed[0]
    for j in range(1, chips):
        input_grad = input_grad + m.chip_shift(summed[j].astype(LOW), chips - j).astype(F32)
    return (
        layer_output[None],
        input_grad[None],
        grad_query,
        grad_key,
        grad_value,
        grad_output,
        grad_inner,
        grad_outer,
        vector_out[0],
        vector_out[1],
        vector_out[2],
        inner_out,
        vector_out[3],
        vector_out[4],
        vector_out[5],
        vector_out[6],
        vector_out[7],
        clipped_query,
        clipped_key,
        maxima,
    )


def head_ring_kernel(where, *refs, kind, targets, cut):
    refs = list(refs)
    parts = []
    for _ in range(targets):
        part, small = refs.pop(0), refs.pop(0)
        parts.append(jnp.concatenate([part[0].astype(F32), small[0]], axis=0))
    if kind == "first":
        up, down = refs
        up[...] = parts[0][:cut].astype(LOW)
        down[...] = parts[0][cut:].astype(LOW)
    elif kind == "second":
        above, below, up, down = refs
        up[:cut, :] = (parts[0][:cut] + above[...].astype(F32)).astype(LOW)
        up[cut:, :] = parts[0][cut:].astype(LOW)
        down[:cut, :] = parts[1][:cut].astype(LOW)
        down[cut:, :] = (parts[1][cut:] + below[...].astype(F32)).astype(LOW)
    elif kind == "later":
        above, below, up, down = refs
        up[...] = (parts[0] + above[...].astype(F32)).astype(LOW)
        down[...] = (parts[1] + below[...].astype(F32)).astype(LOW)
    else:
        above, below, out = refs
        out[...] = (parts[0] + above[...].astype(F32) + below[...].astype(F32)).astype(LOW)


def head_ring_step(where, parts, small, m, slots, received, kind):
    half = parts.shape[2]
    rows = parts.shape[1] + small.shape[1]
    cut = rows // 2 // 16 * 16
    specs, args = [], []
    for slot in slots:
        specs.append(
            pl.BlockSpec((1,) + parts.shape[1:], lambda i, where, at=m.placed + slot: (where[at], 0, 0))
        )
        specs.append(pl.BlockSpec((1,) + small.shape[1:], lambda i, where, at=m.sums + slot: (where[at], 0, 0)))
        args += [parts, small]
    specs += [pl.BlockSpec(a.shape, lambda i, where: (0, 0)) for a in received]
    shapes = [(rows, half)] if kind == "last" else [(rows, half)] * 2
    if kind == "first":
        shapes = [(cut, half), (rows - cut, half)]
    return pl.pallas_call(
        functools.partial(head_ring_kernel, kind=kind, targets=len(slots), cut=cut),
        grid_spec=pltpu.PrefetchScalarGridSpec(
            num_scalar_prefetch=1,
            grid=(1,),
            in_specs=specs,
            out_specs=[pl.BlockSpec(s, lambda i, where: (0, 0)) for s in shapes],
        ),
        out_shape=[struct(s) for s in shapes],
        compiler_params=pltpu.CompilerParams(vmem_limit_bytes=32 << 20),
        cost_estimate=pl.CostEstimate(flops=10**6, bytes_accessed=2 << 20, transcendentals=0),
        name="head_ring_" + kind,
    )(where, *args, *received)


def solution(mesh):
    tokens = P("wshard", "ctx", None)
    sequence = P("wshard", None)
    matrix = P(None, "wshard")
    vector = P("wshard")
    in_specs = (tokens, sequence, sequence, P(), P()) + (matrix,) * 6 + (vector,) * 9 + (tokens,)
    out_specs = (tokens, tokens) + (matrix,) * 6 + (vector,) * 9 + (matrix, matrix, P())
    return jax.shard_map(
        functools.partial(per_device, mesh.shape["ctx"], mesh.shape["wshard"]),
        mesh=mesh,
        in_specs=in_specs,
        out_specs=out_specs,
        check_vma=False,
    )
```

time: 482 us -> 367 us (0.76)
  Pallas kernels: 57.1 us -> 141 us
  matrix products: 69.8 us -> 0 us
  between operations: 48.7 us -> 3.51 us
  other arithmetic: 48 us -> 8.53 us
  local copies, waits for them, and re-layouts: 75.5 us -> 37 us
  starting transfers between devices: 107 us -> 86.8 us
  waiting for transfers between devices: 66.9 us -> 84.4 us
    pallas_call x2 -> x31, Pallas kernels: 57.1 us -> 141 us  [the longest x10 74.3 us: simple_call(): pl.pallas_call(kernel, in_specs=specs, out_specs=jax.tree.map(lambda _: v...]
    dot_general x21 -> x0, matrix products: 69.8 us -> none  [the longest x6 25.3 us: dot_nn(): lax.dot_general(left, right, (((1,), (0,)), ((), ())), preferred_element_...]
    dynamic_update_slice x38 -> x0, local copies, waits for them, and re-layouts: 33.5 us -> none  [the longest x35 31 us: put(): lax.dynamic_update_slice_in_dim(whole, part, self.shard_at(delta) * rows...]
    ppermute x32 -> x24, starting transfers between devices: 36.5 us -> 12.3 us  [up(): return lax.ppermute(value, 'wshard', self.up_perm)]
    ppermute x32 -> x24, waiting for transfers between devices: 37.3 us -> 13.2 us  [up(): return lax.ppermute(value, 'wshard', self.up_perm)]
    ppermute x32 -> x24, waiting for transfers between devices: 24.2 us -> 47.1 us  [down(): return lax.ppermute(value, 'wshard', self.down_perm)]
    unnamed x113 -> x168, local copies, waits for them, and re-layouts: 14.8 us -> 32.5 us
    dynamic_slice x15 -> x2, local copies, waits for them, and re-layouts: 10.3 us -> 0.78 us  [the longest x1 0.7 us: __init__(): lax.dynamic_slice(table, (here, 0), (1, table.shape[1]), allow_negative_i...]
  transfers between devices with their start and end apart: 94 -> 70, of which waited for: 27 -> 24; matrix products, arithmetic and copies ran while one was open for 31% -> 6% of each run, Pallas kernels for 12% -> 27%
where the time goes in v2:
time: 367 us; the launch traced here: 361 us
  Pallas kernels  141 us (38%)
  starting transfers between devices  86.8 us (24%)
  waiting for transfers between devices  84.4 us (23%)
  local copies, waits for them, and re-layouts  37 us (10%)
  other arithmetic  8.53 us (2%)
    pallas_call x10, Pallas kernels, simple_call(): pl.pallas_call(kernel, in_specs=specs, out_specs=jax.tree.map(lambda _: v...  74.3 us
    ppermute x24, waiting for transfers between devices, down(): return lax.ppermute(value, 'wshard', self.down_perm)  47.1 us
    ppermute x15, starting transfers between devices, swap(): return lax.ppermute(value, 'ctx', [(c, c ^ 1) for c in range(self.ctx)])  42.7 us
    unnamed x168, local copies, waits for them, and re-layouts  32.5 us
    pallas_call x3, Pallas kernels, pull(): pl.pallas_call(functools.partial(pull_kernel, heads=heads, pair=pair, sha...  29.5 us
    ppermute x24, starting transfers between devices, down(): return lax.ppermute(value, 'wshard', self.down_perm)  27.7 us
    pallas_call x3, Pallas kernels, attend(): pl.pallas_call(functools.partial(attend_kernel, heads=heads, pair=pair, s...  26.5 us
    ppermute x24, waiting for transfers between devices, up(): return lax.ppermute(value, 'wshard', self.up_perm)  13.2 us
  transfers between devices with their start and end apart: 70, of which 24 were waited for; matrix products, arithmetic and copies ran while one was open for 6% of the time, Pallas kernels for 27%

profile of v2, /device:TPU:1, one launch (start us, length us, event | category | flops | bytes accessed | tf_op | source)
XLA Modules:
  0.0 361.1 jit_solution(1893393624896131094)
XLA Ops:
  5.8 1.5 pack_heads.1
  7.3 2.1 collective-permute-start.4
  10.4 1.4 collective-permute-start.29
  17.2 1.7 copy.103.outer
  23.3 1.3 collective-permute-start.5
  26.8 2.5 collective-permute-done.5
  30.9 3.4 collective-permute-done.6
  34.3 1.3 collective-permute-start.7
  36.0 1.5 pad_maximum_fusion.mine.refs_12_
  37.4 4.5 %collective-permute-start.30 = (bf16[1024,768]{1,0:T(8,128)(2,1)S(1)}, bf16[1024,768]{1,0:T(8,128)(2,1)S(1)}, u32[]{:S(2)}, u32[]{:S(2)}) collective-permute-start(bf16[1024,768]{1,0:T(8,128)(2,1)S(1)} %pad_maximum_fusion.mine.refs_12_), channel_id=1, source_target_pairs={{0,8},{8,0},{16,24},{24,16},{1,9},{9,1},{17,25},{25,17},{2,10},{10... | collective-permute-start | bytes 4718600 | tf_op jit(solution)/shard_map/ppermute | solution.py:816
  45.1 3.0 collective-permute-done.9
  48.1 6.3 %collective-permute-start.28 = (bf16[8,304,384]{2,1,0:T(8,128)(2,1)S(1)}, bf16[8,304,384]{2,1,0:T(8,128)(2,1)S(1)}, u32[]{:S(2)}, u32[]{:S(2)}) collective-permute-start(bf16[8,304,384]{2,1,0:T(8,128)(2,1)S(1)} %bitcast_dynamic-update-slice_fusion.10.got), channel_id=1, source_target_pairs={{0,8},{8,0},{16,24},{24,16},{1,9},{9,1},{17,25},{25,17},{2,10},{10... | collective-permute-start | bytes 5603336 | tf_op jit(solution)/shard_map/ppermute | solution.py:816
  54.4 1.3 collective-permute-start.11
  57.3 2.3 collective-permute-start.20
  59.5 4.0 %collective-permute-done.11 = bf16[384,384]{1,0:T(8,128)(2,1)S(1)} collective-permute-done((bf16[384,384]{1,0:T(8,128)(2,1)S(1)}, bf16[384,384]{1,0:T(8,128)(2,1)S(1)}, u32[]{:S(2)}, u32[]{:S(2)}) %collective-permute-start.11) | collective-permute-done | bytes 294944 | tf_op jit(solution)/shard_map/ppermute | solution.py:813
  63.5 1.3 collective-permute-start.21
  64.9 1.4 collective-permute-start.13
  66.3 5.2 %collective-permute-done.21 = bf16[480,384]{1,0:T(8,128)(2,1)S(1)} collective-permute-done((bf16[480,384]{1,0:T(8,128)(2,1)S(1)}, bf16[480,384]{1,0:T(8,128)(2,1)S(1)}, u32[]{:S(2)}, u32[]{:S(2)}) %collective-permute-start.21) | collective-permute-done | bytes 368672 | tf_op jit(solution)/shard_map/ppermute | solution.py:813
  73.0 4.7 %collective-permute-done.13 = bf16[384,384]{1,0:T(8,128)(2,1)S(1)} collective-permute-done((bf16[384,384]{1,0:T(8,128)(2,1)S(1)}, bf16[384,384]{1,0:T(8,128)(2,1)S(1)}, u32[]{:S(2)}, u32[]{:S(2)}) %collective-permute-start.13) | collective-permute-done | bytes 294944 | tf_op jit(solution)/shard_map/ppermute | solution.py:813
  79.5 6.2 %collective-permute-done.23 = bf16[480,384]{1,0:T(8,128)(2,1)S(1)} collective-permute-done((bf16[480,384]{1,0:T(8,128)(2,1)S(1)}, bf16[480,384]{1,0:T(8,128)(2,1)S(1)}, u32[]{:S(2)}, u32[]{:S(2)}) %collective-permute-start.23) | collective-permute-done | bytes 368672 | tf_op jit(solution)/shard_map/ppermute | solution.py:813
  86.5 1.7 collective-permute-done.22
  88.2 5.2 %collective-permute-start.16 = (bf16[5,384,384]{2,1,0:T(8,128)(2,1)S(1)}, bf16[5,384,384]{2,1,0:T(8,128)(2,1)}, u32[]{:S(2)}, u32[]{:S(2)}) collective-permute-start(bf16[5,384,384]{2,1,0:T(8,128)(2,1)S(1)} %bitcast_dynamic-update-slice_fusion.5.one_a), channel_id=1, source_target_pairs={{0,8},{8,0},{16,24},{24,16},{1,9},{9,1},{17,25},{25,17},{2,10},{10... | collective-permute-start | bytes 4423688 | tf_op jit(solution)/shard_map/ppermute | solution.py:816
  95.3 4.4 %collective-permute-done.25 = bf16[240,384]{1,0:T(8,128)(2,1)S(1)} collective-permute-done((bf16[240,384]{1,0:T(8,128)(2,1)S(1)}, bf16[240,384]{1,0:T(8,128)(2,1)S(1)}, u32[]{:S(2)}, u32[]{:S(2)}) %collective-permute-start.25) | collective-permute-done | bytes 184352 | tf_op jit(solution)/shard_map/ppermute | solution.py:813
  100.5 1.3 collective-permute-start.17
  102.2 11.6 %project.1 = (bf16[2048,384]{1,0:T(8,128)(2,1)S(1)}, bf16[2048,384]{1,0:T(8,128)(2,1)S(1)}, bf16[2048,384]{1,0:T(8,128)(2,1)S(1)}, bf16[2,3,384,384]{3,2,1,0:T(8...) custom-call(s32[28]{0:T(128)S(1)} %get-tuple-element.337.where, ...), custom_call_target="tpu_custom_call" | custom-call | flops 3623878656 | bytes 12582912 | tf_op jit(solution)/shard_map/project/pallas_call | solution.py:359
  113.8 8.9 %attend.3 = (bf16[1024,128]{1,0:T(8,128)(2,1)S(1)}, bf16[16,128,512]{2,1,0:T(8,128)(2,1)S(1)}, bf16[64,128]{1,0:T(8,128)(2,1)S(1)}, bf16[128,2048]{1,0:T(8,128)(2,1)S(1)}, f32[128,128]{1,0:T(8,128)S(1)}) custom-call(s32[768]{0:T(1024)S(1)} %reshape.156.index, s32[768]{0:T(1024)S(1)} %broadcast_select_fusion.active, s32[2]{0:T(128)S(1)} %bitcast.76, ...), custom_call_target="tpu_custom_call" | custom-call | flops 10737418240 | bytes 6291456 | tf_op jit(solution)/shard_map/attend/pallas_call | solution.py:293
  122.7 1.3 copy-done.46
  124.9 8.8 %attend.4 = (bf16[1024,128]{1,0:T(8,128)(2,1)S(1)}, bf16[16,128,512]{2,1,0:T(8,128)(2,1)S(1)}, bf16[64,128]{1,0:T(8,128)(2,1)S(1)}, bf16[128,2048]{1,0:T(8,128)(2,1)S(1)}, f32[128,128]{1,0:T(8,128)S(1)}) custom-call(s32[768]{0:T(1024)S(1)} %reshape.156.index, s32[768]{0:T(1024)S(1)} %broadcast_select_fusion.active, s32[2]{0:T(128)S(1)} %bitcast.77, ...), custom_call_target="tpu_custom_call" | custom-call | flops 10737418240 | bytes 6291456 | tf_op jit(solution)/shard_map/attend/pallas_call | solution.py:293
  134.4 1.3 copy-done.44
  135.7 8.8 %attend.5 = (bf16[1024,128]{1,0:T(8,128)(2,1)S(1)}, bf16[16,128,512]{2,1,0:T(8,128)(2,1)S(1)}, bf16[64,128]{1,0:T(8,128)(2,1)S(1)}, bf16[128,2048]{1,0:T(8,128)(2,1)S(1)}, f32[128,128]{1,0:T(8,128)S(1)}) custom-call(s32[768]{0:T(1024)S(1)} %reshape.156.index, s32[768]{0:T(1024)S(1)} %broadcast_select_fusion.active, s32[2]{0:T(128)S(1)} %bitcast.78, ...), custom_call_target="tpu_custom_call" | custom-call | flops 10737418240 | bytes 6291456 | tf_op jit(solution)/shard_map/attend/pallas_call | solution.py:293
  144.6 1.3 copy-done.42
  146.2 2.7 collective-permute-done.31.refs_4_
  150.8 1.6 collective-permute-start.32
  152.5 1.3 collective-permute-done.32.att_other
  155.2 41.8 %dense.1 = (f32[512,768]{1,0:T(8,128)}, f32[512,768]{1,0:T(8,128)}, bf16[512,384]{1,0:T(8,128)(2,1)}, bf16[512,384]{1,0:T(8,128)(2,1)}, bf16[8,384,384]{2,1,0:T(...) custom-call(s32[28]{0:T(128)} %copy-done.7, ...), custom_call_target="tpu_custom_call" | custom-call | flops 9663676416 | bytes 31457280 | tf_op jit(solution)/shard_map/dense/pallas_call | solution.py:359
  198.0 8.1 %collective-permute-done.36.refs_1_.refs_3_ = bf16[8,384,384]{2,1,0:T(8,128)(2,1)S(1)} collective-permute-done((bf16[8,384,384]{2,1,0:T(8,128)(2,1)}, bf16[8,384,384]{2,1,0:T(8,128)(2,1)S(1)}, u32[]{:S(2)}, u32[]{:S(2)}) %collective-permute-start.36) | collective-permute-done | bytes 2359328 | tf_op jit(solution)/shard_map/ppermute | solution.py:816
  206.1 1.7 copy-done.3
  208.4 1.3 collective-permute-start.40
  210.9 2.7 collective-permute-done.40.refs_5_
  215.2 1.4 collective-permute-start.44
  217.4 1.4 collective-permute-start.38
  219.2 9.8 %pull.3 = (bf16[2048,128]{1,0:T(8,128)(2,1)S(1)}, bf16[2048,128]{1,0:T(8,128)(2,1)S(1)}, bf16[2048,128]{1,0:T(8,128)(2,1)S(1)}) custom-call(s32[768]{0:T(1024)S(1)} %reshape.156.index, s32[768]{0:T(1024)S(1)} %broadcast_select_fusion.active, s32[2]{0:T(128)S(1)} %bitcast.81, s32[28]{0:T(128)S(1)} %copy-done.8, bf16[2048,384]{1,0:T(8,128)(2,1)S(1)} %copy-done.28, ...), custom_call_target="tpu_custom_call" | custom-call | flops 10737418240 | bytes 8388608 | tf_op jit(solution)/shard_map/pull/pallas_call | solution.py:334
  229.8 1.4 collective-permute-start.48
  232.1 1.4 collective-permute-start.42
  233.6 9.8 %pull.4 = (bf16[2048,128]{1,0:T(8,128)(2,1)S(1)}, bf16[2048,128]{1,0:T(8,128)(2,1)S(1)}, bf16[2048,128]{1,0:T(8,128)(2,1)S(1)}) custom-call(s32[768]{0:T(1024)S(1)} %reshape.156.index, s32[768]{0:T(1024)S(1)} %broadcast_select_fusion.active, s32[2]{0:T(128)S(1)} %bitcast.82, s32[28]{0:T(128)S(1)} %copy-done.8, bf16[2048,384]{1,0:T(8,128)(2,1)S(1)} %copy-done.28, ...), custom_call_target="tpu_custom_call" | custom-call | flops 10737418240 | bytes 8388608 | tf_op jit(solution)/shard_map/pull/pallas_call | solution.py:334
  247.4 10.0 %pull.5 = (bf16[2048,128]{1,0:T(8,128)(2,1)S(1)}, bf16[2048,128]{1,0:T(8,128)(2,1)S(1)}, bf16[2048,128]{1,0:T(8,128)(2,1)S(1)}) custom-call(s32[768]{0:T(1024)S(1)} %reshape.156.index, s32[768]{0:T(1024)S(1)} %broadcast_select_fusion.active, s32[2]{0:T(128)S(1)} %bitcast.83, s32[28]{0:T(128)S(1)} %copy-done.8, bf16[2048,384]{1,0:T(8,128)(2,1)S(1)} %copy-done.28, ...), custom_call_target="tpu_custom_call" | custom-call | flops 10737418240 | bytes 8388608 | tf_op jit(solution)/shard_map/pull/pallas_call | solution.py:334
  261.0 5.7 %weight_grad.1 = (bf16[4,288,384]{2,1,0:T(8,128)(2,1)S(1)}, bf16[4,288,384]{2,1,0:T(8,128)(2,1)S(1)}, f32[8,16,384]{2,1,0:T(8,128)S(1)}) custom-call(s32[28]{0:T(128)S(1)} %copy-done.8, bf16[2048,128]{1,0:T(8,128)(2,1)S(1)} %get-tuple-element.208.refs_0_, bf16[2048,128]{1,0:T(8,128)(2,1)S(1)} %get-tuple-element.209.refs_1_, ...), custom_call_target="tpu_custom_call" | custom-call | flops 3623878656 | bytes 12582912 | tf_op jit(solution)/shard_map/weight_grad/pallas_call | solution.py:359
  266.7 4.2 %collective-permute-start.51 = (bf16[4,288,384]{2,1,0:T(8,128)(2,1)S(1)}, bf16[4,288,384]{2,1,0:T(8,128)(2,1)S(1)}, u32[]{:S(2)}, u32[]{:S(2)}) collective-permute-start(bf16[4,288,384]{2,1,0:T(8,128)(2,1)S(1)} %get-tuple-element.226), channel_id=1, source_target_pairs={{0,8},{8,0},{16,24},{24,16},{1,9},{9,1},{17,25},{25,17},{2,10},{10... | collective-permute-start | bytes 2654216 | tf_op jit(solution)/shard_map/ppermute | solution.py:816
  271.8 6.5 %token_grad.1 = (bf16[1024,768]{1,0:T(8,128)(2,1)S(1)}, bf16[1024,768]{1,0:T(8,128)(2,1)S(1)}) custom-call(s32[28]{0:T(128)S(1)} %copy-done.8, bf16[2048,128]{1,0:T(8,128)(2,1)S(1)} %get-tuple-element.208.refs_0_, bf16[2048,128]{1,0:T(8,128)(2,1)S(1)} %get-tuple-element.209.refs_1_, bf16[2048,128]{1,0:T(8,128)(2,1)S(1)} %get-tuple-element.210.refs_2_, ...), custom_call_target="tpu_custom_call" | custom-call | flops 3623878656 | bytes 12582912 | tf_op jit(solution)/shard_map/token_grad/pallas_call | solution.py:359
  281.4 3.5 collective-permute-done.52.refs_4_
  288.6 3.1 collective-permute-done.54.refs_4_
  293.8 4.7 %collective-permute-done.63.refs_3_ = bf16[384,384]{1,0:T(8,128)(2,1)S(1)} collective-permute-done((bf16[384,384]{1,0:T(8,128)(2,1)S(1)}, bf16[384,384]{1,0:T(8,128)(2,1)S(1)}, u32[]{:S(2)}, u32[]{:S(2)}) %collective-permute-start.63) | collective-permute-done | bytes 294944 | tf_op jit(solution)/shard_map/ppermute | solution.py:813
  298.7 1.3 collective-permute-start.57
  300.7 5.7 %collective-permute-done.67.refs_3_ = bf16[480,384]{1,0:T(8,128)(2,1)S(1)} collective-permute-done((bf16[480,384]{1,0:T(8,128)(2,1)S(1)}, bf16[480,384]{1,0:T(8,128)(2,1)S(1)}, u32[]{:S(2)}, u32[]{:S(2)}) %collective-permute-start.67) | collective-permute-done | bytes 368672 | tf_op jit(solution)/shard_map/ppermute | solution.py:813
  308.7 2.2 collective-permute-done.56.refs_4_
  312.4 1.4 collective-permute-start.59
  315.6 5.2 %collective-permute-start.65 = (bf16[384,384]{1,0:T(8,128)(2,1)S(1)}, bf16[384,384]{1,0:T(8,128)(2,1)S(1)}, u32[]{:S(2)}, u32[]{:S(2)}) collective-permute-start(bf16[384,384]{1,0:T(8,128)(2,1)S(1)} %add_convert_fusion.1.own_one), channel_id=1, source_target_pairs={{0,8},{8,0},{16,24},{24,16},{1,9},{9,1},{17,25},{25,17},{2,10},{10... | collective-permute-start | bytes 884744 | tf_op jit(solution)/shard_map/ppermute | solution.py:816
  321.8 6.9 %collective-permute-start.69 = (bf16[480,384]{1,0:T(8,128)(2,1)S(1)}, bf16[480,384]{1,0:T(8,128)(2,1)S(1)}, u32[]{:S(2)}, u32[]{:S(2)}) collective-permute-start(bf16[480,384]{1,0:T(8,128)(2,1)S(1)} %add_convert_fusion.own_two), channel_id=1, source_target_pairs={{0,8},{8,0},{16,24},{24,16},{1,9},{9,1},{17,25},{25,17},{2,10},{10... | collective-permute-start | bytes 1105928 | tf_op jit(solution)/shard_map/ppermute | solution.py:816
  328.7 11.9 %collective-permute-done.60 = bf16[304,384]{1,0:T(8,128)(2,1)S(1)} collective-permute-done((bf16[304,384]{1,0:T(8,128)(2,1)S(1)}, bf16[304,384]{1,0:T(8,128)(2,1)S(1)}, u32[]{:S(2)}, u32[]{:S(2)}) %collective-permute-start.60) | collective-permute-done | bytes 233504 | tf_op jit(solution)/shard_map/ppermute | solution.py:822
  340.6 5.1 %collective-permute-start.61 = (bf16[304,384]{1,0:T(8,128)(2,1)S(1)}, bf16[304,384]{1,0:T(8,128)(2,1)S(1)}, u32[]{:S(2)}, u32[]{:S(2)}) collective-permute-start(bf16[304,384]{1,0:T(8,128)(2,1)S(1)} %add_convert_fusion.2.own), channel_id=1, source_target_pairs={{0,8},{8,0},{16,24},{24,16},{1,9},{9,1},{17,25},{25,17},{2,10},{10... | collective-permute-start | bytes 700424 | tf_op jit(solution)/shard_map/ppermute | solution.py:816
  345.8 2.6 finish_rest.1
  349.3 1.5 copy.118
  350.7 1.7 finish_heads.1
  357.4 3.5 fusion.1
  (328 shorter events, 73.2 us)
Async XLA Ops:
  7.3 16.0 %collective-permute-start.4 = (bf16[304,384]{1,0:T(8,128)(2,1)}, bf16[304,384]{1,0:T(8,128)(2,1)}, u32[]{:S(2)}, u32[]{:S(2)}) collective-permute-start(bf16[304,384]{1,0:T(8,128)(2,1)} %pack_heads.1), channel_id=1, source_target_pairs={{2,0},{4,2},{6,4},{7,6},{5,7},{3,5},{1,3},{0,1},{10,8},{12,10},{14... | collective-permute-start | bytes 700424 | tf_op jit(solution)/shard_map/ppermute | solution.py:813
  9.3 15.2 %collective-permute-start = (bf16[304,384]{1,0:T(8,128)(2,1)}, bf16[304,384]{1,0:T(8,128)(2,1)}, u32[]{:S(2)}, u32[]{:S(2)}) collective-permute-start(bf16[304,384]{1,0:T(8,128)(2,1)} %pack_heads.1), channel_id=1, source_target_pairs={{0,2},{2,4},{4,6},{6,7},{7,5},{5,3},{3,1},{1,0},{8,10},{10,12},{12... | collective-permute-start | bytes 700424 | tf_op jit(solution)/shard_map/ppermute | solution.py:810
  10.4 25.6 %collective-permute-start.29 = (bf16[512,768]{1,0:T(8,128)(2,1)}, bf16[512,768]{1,0:T(8,128)(2,1)}, u32[]{:S(2)}, u32[]{:S(2)}) collective-permute-start(bf16[512,768]{1,0:T(8,128)(2,1)} %bitcast_convert_fusion), channel_id=1, source_target_pairs={{0,16},{8,24},{16,0},{24,8},{1,17},{9,25},{17,1},{25,9},{2,18},{10... | collective-permute-start | bytes 2359304 | tf_op jit(solution)/shard_map/ppermute | solution.py:819
  23.3 6.0 %collective-permute-start.5 = (bf16[304,384]{1,0:T(8,128)(2,1)}, bf16[304,384]{1,0:T(8,128)(2,1)S(1)}, u32[]{:S(2)}, u32[]{:S(2)}) collective-permute-start(bf16[304,384]{1,0:T(8,128)(2,1)} %collective-permute-done.4), channel_id=1, source_target_pairs={{2,0},{4,2},{6,4},{7,6},{5,7},{3,5},{1,3},{0,1},{10,8},{12,10},{14... | collective-permute-start | bytes 700424 | tf_op jit(solution)/shard_map/ppermute | solution.py:813
  24.6 6.0 %collective-permute-start.1 = (bf16[304,384]{1,0:T(8,128)(2,1)}, bf16[304,384]{1,0:T(8,128)(2,1)S(1)}, u32[]{:S(2)}, u32[]{:S(2)}) collective-permute-start(bf16[304,384]{1,0:T(8,128)(2,1)} %collective-permute-done), channel_id=1, source_target_pairs={{0,2},{2,4},{4,6},{6,7},{7,5},{5,3},{3,1},{1,0},{8,10},{10,12},{12... | collective-permute-start | bytes 700424 | tf_op jit(solution)/shard_map/ppermute | solution.py:810
  30.6 5.2 %collective-permute-start.2 = (bf16[304,384]{1,0:T(8,128)(2,1)S(1)}, bf16[304,384]{1,0:T(8,128)(2,1)S(1)}, u32[]{:S(2)}, u32[]{:S(2)}) collective-permute-start(bf16[304,384]{1,0:T(8,128)(2,1)S(1)} %collective-permute-done.1), channel_id=1, source_target_pairs={{0,2},{2,4},{4,6},{6,7},{7,5},{5,3},{3,1},{1,0},{8,10},{10,12},{12... | collective-permute-start | bytes 700424 | tf_op jit(solution)/shard_map/ppermute | solution.py:810
  34.3 7.7 %collective-permute-start.7 = (bf16[160,384]{1,0:T(8,128)(2,1)S(1)}, bf16[160,384]{1,0:T(8,128)(2,1)S(1)}, u32[]{:S(2)}, u32[]{:S(2)}) collective-permute-start(bf16[160,384]{1,0:T(8,128)(2,1)S(1)} %slice.50), channel_id=1, source_target_pairs={{2,0},{4,2},{6,4},{7,6},{5,7},{3,5},{1,3},{0,1},{10,8},{12,10},{14... | collective-permute-start | bytes 368648 | tf_op jit(solution)/shard_map/ppermute | solution.py:813
  35.8 6.1 %collective-permute-start.3 = (bf16[144,384]{1,0:T(8,128)(2,1)S(1)}, bf16[144,384]{1,0:T(8,128)(2,1)S(1)}, u32[]{:S(2)}, u32[]{:S(2)}) collective-permute-start(bf16[144,384]{1,0:T(8,128)(2,1)S(1)} %slice.49), channel_id=1, source_target_pairs={{0,2},{2,4},{4,6},{6,7},{7,5},{5,3},{3,1},{1,0},{8,10},{10,12},{12... | collective-permute-start | bytes 331784 | tf_op jit(solution)/shard_map/ppermute | solution.py:810
  37.4 64.6 %collective-permute-start.30 = (bf16[1024,768]{1,0:T(8,128)(2,1)S(1)}, bf16[1024,768]{1,0:T(8,128)(2,1)S(1)}, u32[]{:S(2)}, u32[]{:S(2)}) collective-permute-start(bf16[1024,768]{1,0:T(8,128)(2,1)S(1)} %pad_maximum_fusion.mine.refs_12_), channel_id=1, source_target_pairs={{0,8},{8,0},{16,24},{24,16},{1,9},{9,1},{17,25},{25,17},{2,10},{10... | collective-permute-start | bytes 4718600 | tf_op jit(solution)/shard_map/ppermute | solution.py:816
  42.0 6.1 %collective-permute-start.9 = (bf16[384,384]{1,0:T(8,128)(2,1)S(1)}, bf16[384,384]{1,0:T(8,128)(2,1)S(1)}, u32[]{:S(2)}, u32[]{:S(2)}) collective-permute-start(bf16[384,384]{1,0:T(8,128)(2,1)S(1)} %get-tuple-element.140), channel_id=1, source_target_pairs={{2,0},{4,2},{6,4},{7,6},{5,7},{3,5},{1,3},{0,1},{10,8},{12,10},{14... | collective-permute-start | bytes 884744 | tf_op jit(solution)/shard_map/ppermute | solution.py:813
  43.1 11.3 %collective-permute-start.8 = (bf16[384,384]{1,0:T(8,128)(2,1)S(1)}, bf16[384,384]{1,0:T(8,128)(2,1)S(1)}, u32[]{:S(2)}, u32[]{:S(2)}) collective-permute-start(bf16[384,384]{1,0:T(8,128)(2,1)S(1)} %get-tuple-element.140), channel_id=1, source_target_pairs={{0,2},{2,4},{4,6},{6,7},{7,5},{5,3},{3,1},{1,0},{8,10},{10,12},{12... | collective-permute-start | bytes 884744 | tf_op jit(solution)/shard_map/ppermute | solution.py:810
  43.5 13.8 %collective-permute-start.19 = (bf16[480,384]{1,0:T(8,128)(2,1)S(1)}, bf16[480,384]{1,0:T(8,128)(2,1)S(1)}, u32[]{:S(2)}, u32[]{:S(2)}) collective-permute-start(bf16[480,384]{1,0:T(8,128)(2,1)S(1)} %get-tuple-element.141), channel_id=1, source_target_pairs={{2,0},{4,2},{6,4},{7,6},{5,7},{3,5},{1,3},{0,1},{10,8},{12,10},{14... | collective-permute-start | bytes 1105928 | tf_op jit(solution)/shard_map/ppermute | solution.py:813
  44.6 12.0 %collective-permute-start.18 = (bf16[480,384]{1,0:T(8,128)(2,1)S(1)}, bf16[480,384]{1,0:T(8,128)(2,1)S(1)}, u32[]{:S(2)}, u32[]{:S(2)}) collective-permute-start(bf16[480,384]{1,0:T(8,128)(2,1)S(1)} %get-tuple-element.141), channel_id=1, source_target_pairs={{0,2},{2,4},{4,6},{6,7},{7,5},{5,3},{3,1},{1,0},{8,10},{10,12},{12... | collective-permute-start | bytes 1105928 | tf_op jit(solution)/shard_map/ppermute | solution.py:810
  48.1 54.1 %collective-permute-start.28 = (bf16[8,304,384]{2,1,0:T(8,128)(2,1)S(1)}, bf16[8,304,384]{2,1,0:T(8,128)(2,1)S(1)}, u32[]{:S(2)}, u32[]{:S(2)}) collective-permute-start(bf16[8,304,384]{2,1,0:T(8,128)(2,1)S(1)} %bitcast_dynamic-update-slice_fusion.10.got), channel_id=1, source_target_pairs={{0,8},{8,0},{16,24},{24,16},{1,9},{9,1},{17,25},{25,17},{2,10},{10... | collective-permute-start | bytes 5603336 | tf_op jit(solution)/shard_map/ppermute | solution.py:816
  54.4 9.1 %collective-permute-start.11 = (bf16[384,384]{1,0:T(8,128)(2,1)S(1)}, bf16[384,384]{1,0:T(8,128)(2,1)S(1)}, u32[]{:S(2)}, u32[]{:S(2)}) collective-permute-start(bf16[384,384]{1,0:T(8,128)(2,1)S(1)} %collective-permute-done.9), channel_id=1, source_target_pairs={{2,0},{4,2},{6,4},{7,6},{5,7},{3,5},{1,3},{0,1},{10,8},{12,10},{14... | collective-permute-start | bytes 884744 | tf_op jit(solution)/shard_map/ppermute | solution.py:813
  56.6 8.3 %collective-permute-start.10 = (bf16[384,384]{1,0:T(8,128)(2,1)S(1)}, bf16[384,384]{1,0:T(8,128)(2,1)S(1)}, u32[]{:S(2)}, u32[]{:S(2)}) collective-permute-start(bf16[384,384]{1,0:T(8,128)(2,1)S(1)} %collective-permute-done.8), channel_id=1, source_target_pairs={{0,2},{2,4},{4,6},{6,7},{7,5},{5,3},{3,1},{1,0},{8,10},{10,12},{12... | collective-permute-start | bytes 884744 | tf_op jit(solution)/shard_map/ppermute | solution.py:810
  57.3 14.9 %collective-permute-start.20 = (bf16[480,384]{1,0:T(8,128)(2,1)S(1)}, bf16[480,384]{1,0:T(8,128)(2,1)S(1)}, u32[]{:S(2)}, u32[]{:S(2)}) collective-permute-start(bf16[480,384]{1,0:T(8,128)(2,1)S(1)} %collective-permute-done.18), channel_id=1, source_target_pairs={{0,2},{2,4},{4,6},{6,7},{7,5},{5,3},{3,1},{1,0},{8,10},{10,12},{12... | collective-permute-start | bytes 1105928 | tf_op jit(solution)/shard_map/ppermute | solution.py:810
  63.5 7.9 %collective-permute-start.21 = (bf16[480,384]{1,0:T(8,128)(2,1)S(1)}, bf16[480,384]{1,0:T(8,128)(2,1)S(1)}, u32[]{:S(2)}, u32[]{:S(2)}) collective-permute-start(bf16[480,384]{1,0:T(8,128)(2,1)S(1)} %collective-permute-done.19), channel_id=1, source_target_pairs={{2,0},{4,2},{6,4},{7,6},{5,7},{3,5},{1,3},{0,1},{10,8},{12,10},{14... | collective-permute-start | bytes 1105928 | tf_op jit(solution)/shard_map/ppermute | solution.py:813
  64.9 12.9 %collective-permute-start.13 = (bf16[384,384]{1,0:T(8,128)(2,1)S(1)}, bf16[384,384]{1,0:T(8,128)(2,1)S(1)}, u32[]{:S(2)}, u32[]{:S(2)}) collective-permute-start(bf16[384,384]{1,0:T(8,128)(2,1)S(1)} %collective-permute-done.11), channel_id=1, source_target_pairs={{2,0},{4,2},{6,4},{7,6},{5,7},{3,5},{1,3},{0,1},{10,8},{12,10},{14... | collective-permute-start | bytes 884744 | tf_op jit(solution)/shard_map/ppermute | solution.py:813
  71.5 7.1 %collective-permute-start.12 = (bf16[384,384]{1,0:T(8,128)(2,1)S(1)}, bf16[384,384]{1,0:T(8,128)(2,1)S(1)}, u32[]{:S(2)}, u32[]{:S(2)}) collective-permute-start(bf16[384,384]{1,0:T(8,128)(2,1)S(1)} %collective-permute-done.10), channel_id=1, source_target_pairs={{0,2},{2,4},{4,6},{6,7},{7,5},{5,3},{3,1},{1,0},{8,10},{10,12},{12... | collective-permute-start | bytes 884744 | tf_op jit(solution)/shard_map/ppermute | solution.py:810
  72.2 13.5 %collective-permute-start.23 = (bf16[480,384]{1,0:T(8,128)(2,1)S(1)}, bf16[480,384]{1,0:T(8,128)(2,1)S(1)}, u32[]{:S(2)}, u32[]{:S(2)}) collective-permute-start(bf16[480,384]{1,0:T(8,128)(2,1)S(1)} %collective-permute-done.21), channel_id=1, source_target_pairs={{2,0},{4,2},{6,4},{7,6},{5,7},{3,5},{1,3},{0,1},{10,8},{12,10},{14... | collective-permute-start | bytes 1105928 | tf_op jit(solution)/shard_map/ppermute | solution.py:813
  77.8 10.4 %collective-permute-start.22 = (bf16[480,384]{1,0:T(8,128)(2,1)S(1)}, bf16[480,384]{1,0:T(8,128)(2,1)S(1)}, u32[]{:S(2)}, u32[]{:S(2)}) collective-permute-start(bf16[480,384]{1,0:T(8,128)(2,1)S(1)} %collective-permute-done.20), channel_id=1, source_target_pairs={{0,2},{2,4},{4,6},{6,7},{7,5},{5,3},{3,1},{1,0},{8,10},{10,12},{12... | collective-permute-start | bytes 1105928 | tf_op jit(solution)/shard_map/ppermute | solution.py:810
  78.6 14.8 %collective-permute-start.15 = (bf16[192,384]{1,0:T(8,128)(2,1)S(1)}, bf16[192,384]{1,0:T(8,128)(2,1)S(1)}, u32[]{:S(2)}, u32[]{:S(2)}) collective-permute-start(bf16[192,384]{1,0:T(8,128)(2,1)S(1)} %slice.52), channel_id=1, source_target_pairs={{2,0},{4,2},{6,4},{7,6},{5,7},{3,5},{1,3},{0,1},{10,8},{12,10},{14... | collective-permute-start | bytes 442376 | tf_op jit(solution)/shard_map/ppermute | solution.py:813
  85.7 8.9 %collective-permute-start.14 = (bf16[192,384]{1,0:T(8,128)(2,1)S(1)}, bf16[192,384]{1,0:T(8,128)(2,1)S(1)}, u32[]{:S(2)}, u32[]{:S(2)}) collective-permute-start(bf16[192,384]{1,0:T(8,128)(2,1)S(1)} %slice.51), channel_id=1, source_target_pairs={{0,2},{2,4},{4,6},{6,7},{7,5},{5,3},{3,1},{1,0},{8,10},{10,12},{12... | collective-permute-start | bytes 442376 | tf_op jit(solution)/shard_map/ppermute | solution.py:810
  88.2 64.3 %collective-permute-start.16 = (bf16[5,384,384]{2,1,0:T(8,128)(2,1)S(1)}, bf16[5,384,384]{2,1,0:T(8,128)(2,1)}, u32[]{:S(2)}, u32[]{:S(2)}) collective-permute-start(bf16[5,384,384]{2,1,0:T(8,128)(2,1)S(1)} %bitcast_dynamic-update-slice_fusion.5.one_a), channel_id=1, source_target_pairs={{0,8},{8,0},{16,24},{24,16},{1,9},{9,1},{17,25},{25,17},{2,10},{10... | collective-permute-start | bytes 4423688 | tf_op jit(solution)/shard_map/ppermute | solution.py:816
  93.4 6.3 %collective-permute-start.25 = (bf16[240,384]{1,0:T(8,128)(2,1)S(1)}, bf16[240,384]{1,0:T(8,128)(2,1)S(1)}, u32[]{:S(2)}, u32[]{:S(2)}) collective-permute-start(bf16[240,384]{1,0:T(8,128)(2,1)S(1)} %slice.54), channel_id=1, source_target_pairs={{2,0},{4,2},{6,4},{7,6},{5,7},{3,5},{1,3},{0,1},{10,8},{12,10},{14... | collective-permute-start | bytes 552968 | tf_op jit(solution)/shard_map/ppermute | solution.py:813
  94.6 6.0 %collective-permute-start.24 = (bf16[240,384]{1,0:T(8,128)(2,1)S(1)}, bf16[240,384]{1,0:T(8,128)(2,1)S(1)}, u32[]{:S(2)}, u32[]{:S(2)}) collective-permute-start(bf16[240,384]{1,0:T(8,128)(2,1)S(1)} %slice.53), channel_id=1, source_target_pairs={{0,2},{2,4},{4,6},{6,7},{7,5},{5,3},{3,1},{1,0},{8,10},{10,12},{12... | collective-permute-start | bytes 552968 | tf_op jit(solution)/shard_map/ppermute | solution.py:810
  99.8 54.1 %collective-permute-start.26 = (bf16[5,480,384]{2,1,0:T(8,128)(2,1)S(1)}, bf16[5,480,384]{2,1,0:T(8,128)(2,1)S(1)}, u32[]{:S(2)}, u32[]{:S(2)}) collective-permute-start(bf16[5,480,384]{2,1,0:T(8,128)(2,1)S(1)} %bitcast_dynamic-update-slice_fusion.two_a), channel_id=1, source_target_pairs={{0,8},{8,0},{16,24},{24,16},{1,9},{9,1},{17,25},{25,17},{2,10},{10... | collective-permute-start | bytes 5529608 | tf_op jit(solution)/shard_map/ppermute | solution.py:816
  100.5 51.9 %collective-permute-start.17 = (bf16[3,384,384]{2,1,0:T(8,128)(2,1)S(1)}, bf16[3,384,384]{2,1,0:T(8,128)(2,1)S(1)}, u32[]{:S(2)}, u32[]{:S(2)}) collective-permute-start(bf16[3,384,384]{2,1,0:T(8,128)(2,1)S(1)} %pad_maximum_fusion.2.one_b), channel_id=1, source_target_pairs={{0,8},{8,0},{16,24},{24,16},{1,9},{9,1},{17,25},{25,17},{2,10},{10... | collective-permute-start | bytes 2654216 | tf_op jit(solution)/shard_map/ppermute | solution.py:816
  102.1 51.8 %collective-permute-start.27 = (bf16[3,480,384]{2,1,0:T(8,128)(2,1)S(1)}, bf16[3,480,384]{2,1,0:T(8,128)(2,1)}, u32[]{:S(2)}, u32[]{:S(2)}) collective-permute-start(bf16[3,480,384]{2,1,0:T(8,128)(2,1)S(1)} %pad_maximum_fusion.1.two_b), channel_id=1, source_target_pairs={{0,8},{8,0},{16,24},{24,16},{1,9},{9,1},{17,25},{25,17},{2,10},{10... | collective-permute-start | bytes 3317768 | tf_op jit(solution)/shard_map/ppermute | solution.py:816
  197.0 19.7 %collective-permute-start.35 = (bf16[8,480,384]{2,1,0:T(8,128)(2,1)}, bf16[8,480,384]{2,1,0:T(8,128)(2,1)S(1)}, u32[]{:S(2)}, u32[]{:S(2)}) collective-permute-start(bf16[8,480,384]{2,1,0:T(8,128)(2,1)} %get-tuple-element.168), channel_id=1, source_target_pairs={{0,8},{8,0},{16,24},{24,16},{1,9},{9,1},{17,25},{25,17},{2,10},{10... | collective-permute-start | bytes 8847368 | tf_op jit(solution)/shard_map/ppermute | solution.py:816
  197.5 8.6 %collective-permute-start.36 = (bf16[8,384,384]{2,1,0:T(8,128)(2,1)}, bf16[8,384,384]{2,1,0:T(8,128)(2,1)S(1)}, u32[]{:S(2)}, u32[]{:S(2)}) collective-permute-start(bf16[8,384,384]{2,1,0:T(8,128)(2,1)} %get-tuple-element.171), channel_id=1, source_target_pairs={{0,8},{8,0},{16,24},{24,16},{1,9},{9,1},{17,25},{25,17},{2,10},{10... | collective-permute-start | bytes 7077896 | tf_op jit(solution)/shard_map/ppermute | solution.py:816
  197.6 12.3 %collective-permute-start.33 = (bf16[512,384]{1,0:T(8,128)(2,1)}, bf16[512,384]{1,0:T(8,128)(2,1)S(1)}, u32[]{:S(2)}, u32[]{:S(2)}) collective-permute-start(bf16[512,384]{1,0:T(8,128)(2,1)} %get-tuple-element.160), channel_id=1, source_target_pairs={{0,8},{8,0},{16,24},{24,16},{1,9},{9,1},{17,25},{25,17},{2,10},{10... | collective-permute-start | bytes 1179656 | tf_op jit(solution)/shard_map/ppermute | solution.py:816
  208.4 5.2 %collective-permute-start.40 = (bf16[192,384]{1,0:T(8,128)(2,1)S(1)}, bf16[192,384]{1,0:T(8,128)(2,1)S(1)}, u32[]{:S(2)}, u32[]{:S(2)}) collective-permute-start(bf16[192,384]{1,0:T(8,128)(2,1)S(1)} %get-tuple-element.179), channel_id=1, source_target_pairs={{2,0},{4,2},{6,4},{7,6},{5,7},{3,5},{1,3},{0,1},{10,8},{12,10},{14... | collective-permute-start | bytes 442376 | tf_op jit(solution)/shard_map/ppermute | solution.py:813
  210.5 8.4 %collective-permute-start.34 = (bf16[64,384]{1,0:T(8,128)(2,1)S(1)}, bf16[64,384]{1,0:T(8,128)(2,1)S(1)}, u32[]{:S(2)}, u32[]{:S(2)}) collective-permute-start(bf16[64,384]{1,0:T(8,128)(2,1)S(1)} %get-tuple-element.165), channel_id=1, source_target_pairs={{0,16},{8,24},{16,0},{24,8},{1,17},{9,25},{17,1},{25,9},{2,18},{10... | collective-permute-start | bytes 147464 | tf_op jit(solution)/shard_map/ppermute | solution.py:819
  215.2 13.8 %collective-permute-start.44 = (bf16[384,384]{1,0:T(8,128)(2,1)S(1)}, bf16[384,384]{1,0:T(8,128)(2,1)S(1)}, u32[]{:S(2)}, u32[]{:S(2)}) collective-permute-start(bf16[384,384]{1,0:T(8,128)(2,1)S(1)} %get-tuple-element.193), channel_id=1, source_target_pairs={{2,0},{4,2},{6,4},{7,6},{5,7},{3,5},{1,3},{0,1},{10,8},{12,10},{14... | collective-permute-start | bytes 884744 | tf_op jit(solution)/shard_map/ppermute | solution.py:813
  216.6 12.4 %collective-permute-start.43 = (bf16[384,384]{1,0:T(8,128)(2,1)S(1)}, bf16[384,384]{1,0:T(8,128)(2,1)S(1)}, u32[]{:S(2)}, u32[]{:S(2)}) collective-permute-start(bf16[384,384]{1,0:T(8,128)(2,1)S(1)} %get-tuple-element.180), channel_id=1, source_target_pairs={{0,2},{2,4},{4,6},{6,7},{7,5},{5,3},{3,1},{1,0},{8,10},{10,12},{12... | collective-permute-start | bytes 884744 | tf_op jit(solution)/shard_map/ppermute | solution.py:810
  217.4 13.9 %collective-permute-start.38 = (bf16[240,384]{1,0:T(8,128)(2,1)S(1)}, bf16[240,384]{1,0:T(8,128)(2,1)S(1)}, u32[]{:S(2)}, u32[]{:S(2)}) collective-permute-start(bf16[240,384]{1,0:T(8,128)(2,1)S(1)} %get-tuple-element.177), channel_id=1, source_target_pairs={{2,0},{4,2},{6,4},{7,6},{5,7},{3,5},{1,3},{0,1},{10,8},{12,10},{14... | collective-permute-start | bytes 552968 | tf_op jit(solution)/shard_map/ppermute | solution.py:813
  218.8 12.5 %collective-permute-start.37 = (bf16[240,384]{1,0:T(8,128)(2,1)S(1)}, bf16[240,384]{1,0:T(8,128)(2,1)S(1)}, u32[]{:S(2)}, u32[]{:S(2)}) collective-permute-start(bf16[240,384]{1,0:T(8,128)(2,1)S(1)} %get-tuple-element.169), channel_id=1, source_target_pairs={{0,2},{2,4},{4,6},{6,7},{7,5},{5,3},{3,1},{1,0},{8,10},{10,12},{12... | collective-permute-start | bytes 552968 | tf_op jit(solution)/shard_map/ppermute | solution.py:810
  229.8 13.6 %collective-permute-start.48 = (bf16[384,384]{1,0:T(8,128)(2,1)S(1)}, bf16[384,384]{1,0:T(8,128)(2,1)S(1)}, u32[]{:S(2)}, u32[]{:S(2)}) collective-permute-start(bf16[384,384]{1,0:T(8,128)(2,1)S(1)} %get-tuple-element.206), channel_id=1, source_target_pairs={{2,0},{4,2},{6,4},{7,6},{5,7},{3,5},{1,3},{0,1},{10,8},{12,10},{14... | collective-permute-start | bytes 884744 | tf_op jit(solution)/shard_map/ppermute | solution.py:813
  231.2 12.3 %collective-permute-start.47 = (bf16[384,384]{1,0:T(8,128)(2,1)S(1)}, bf16[384,384]{1,0:T(8,128)(2,1)S(1)}, u32[]{:S(2)}, u32[]{:S(2)}) collective-permute-start(bf16[384,384]{1,0:T(8,128)(2,1)S(1)} %get-tuple-element.194), channel_id=1, source_target_pairs={{0,2},{2,4},{4,6},{6,7},{7,5},{5,3},{3,1},{1,0},{8,10},{10,12},{12... | collective-permute-start | bytes 884744 | tf_op jit(solution)/shard_map/ppermute | solution.py:810
  232.1 12.1 %collective-permute-start.42 = (bf16[480,384]{1,0:T(8,128)(2,1)S(1)}, bf16[480,384]{1,0:T(8,128)(2,1)S(1)}, u32[]{:S(2)}, u32[]{:S(2)}) collective-permute-start(bf16[480,384]{1,0:T(8,128)(2,1)S(1)} %get-tuple-element.191), channel_id=1, source_target_pairs={{2,0},{4,2},{6,4},{7,6},{5,7},{3,5},{1,3},{0,1},{10,8},{12,10},{14... | collective-permute-start | bytes 1105928 | tf_op jit(solution)/shard_map/ppermute | solution.py:813
  233.5 11.4 %collective-permute-start.41 = (bf16[480,384]{1,0:T(8,128)(2,1)S(1)}, bf16[480,384]{1,0:T(8,128)(2,1)S(1)}, u32[]{:S(2)}, u32[]{:S(2)}) collective-permute-start(bf16[480,384]{1,0:T(8,128)(2,1)S(1)} %get-tuple-element.178), channel_id=1, source_target_pairs={{0,2},{2,4},{4,6},{6,7},{7,5},{5,3},{3,1},{1,0},{8,10},{10,12},{12... | collective-permute-start | bytes 1105928 | tf_op jit(solution)/shard_map/ppermute | solution.py:810
  245.8 25.1 %collective-permute-start.46 = (bf16[480,384]{1,0:T(8,128)(2,1)S(1)}, bf16[480,384]{1,0:T(8,128)(2,1)S(1)}, u32[]{:S(2)}, u32[]{:S(2)}) collective-permute-start(bf16[480,384]{1,0:T(8,128)(2,1)S(1)} %get-tuple-element.204), channel_id=1, source_target_pairs={{2,0},{4,2},{6,4},{7,6},{5,7},{3,5},{1,3},{0,1},{10,8},{12,10},{14... | collective-permute-start | bytes 1105928 | tf_op jit(solution)/shard_map/ppermute | solution.py:813
  246.5 24.4 %collective-permute-start.45 = (bf16[480,384]{1,0:T(8,128)(2,1)S(1)}, bf16[480,384]{1,0:T(8,128)(2,1)S(1)}, u32[]{:S(2)}, u32[]{:S(2)}) collective-permute-start(bf16[480,384]{1,0:T(8,128)(2,1)S(1)} %get-tuple-element.192), channel_id=1, source_target_pairs={{0,2},{2,4},{4,6},{6,7},{7,5},{5,3},{3,1},{1,0},{8,10},{10,12},{12... | collective-permute-start | bytes 1105928 | tf_op jit(solution)/shard_map/ppermute | solution.py:810
  266.7 12.4 %collective-permute-start.51 = (bf16[4,288,384]{2,1,0:T(8,128)(2,1)S(1)}, bf16[4,288,384]{2,1,0:T(8,128)(2,1)S(1)}, u32[]{:S(2)}, u32[]{:S(2)}) collective-permute-start(bf16[4,288,384]{2,1,0:T(8,128)(2,1)S(1)} %get-tuple-element.226), channel_id=1, source_target_pairs={{0,8},{8,0},{16,24},{24,16},{1,9},{9,1},{17,25},{25,17},{2,10},{10... | collective-permute-start | bytes 2654216 | tf_op jit(solution)/shard_map/ppermute | solution.py:816
  278.4 35.5 %collective-permute-start.49 = (bf16[1024,768]{1,0:T(8,128)(2,1)S(1)}, bf16[1024,768]{1,0:T(8,128)(2,1)S(1)}, u32[]{:S(2)}, u32[]{:S(2)}) collective-permute-start(bf16[1024,768]{1,0:T(8,128)(2,1)S(1)} %get-tuple-element.219), channel_id=1, source_target_pairs={{0,8},{8,0},{16,24},{24,16},{1,9},{9,1},{17,25},{25,17},{2,10},{10... | collective-permute-start | bytes 4718600 | tf_op jit(solution)/shard_map/ppermute | solution.py:816
  285.6 6.1 %collective-permute-start.54 = (bf16[304,384]{1,0:T(8,128)(2,1)S(1)}, bf16[304,384]{1,0:T(8,128)(2,1)S(1)}, u32[]{:S(2)}, u32[]{:S(2)}) collective-permute-start(bf16[304,384]{1,0:T(8,128)(2,1)S(1)} %get-tuple-element.230), channel_id=1, source_target_pairs={{0,2},{2,4},{4,6},{6,7},{7,5},{5,3},{3,1},{1,0},{8,10},{10,12},{12... | collective-permute-start | bytes 700424 | tf_op jit(solution)/shard_map/ppermute | solution.py:810
  286.4 5.9 %collective-permute-start.55 = (bf16[304,384]{1,0:T(8,128)(2,1)S(1)}, bf16[304,384]{1,0:T(8,128)(2,1)S(1)}, u32[]{:S(2)}, u32[]{:S(2)}) collective-permute-start(bf16[304,384]{1,0:T(8,128)(2,1)S(1)} %get-tuple-element.231), channel_id=1, source_target_pairs={{2,0},{4,2},{6,4},{7,6},{5,7},{3,5},{1,3},{0,1},{10,8},{12,10},{14... | collective-permute-start | bytes 700424 | tf_op jit(solution)/shard_map/ppermute | solution.py:813
  287.1 11.4 %collective-permute-start.63 = (bf16[384,384]{1,0:T(8,128)(2,1)S(1)}, bf16[384,384]{1,0:T(8,128)(2,1)S(1)}, u32[]{:S(2)}, u32[]{:S(2)}) collective-permute-start(bf16[384,384]{1,0:T(8,128)(2,1)S(1)} %get-tuple-element.239), channel_id=1, source_target_pairs={{2,0},{4,2},{6,4},{7,6},{5,7},{3,5},{1,3},{0,1},{10,8},{12,10},{14... | collective-permute-start | bytes 884744 | tf_op jit(solution)/shard_map/ppermute | solution.py:813
  287.7 11.0 %collective-permute-start.62 = (bf16[384,384]{1,0:T(8,128)(2,1)S(1)}, bf16[384,384]{1,0:T(8,128)(2,1)S(1)}, u32[]{:S(2)}, u32[]{:S(2)}) collective-permute-start(bf16[384,384]{1,0:T(8,128)(2,1)S(1)} %get-tuple-element.207), channel_id=1, source_target_pairs={{0,2},{2,4},{4,6},{6,7},{7,5},{5,3},{3,1},{1,0},{8,10},{10,12},{12... | collective-permute-start | bytes 884744 | tf_op jit(solution)/shard_map/ppermute | solution.py:810
  291.7 14.7 %collective-permute-start.67 = (bf16[480,384]{1,0:T(8,128)(2,1)S(1)}, bf16[480,384]{1,0:T(8,128)(2,1)S(1)}, u32[]{:S(2)}, u32[]{:S(2)}) collective-permute-start(bf16[480,384]{1,0:T(8,128)(2,1)S(1)} %get-tuple-element.240), channel_id=1, source_target_pairs={{2,0},{4,2},{6,4},{7,6},{5,7},{3,5},{1,3},{0,1},{10,8},{12,10},{14... | collective-permute-start | bytes 1105928 | tf_op jit(solution)/shard_map/ppermute | solution.py:813
  292.3 14.4 %collective-permute-start.66 = (bf16[480,384]{1,0:T(8,128)(2,1)S(1)}, bf16[480,384]{1,0:T(8,128)(2,1)S(1)}, u32[]{:S(2)}, u32[]{:S(2)}) collective-permute-start(bf16[480,384]{1,0:T(8,128)(2,1)S(1)} %get-tuple-element.205), channel_id=1, source_target_pairs={{0,2},{2,4},{4,6},{6,7},{7,5},{5,3},{3,1},{1,0},{8,10},{10,12},{12... | collective-permute-start | bytes 1105928 | tf_op jit(solution)/shard_map/ppermute | solution.py:810
  298.5 12.4 %collective-permute-start.56 = (bf16[304,384]{1,0:T(8,128)(2,1)S(1)}, bf16[304,384]{1,0:T(8,128)(2,1)S(1)}, u32[]{:S(2)}, u32[]{:S(2)}) collective-permute-start(bf16[304,384]{1,0:T(8,128)(2,1)S(1)} %get-tuple-element.232), channel_id=1, source_target_pairs={{0,2},{2,4},{4,6},{6,7},{7,5},{5,3},{3,1},{1,0},{8,10},{10,12},{12... | collective-permute-start | bytes 700424 | tf_op jit(solution)/shard_map/ppermute | solution.py:810
  298.7 12.8 %collective-permute-start.57 = (bf16[304,384]{1,0:T(8,128)(2,1)S(1)}, bf16[304,384]{1,0:T(8,128)(2,1)S(1)}, u32[]{:S(2)}, u32[]{:S(2)}) collective-permute-start(bf16[304,384]{1,0:T(8,128)(2,1)S(1)} %get-tuple-element.233), channel_id=1, source_target_pairs={{2,0},{4,2},{6,4},{7,6},{5,7},{3,5},{1,3},{0,1},{10,8},{12,10},{14... | collective-permute-start | bytes 700424 | tf_op jit(solution)/shard_map/ppermute | solution.py:813
  306.4 9.1 %collective-permute-start.64 = (bf16[384,384]{1,0:T(8,128)(2,1)S(1)}, bf16[384,384]{1,0:T(8,128)(2,1)S(1)}, u32[]{:S(2)}, u32[]{:S(2)}) collective-permute-start(bf16[384,384]{1,0:T(8,128)(2,1)S(1)} %ring_last.2), channel_id=1, source_target_pairs={{0,16},{8,24},{16,0},{24,8},{1,17},{9,25},{17,1},{25,9},{2,18},{10... | collective-permute-start | bytes 884744 | tf_op jit(solution)/shard_map/ppermute | solution.py:822
  307.4 14.3 %collective-permute-start.68 = (bf16[480,384]{1,0:T(8,128)(2,1)S(1)}, bf16[480,384]{1,0:T(8,128)(2,1)S(1)}, u32[]{:S(2)}, u32[]{:S(2)}) collective-permute-start(bf16[480,384]{1,0:T(8,128)(2,1)S(1)} %ring_last.3), channel_id=1, source_target_pairs={{0,16},{8,24},{16,0},{24,8},{1,17},{9,25},{17,1},{25,9},{2,18},{10... | collective-permute-start | bytes 1105928 | tf_op jit(solution)/shard_map/ppermute | solution.py:822
  312.1 8.7 %collective-permute-start.58 = (bf16[304,384]{1,0:T(8,128)(2,1)S(1)}, bf16[304,384]{1,0:T(8,128)(2,1)S(1)}, u32[]{:S(2)}, u32[]{:S(2)}) collective-permute-start(bf16[304,384]{1,0:T(8,128)(2,1)S(1)} %get-tuple-element.234), channel_id=1, source_target_pairs={{0,2},{2,4},{4,6},{6,7},{7,5},{5,3},{3,1},{1,0},{8,10},{10,12},{12... | collective-permute-start | bytes 700424 | tf_op jit(solution)/shard_map/ppermute | solution.py:810
  312.4 8.3 %collective-permute-start.59 = (bf16[304,384]{1,0:T(8,128)(2,1)S(1)}, bf16[304,384]{1,0:T(8,128)(2,1)S(1)}, u32[]{:S(2)}, u32[]{:S(2)}) collective-permute-start(bf16[304,384]{1,0:T(8,128)(2,1)S(1)} %get-tuple-element.235), channel_id=1, source_target_pairs={{2,0},{4,2},{6,4},{7,6},{5,7},{3,5},{1,3},{0,1},{10,8},{12,10},{14... | collective-permute-start | bytes 700424 | tf_op jit(solution)/shard_map/ppermute | solution.py:813
  315.3 42.1 %collective-permute-start.50 = (bf16[512,768]{1,0:T(8,128)(2,1)}, bf16[512,768]{1,0:T(8,128)(2,1)}, u32[]{:S(2)}, u32[]{:S(2)}) collective-permute-start(bf16[512,768]{1,0:T(8,128)(2,1)} %slice.65), channel_id=1, source_target_pairs={{0,16},{8,24},{16,0},{24,8},{1,17},{9,25},{17,1},{25,9},{2,18},{10... | collective-permute-start | bytes 2359304 | tf_op jit(solution)/shard_map/ppermute | solution.py:819
  315.6 30.1 %collective-permute-start.65 = (bf16[384,384]{1,0:T(8,128)(2,1)S(1)}, bf16[384,384]{1,0:T(8,128)(2,1)S(1)}, u32[]{:S(2)}, u32[]{:S(2)}) collective-permute-start(bf16[384,384]{1,0:T(8,128)(2,1)S(1)} %add_convert_fusion.1.own_one), channel_id=1, source_target_pairs={{0,8},{8,0},{16,24},{24,16},{1,9},{9,1},{17,25},{25,17},{2,10},{10... | collective-permute-start | bytes 884744 | tf_op jit(solution)/shard_map/ppermute | solution.py:816
  321.4 19.1 %collective-permute-start.60 = (bf16[304,384]{1,0:T(8,128)(2,1)S(1)}, bf16[304,384]{1,0:T(8,128)(2,1)S(1)}, u32[]{:S(2)}, u32[]{:S(2)}) collective-permute-start(bf16[304,384]{1,0:T(8,128)(2,1)S(1)} %head_ring_last.1), channel_id=1, source_target_pairs={{0,16},{8,24},{16,0},{24,8},{1,17},{9,25},{17,1},{25,9},{2,18},{10... | collective-permute-start | bytes 700424 | tf_op jit(solution)/shard_map/ppermute | solution.py:822
  321.8 23.9 %collective-permute-start.69 = (bf16[480,384]{1,0:T(8,128)(2,1)S(1)}, bf16[480,384]{1,0:T(8,128)(2,1)S(1)}, u32[]{:S(2)}, u32[]{:S(2)}) collective-permute-start(bf16[480,384]{1,0:T(8,128)(2,1)S(1)} %add_convert_fusion.own_two), channel_id=1, source_target_pairs={{0,8},{8,0},{16,24},{24,16},{1,9},{9,1},{17,25},{25,17},{2,10},{10... | collective-permute-start | bytes 1105928 | tf_op jit(solution)/shard_map/ppermute | solution.py:816
  340.6 10.1 %collective-permute-start.61 = (bf16[304,384]{1,0:T(8,128)(2,1)S(1)}, bf16[304,384]{1,0:T(8,128)(2,1)S(1)}, u32[]{:S(2)}, u32[]{:S(2)}) collective-permute-start(bf16[304,384]{1,0:T(8,128)(2,1)S(1)} %add_convert_fusion.2.own), channel_id=1, source_target_pairs={{0,8},{8,0},{16,24},{24,16},{1,9},{9,1},{17,25},{25,17},{2,10},{10... | collective-permute-start | bytes 700424 | tf_op jit(solution)/shard_map/ppermute | solution.py:816
  (74 other events, 670.6 us)
